TPU v7x, 32 devices: a whole 2x2x4 slice. The times are simulated.
32 devices in a mesh: frag: 2 (over y), aux: 4 (over z), pair: 4 (over x, core).
Axes of the slice: x: 2, y: 2, z: 4, core: 2. Of those that a mesh axis runs over, the one named last changes fastest.
Arguments:
- half_ints: bfloat16 [2560, 8, 4, 128], P(('frag', 'aux', 'pair')), parts along dimension 0, may hold values from -3.5 to 3.5
- partners: int32 [16, 3], P(('frag', 'aux')), parts along dimension 0, may hold values from 0 to 7, as said below
- domains: int32 [16, 128], P('frag'), parts along dimension 0, may hold values from 0 to 1023
- occ_energy: float32 [16, 4], P('frag'), parts along dimension 0, may hold values from -1 to -0.3
- vir_energy: float32 [2048], P('frag'), parts along dimension 0, may hold values from 0.2 to 1.5
Outputs:
- amplitudes: float32 [16, 3, 512, 512], P(('frag', 'aux'), None, 'pair'), parts along dimension 0
- pair_energy: float32 [16, 3, 4, 4], P(('frag', 'aux')), parts along dimension 0
There are 2 independent parts, one for each index of `frag`. A program takes and returns all parts, laid end to end along the dimension named above; each array names one. Nothing has to cross between parts.
Inputs may be any that keep to these rules, and one draw needn't show every extreme that they name: partners[I, 0] = I; every partner J of block I has |J - I| <= 2, and slot 1 is at distance exactly 2.
All inputs are finite; a program needn't handle non-finite values.
Results may differ from a plain program's by a relative error of at most 0.0003.
Values may be sent and summed in bfloat16 or wider, within the bound.
No kernel may reach another device: no remote copies, remote signals or barrier semaphores. Data moves between devices by JAX's collectives and lax.ppermute only.
A program may use at most 128 MiB of HBM per device.

v0:
```python
import jax
import jax.numpy as jnp
from jax import lax
from jax.sharding import PartitionSpec as P


def padded(shard, sides, width):
    for axis, dim in sides:
        size, length = (lax.axis_size(axis), shard.shape[dim])
        up = [(i, (i + 1) % size) for i in range(size - 1)]
        down = [(j, i) for i, j in up]
        last = lax.slice_in_dim(shard, length - width, length, axis=dim)
        first = lax.slice_in_dim(shard, 0, width, axis=dim)
        before = lax.ppermute(last, axis, up)
        after = lax.ppermute(first, axis, down)
        shard = jnp.concatenate([before, shard, after], axis=dim)
    return shard


def on_device(half_ints, partners, domains, occ_energy, vir_energy):
    blocks_here, slots = partners.shape
    orbitals = half_ints.shape[2]
    domain = half_ints.shape[3]
    row_width = orbitals * domain
    first_block = lax.axis_index("aux") * blocks_here
    owned = lax.all_to_all(half_ints, "aux", split_axis=1, concat_axis=0, tiled=True)
    widened = padded(owned, (("aux", 1),), blocks_here)
    flat_rows = widened.reshape(widened.shape[0], 3 * blocks_here, row_width)
    own_blocks = flat_rows[:, blocks_here : 2 * blocks_here]
    positions = (partners - first_block + blocks_here).reshape(-1)
    partner_rows = jnp.take(flat_rows, positions, axis=1).reshape(
        flat_rows.shape[0], blocks_here, slots, row_width
    )
    partial_terms = jnp.einsum(
        "qlr,qlsc->lsrc", own_blocks, partner_rows, preferred_element_type=jnp.float32
    )
    my_sums = lax.psum_scatter(partial_terms, "pair", scatter_dimension=2, tiled=True)
    row_count = my_sums.shape[2]
    row_start = lax.axis_index("pair") * row_count
    block_ids = first_block + jnp.arange(blocks_here, dtype=jnp.int32)
    row_vals = (
        jnp.take(occ_energy, block_ids, axis=0)[:, :, None]
        - jnp.take(vir_energy, jnp.take(domains, block_ids, axis=0), axis=0)[:, None, :]
    )
    row_vals = lax.dynamic_slice_in_dim(
        row_vals.reshape(blocks_here, row_width), row_start, row_count, 1
    )
    col_vals = (
        jnp.take(occ_energy, partners, axis=0)[:, :, :, None]
        - jnp.take(vir_energy, jnp.take(domains, partners, axis=0), axis=0)[:, :, None, :]
    )
    col_vals = col_vals.reshape(blocks_here, slots, row_width)
    denominator = row_vals[:, None, :, None] + col_vals[:, :, None, :]
    amplitudes = my_sums / denominator
    weighted = (
        (my_sums * amplitudes).reshape(blocks_here, slots, row_count, orbitals, domain).sum(axis=4)
    )
    orbital_of = (row_start + jnp.arange(row_count, dtype=jnp.int32)) // domain
    selector = (orbital_of[:, None] == jnp.arange(orbitals, dtype=jnp.int32)[None, :]).astype(
        jnp.float32
    )
    partial_energy = jnp.einsum(
        "lskj,ki->lsij", weighted, selector, precision=lax.Precision.HIGHEST
    )
    pair_energy = lax.psum(partial_energy, "pair") / (domain * domain)
    return (amplitudes, pair_energy)


def solution(mesh):
    return jax.shard_map(
        on_device,
        mesh=mesh,
        in_specs=(
            P(("frag", "aux", "pair"), None, None, None),
            P(("frag", "aux"), None),
            P("frag", None),
            P("frag", None),
            P("frag"),
        ),
        out_specs=(P(("frag", "aux"), None, "pair", None), P(("frag", "aux"), None, None, None)),
        check_vma=False,
    )
```

profile of v0, /device:TPU:0, one launch (start us, length us, event | category | flops | bytes accessed | tf_op | source)
XLA Modules:
  0.0 143.3 jit_solution(1304620717668638591)
XLA Ops:
  7.2 2.2 %copy.21 = bf16[80,8,4,128]{3,2,0,1:T(4,128)(2,1)} copy(bf16[80,8,4,128]{3,2,1,0:T(4,128)(2,1)} %param.5) | data formatting | bytes 1310720 | tf_op args[0]
  9.4 6.3 %all-to-all-start = ((bf16[80,8,4,128]{3,2,0,1:T(4,128)(2,1)}), bf16[80,8,4,128]{3,2,0,1:T(4,128)(2,1)S(1)}, u32[]{:S(2)}, u32[]{:S(2)}) async-start(bf16[80,8,4,128]{3,2,0,1:T(4,128)(2,1)} %copy.21), calls=%async_computation | async-start | bytes 1310720 | tf_op jit(solution)/shard_map/all_to_all | solution.py:26
  15.7 17.3 %all-to-all-done = bf16[80,8,4,128]{3,2,0,1:T(4,128)(2,1)S(1)} async-done(((bf16[80,8,4,128]{3,2,0,1:T(4,128)(2,1)}), bf16[80,8,4,128]{3,2,0,1:T(4,128)(2,1)S(1)}, u32[]{:S(2)}, u32[]{:S(2)}) %all-to-all-start) | async-done | bytes 655392 | tf_op jit(solution)/shard_map/all_to_all | solution.py:26
  33.2 1.3 collective-permute-start.1
  34.5 4.6 %collective-permute-start = (bf16[320,2,4,128]{3,2,0,1:T(4,128)(2,1)S(1)}, bf16[320,2,4,128]{3,2,0,1:T(4,128)(2,1)S(1)}, u32[]{:S(2)}, u32[]{:S(2)}) collective-permute-start(bf16[320,2,4,128]{3,2,0,1:T(4,128)(2,1)S(1)} %bitcast.57), channel_id=1, source_target_pairs={{0,4},{4,8},{8,12},{1,5},{5,9},{9,13},{2,6},{6,10},{10,14},{3,7},{... | collective-permute-start | bytes 1966088 | tf_op jit(solution)/shard_map/ppermute | solution.py:14
  39.7 11.1 %collective-permute-done.1 = bf16[320,2,4,128]{3,2,0,1:T(4,128)(2,1)S(1)} collective-permute-done((bf16[320,2,4,128]{3,2,0,1:T(4,128)(2,1)S(1)}, bf16[320,2,4,128]{3,2,0,1:T(4,128)(2,1)S(1)}, u32[]{:S(2)}, u32[]{:S(2)}) %collective-permute-start.1) | collective-permute-done | bytes 655392 | tf_op jit(solution)/shard_map/ppermute | solution.py:15
  50.8 1.1 concatenate.12
  52.0 1.1 concatenate.10
  53.1 1.5 %pad_maximum_fusion = bf16[320,6,512]{2,0,1:T(8,128)(2,1)S(1)} fusion(bf16[320,2,512]{2,0,1:T(8,128)(2,1)} %concatenate.12, bf16[320,2,512]{2,0,1:T(8,128)(2,1)S(1)} %concatenate.11, bf16[320,2,512]{2,0,1:T(8,128)(2,1)} %concatenate.10), kind=kLoop, calls=%fused_computation.8 | loop fusion | flops 1966080 | bytes 3932160 | tf_op jit(solution)/shard_map/concatenate | solution.py:16
  54.6 2.0 %gather_fusion = bf16[6,320,512]{2,1,0:T(8,128)(2,1)} fusion(bf16[320,6,512]{2,0,1:T(8,128)(2,1)S(1)} %pad_maximum_fusion, s32[1024]{0:T(1024)S(1)} %pad_clamp_fusion.4), kind=kCustom, calls=%fused_computation | custom fusion | bytes 3932184 | tf_op jit(solution)/shard_map/jit(_take)/gather | solution.py:31
  56.6 6.1 %convolution_bitcast_fusion = f32[2,3,512,512]{2,3,1,0:T(8,128)} fusion(bf16[320,2,3,512]{3,0,2,1:T(8,128)(2,1)} %bitcast.55, pred[2,3]{1,0:T(4,128)(4,1)S(1)} %get-tuple-element.11, bf16[320,2,512,1]{2,0,1,3:T(8,128)(2,1)S(1)} %reshape.300), kind=kOutput, calls=%fused_computation.7 | convolution fusion | flops 1007616000 | bytes 8912902 | tf_op jit(solution)/shard_map/qlr,qlsc->lsrc/dot_general | solution.py:34
  62.8 0.6 gather_fusion.5
  63.5 0.6 gather_fusion.4
  64.1 0.6 gather_fusion.2
  64.7 0.6 gather_fusion.1
  65.3 3.2 %gather_fusion.6 = f32[768]{0:T(1024)S(1)} fusion(f32[1024]{0:T(1024)S(1)} %copy-done.1, s32[1024]{0:T(1024)S(1)} %pad_clamp_fusion), kind=kCustom, calls=%fused_computation.6 | custom fusion | bytes 9216 | tf_op jit(solution)/shard_map/jit(_take)/gather | solution.py:50
  69.1 1.4 gather_fusion.3
  70.7 50.7 %reduce-scatter.2.cloned.1.call-done = f32[2,3,128,512]{2,3,1,0:T(8,128)} async-done(((f32[2,3,512,512]{2,3,1,0:T(8,128)}), f32[2,3,128,512]{2,3,1,0:T(8,128)}) %reduce-scatter.2.cloned.1.call-update) | async-done | bytes 1572880 | tf_op jit(solution)/shard_map/reduce_scatter | solution.py:37
  121.4 1.9 %add_divide_fusion = f32[2,3,128,512]{2,3,1,0:T(8,128)S(1)} fusion(f32[2,3,128,512]{2,3,1,0:T(8,128)} %reduce-scatter.2.cloned.1.call-done, f32[2,3,512]{2,1,0:T(4,128)S(1)} %copy.28, f32[2,128]{1,0:T(2,128)S(1)} %constant_dynamic-slice_fusion), kind=kLoop, calls=%fused_computation.12 | loop fusion | flops 786432 | bytes 3159040 | tf_op jit(solution)/shard_map/div | solution.py:54
  123.3 1.6 %copy.29 = f32[2,3,128,512]{3,2,1,0:T(8,128)} copy(f32[2,3,128,512]{2,3,1,0:T(8,128)S(1)} %add_divide_fusion) | data formatting | bytes 3145728
  124.9 0.5 bitcast_reduce_fusion
  125.4 0.3 convolution_bitcast_fusion.1
  125.7 10.1 %psum.7 = f32[2,3,4,4]{3,2,1,0:T(4,128)S(1)} all-reduce(f32[2,3,4,4]{3,2,1,0:T(4,128)S(1)} %convolution_bitcast_fusion.1), channel_id=1, replica_groups=mesh['frag'=2,'aux'=4,'pair'=4] {'pair'}, use_global_device_ids=true, to_apply=%region_2.3 | all-reduce | flops 96 | bytes 768 | tf_op jit(solution)/shard_map/psum | solution.py:65
  135.8 0.6 broadcast_multiply_fusion
  (50 shorter events, 2.1 us)
Async XLA Ops:
  7.2 55.7 %copy-start = (s32[8,128]{1,0:T(8,128)S(1)}, s32[8,128]{1,0:T(8,128)}, u32[]{:S(2)}) copy-start(s32[8,128]{1,0:T(8,128)} %param.7) | copy-start | bytes 12292
  7.2 31.9 %copy-start.3 = (s32[2,3]{1,0:T(2,128)S(1)}, s32[2,3]{1,0:T(2,128)}, u32[]{:S(2)}) copy-start(s32[2,3]{1,0:T(2,128)} %param.6) | copy-start | bytes 76
  9.4 23.6 %all-to-all-start = ((bf16[80,8,4,128]{3,2,0,1:T(4,128)(2,1)}), bf16[80,8,4,128]{3,2,0,1:T(4,128)(2,1)S(1)}, u32[]{:S(2)}, u32[]{:S(2)}) async-start(bf16[80,8,4,128]{3,2,0,1:T(4,128)(2,1)} %copy.21), calls=%async_computation | async-start | bytes 1310720 | tf_op jit(solution)/shard_map/all_to_all | solution.py:26
  15.7 105.7 %reduce-scatter.2.cloned.1.call-start = ((), (), s32[]{:S(2)}) async-start(), calls=%async_computation.2 | async-start | bytes 7864320 | tf_op jit(solution)/shard_map/reduce_scatter | solution.py:37
  33.2 17.6 %collective-permute-start.1 = (bf16[320,2,4,128]{3,2,0,1:T(4,128)(2,1)S(1)}, bf16[320,2,4,128]{3,2,0,1:T(4,128)(2,1)S(1)}, u32[]{:S(2)}, u32[]{:S(2)}) collective-permute-start(bf16[320,2,4,128]{3,2,0,1:T(4,128)(2,1)S(1)} %bitcast.56), channel_id=1, source_target_pairs={{4,0},{8,4},{12,8},{5,1},{9,5},{13,9},{6,2},{10,6},{14,10},{7,3},{... | collective-permute-start | bytes 1966088 | tf_op jit(solution)/shard_map/ppermute | solution.py:15
  34.5 17.5 %collective-permute-start = (bf16[320,2,4,128]{3,2,0,1:T(4,128)(2,1)S(1)}, bf16[320,2,4,128]{3,2,0,1:T(4,128)(2,1)S(1)}, u32[]{:S(2)}, u32[]{:S(2)}) collective-permute-start(bf16[320,2,4,128]{3,2,0,1:T(4,128)(2,1)S(1)} %bitcast.57), channel_id=1, source_target_pairs={{0,4},{4,8},{8,12},{1,5},{5,9},{9,13},{2,6},{6,10},{10,14},{3,7},{... | collective-permute-start | bytes 1966088 | tf_op jit(solution)/shard_map/ppermute | solution.py:14
  62.7 0.7 copy-start.4
  62.7 2.6 %copy-start.1 = (f32[1024]{0:T(1024)S(1)}, f32[1024]{0:T(1024)}, u32[]{:S(2)}) copy-start(f32[1024]{0:T(1024)} %param.9) | copy-start | bytes 12292
  123.3 1.6 %copy-start.2 = (f32[2,3,128,512]{2,3,1,0:T(8,128)S(1)}, f32[2,3,128,512]{2,3,1,0:T(8,128)}, u32[]{:S(2)}) copy-start(f32[2,3,128,512]{2,3,1,0:T(8,128)} %reduce-scatter.2.cloned.1.call-done) | copy-start | bytes 4718596
Sparse Core Ops, SparseCore 0:
  62.9 58.4 reduce-scatter.1
where the time goes:
time: 144 us; the launch traced here: 143 us
  waiting for transfers between devices  79.1 us (55%)
  local copies, waits for them, and re-layouts  16.1 us (11%)
  between operations  14.2 us (10%)
  starting transfers between devices  12.2 us (8%)
  blocking collectives  10.1 us (7%)
  matrix products  6.4 us (4%)
  other arithmetic  5.1 us (4%)
    reduce_scatter x1, waiting for transfers between devices, on_device(): lax.psum_scatter(partial_terms, 'pair', scatter_dimension=2, tiled=True)  50.7 us
    all_to_all x1, waiting for transfers between devices, on_device(): lax.all_to_all(half_ints, 'aux', split_axis=1, concat_axis=0, tiled=True)  17.3 us
    ppermute x1, waiting for transfers between devices, padded(): after = lax.ppermute(first, axis, down)  11.1 us
    psum x1, blocking collectives, on_device(): pair_energy = lax.psum(partial_energy, 'pair') / (domain * domain)  10.1 us
    all_to_all x1, starting transfers between devices, on_device(): lax.all_to_all(half_ints, 'aux', split_axis=1, concat_axis=0, tiled=True)  6.32 us
    dot_general x1, matrix products, on_device(): jnp.einsum('qlr,qlsc->lsrc', own_blocks, partner_rows, preferred_element_...  6.12 us
    ppermute x1, starting transfers between devices, padded(): before = lax.ppermute(last, axis, up)  4.59 us
    unnamed x14, local copies, waits for them, and re-layouts  3.89 us
  transfers between devices with their start and end apart: 4, of which 4 were waited for; matrix products, arithmetic and copies ran while one was open for 7% of the time, Pallas kernels for 0%

commit v1 on v0

--- a/solution.py
+++ b/solution.py
@@ -1,7 +1,318 @@
 import jax
 import jax.numpy as jnp
 from jax import lax
+from jax.experimental import pallas as pl
+from jax.experimental.pallas import tpu as pltpu
 from jax.sharding import PartitionSpec as P
+
+BF16, F16, F32 = jnp.bfloat16, jnp.float16, jnp.float32
+VMEM = pl.BlockSpec(memory_space=pltpu.VMEM)
+SMEM = pl.BlockSpec(memory_space=pltpu.SMEM)
+PARAMS = pltpu.CompilerParams(vmem_limit_bytes=8 * 2**20)
+COST = pl.CostEstimate(flops=20_000_000_000, bytes_accessed=40_000_000, transcendentals=0)
+PEAK_ROWS = 16
+
+
+def shape(*dims, dtype=F32):
+    return jax.ShapeDtypeStruct(dims, dtype)
+
+
+def panel_at(depth, orbital, block):
+    return pl.ds((orbital * 2 + block) * depth, depth)
+
+
+def pack(place, raw, count):
+    depth, blocks, orbitals, domain = raw.shape
+
+    def kernel(place_ref, raw_ref, *refs):
+        near, sends, wide = refs[:3], refs[3:-1], refs[-1]
+        z = place_ref[0]
+        wide[...] = raw_ref[...].astype(F32)
+        peak = jnp.max(jnp.abs(wide[...]).reshape(-1, PEAK_ROWS, domain), axis=0).astype(BF16)
+
+        def panels(out, first):
+            for r in range(2):
+                block = jnp.clip(first + r, 0, blocks - 1)
+                for i in range(orbitals):
+                    rows = pl.ds(block * orbitals + i, depth, stride=blocks * orbitals)
+                    out[panel_at(depth, i, r), :] = wide[rows, :].astype(BF16)
+            out[2 * orbitals * depth :, :] = peak
+
+        for k, out in enumerate(sends, 1):
+            panels(out, 2 * lax.rem(z + k, count))
+        for k, out in enumerate(near):
+            panels(out, 2 * (z - 1 + k))
+
+    one_set = shape(2 * orbitals * depth + PEAK_ROWS, domain, dtype=BF16)
+    return pl.pallas_call(
+        kernel,
+        out_shape=[one_set] * (count + 2),
+        in_specs=[SMEM, VMEM],
+        out_specs=[VMEM] * (count + 2),
+        scratch_shapes=[pltpu.VMEM((depth * blocks * orbitals, domain), F32)],
+        compiler_params=PARAMS,
+        cost_estimate=COST,
+    )(place, raw.reshape(depth * blocks * orbitals, domain))
+
+
+def relay(place, own, rows):
+    count, domain = len(own), own[0].shape[1]
+
+    def kernel(place_ref, *refs):
+        own_refs, outs = refs[:count], refs[count:]
+        even = lax.rem(place_ref[0], 2) == 0
+        for k in range(count - 1):
+            at = slice(k * rows, (k + 1) * rows)
+            rise = own_refs[k][:rows]
+            fall = own_refs[(count - k) % count][:rows]
+            outs[0][at] = jnp.where(even, rise, fall)
+            outs[1][at] = jnp.where(even, fall, rise)
+
+    return pl.pallas_call(
+        kernel,
+        out_shape=[shape((count - 1) * rows, domain, dtype=BF16)] * 2,
+        in_specs=[SMEM] + [VMEM] * count,
+        out_specs=[VMEM] * 2,
+        compiler_params=PARAMS,
+        cost_estimate=COST,
+    )(place, *own)
+
+
+def product(left, right):
+    return lax.dot_general(left, right, (((0,), (0,)), ((), ())), preferred_element_type=F32)
+
+
+def left_rows(place_ref, own_refs, depth, r):
+    p = place_ref[1]
+    x, c = p // 2, lax.rem(p, 2)
+    order = (2 * x + c, 2 * (1 - x) + c, 2 * x + 1 - c, 2 * (1 - x) + 1 - c)
+    columns = [
+        jnp.concatenate([ref[panel_at(depth, i, r), :] for ref in own_refs], axis=0) for i in order
+    ]
+    return jnp.concatenate(columns, axis=1)
+
+
+def own_pairs(place, own, orbitals):
+    count = len(own)
+    domain = own[0].shape[1]
+    depth = (own[0].shape[0] - PEAK_ROWS) // (2 * orbitals)
+    wide = orbitals * domain
+
+    def kernel(place_ref, *refs):
+        own_refs, (mine, other, give, peak) = refs[:count], refs[count:]
+        for r in range(2):
+            right = jnp.concatenate(
+                [
+                    jnp.concatenate([ref[panel_at(depth, j, r), :] for ref in own_refs], axis=0)
+                    for j in range(orbitals)
+                ],
+                axis=1,
+            )
+            sums = product(left_rows(place_ref, own_refs, depth, r), right)
+            mine[r] = sums[:domain]
+            other[r] = sums[domain : 2 * domain]
+            give[0, r] = sums[2 * domain : 3 * domain]
+            give[1, r] = sums[3 * domain :]
+        top = own_refs[0][-PEAK_ROWS:, :].astype(F32)
+        for ref in own_refs[1:]:
+            top = jnp.maximum(top, ref[-PEAK_ROWS:, :].astype(F32))
+        peak[...] = top
+
+    return pl.pallas_call(
+        kernel,
+        out_shape=[
+            shape(2, domain, wide),
+            shape(2, domain, wide),
+            shape(2, 2, domain, wide),
+            shape(PEAK_ROWS, domain),
+        ],
+        in_specs=[SMEM] + [VMEM] * count,
+        out_specs=[VMEM] * 4,
+        compiler_params=PARAMS,
+        cost_estimate=COST,
+    )(place, *own)
+
+
+def near_pairs(place, choice, own, here, sides, orbitals):
+    count = len(own)
+    domain = own[0].shape[1]
+    depth = (own[0].shape[0] - PEAK_ROWS) // (2 * orbitals)
+    rows, wide = 2 * orbitals * depth, orbitals * domain
+
+    def kernel(place_ref, choice_ref, *refs):
+        own_refs, here_refs, side_refs = refs[:count], refs[count : count + 2], refs[count + 2 :][:2]
+        outs, picked = refs[count + 4 : -1], refs[-1]
+        even = lax.rem(place_ref[0], 2) == 0
+
+        def window_panel(w, k, j, parity):
+            if w in (2, 3):
+                return own_refs[k][panel_at(depth, j, w - 2), :]
+            high = w > 3
+            if k == 0:
+                return here_refs[high][panel_at(depth, j, w % 2), :]
+            at = (count - 1 - k if high else k - 1) * rows + (2 * j + w % 2) * depth
+            return side_refs[1 - parity if high else parity][at : at + depth, :]
+
+        def pick(w, parity):
+            for k in range(count):
+                for j in range(orbitals):
+                    picked[k * depth : (k + 1) * depth, j * domain : (j + 1) * domain] = (
+                        window_panel(w, k, j, parity)
+                    )
+
+        for r in range(2):
+            left = left_rows(place_ref, own_refs, depth, r)
+            for s in range(2):
+                chosen = choice_ref[r, s + 1]
+                for w in (r, r + 4) if s == 0 else range(r, r + 5):
+                    if w in (2, 3):
+                        pl.when(chosen == w)(lambda w=w: pick(w, 0))
+                    else:
+                        for parity in range(2):
+                            match = even if parity else jnp.logical_not(even)
+                            pl.when((chosen == w) & match)(
+                                lambda w=w, parity=parity: pick(w, parity)
+                            )
+                sums = product(left, picked[...])
+                mine, other, give = outs[3 * s : 3 * s + 3]
+                mine[r] = sums[:domain]
+                other[r] = sums[domain : 2 * domain]
+                give[0, r] = sums[2 * domain : 3 * domain]
+                give[1, r] = sums[3 * domain :]
+
+    tiles = [shape(2, domain, wide), shape(2, domain, wide), shape(2, 2, domain, wide)]
+    return pl.pallas_call(
+        kernel,
+        out_shape=tiles * 2,
+        in_specs=[SMEM, SMEM] + [VMEM] * (count + 4),
+        out_specs=[VMEM] * 6,
+        scratch_shapes=[pltpu.VMEM((count * depth, wide), BF16)],
+        compiler_params=PARAMS,
+        cost_estimate=COST,
+    )(place, choice, *own, *here, *sides)
+
+
+def finish(totals, row_vals, col_vals, slot, before, out):
+    blocks, rows, width = totals.shape
+    orbitals = width // rows
+
+    def kernel(total_ref, row_ref, col_ref, *refs):
+        amp_ref, energy_ref = refs[-2:]
+        row = row_ref[0]
+        for j in range(orbitals):
+            at = slice(j * rows, (j + 1) * rows)
+            total = total_ref[0, :, at]
+            amp = total / (row + col_ref[0, 0, j : j + 1, :])
+            amp_ref[0, 0, :, at] = amp
+            energy_ref[0, 0, j : j + 1, :] = jnp.sum(total * amp, axis=0, keepdims=True)
+
+    return pl.pallas_call(
+        kernel,
+        grid=(blocks,),
+        out_shape=[shape(*out), shape(blocks, 1, orbitals, rows)],
+        in_specs=[
+            pl.BlockSpec((1, rows, width), lambda r: (r, 0, 0)),
+            pl.BlockSpec((1, rows, rows), lambda r: (r, 0, 0)),
+            pl.BlockSpec((1, 1, orbitals, rows), lambda r: (r, slot, 0, 0)),
+        ]
+        + [pl.BlockSpec(memory_space=pl.ANY)] * len(before),
+        out_specs=[
+            pl.BlockSpec((1, 1, rows, width), lambda r: (r, slot, 0, 0)),
+            pl.BlockSpec((1, 1, orbitals, rows), lambda r: (r, 0, 0, 0)),
+        ],
+        input_output_aliases={3: 0} if before else {},
+        compiler_params=PARAMS,
+        cost_estimate=COST,
+    )(totals, row_vals, col_vals, *before)
+
+
+def energies(place, partners, domains, occ_energy, vir_energy):
+    blocks, domain = domains.shape
+    orbitals = occ_energy.shape[1]
+    here, slots = partners.shape
+    tables = vir_energy.shape[0] // domain
+
+    def kernel(place_ref, partners_ref, occ_ref, domains_ref, vir_ref, row_ref, col_ref, picked):
+        at = domains_ref[...]
+        lane, table = lax.rem(at, domain), lax.div(at, domain)
+        vir = jnp.zeros(at.shape, F32)
+        for t in range(tables):
+            values = jnp.broadcast_to(vir_ref[t : t + 1, :], at.shape)
+            vir = jnp.where(table == t, jnp.take_along_axis(values, lane, axis=1), vir)
+        picked[...] = vir
+        z, p = place_ref[0], place_ref[1]
+        for r in range(here):
+            block = here * z + r
+            value = occ_ref[p, block] - picked[pl.ds(block, 1), :]
+            row_ref[r] = jnp.broadcast_to(value, (domain, domain)).T
+            for s in range(slots):
+                other = partners_ref[r, s]
+                value = picked[pl.ds(other, 1), :]
+                for j in range(orbitals):
+                    col_ref[r, s, j : j + 1, :] = occ_ref[j, other] - value
+
+    return pl.pallas_call(
+        kernel,
+        out_shape=[shape(here, domain, domain), shape(here, slots, orbitals, domain)],
+        in_specs=[SMEM] * 3 + [VMEM] * 2,
+        out_specs=[VMEM] * 2,
+        scratch_shapes=[pltpu.VMEM((blocks, domain), F32)],
+        compiler_params=PARAMS,
+    )(place, partners, occ_energy.T, domains, vir_energy.reshape(tables, domain))
+
+
+def fast(half_ints, partners, domains, occ_energy, vir_energy):
+    depth, _, orbitals, domain = half_ints.shape
+    count = lax.axis_size("aux")
+    z, p = lax.axis_index("aux"), lax.axis_index("pair")
+    place = jnp.stack([z, p]).astype(jnp.int32)
+    sides = [[], []]
+    for i in range(count - 1):
+        sides[i % 2] += [(i, i + 1), (i + 1, i)]
+    swap = [(i, i ^ 1) for i in range(4)]
+    cross = [(i, i ^ 2) for i in range(4)]
+    choice = partners - 2 * z + 2
+
+    low_here, own_here, high_here, *sends = pack(place, half_ints, count)
+    own = [own_here]
+    for k, send in enumerate(sends, 1):
+        own.append(lax.ppermute(send, "aux", [(i, (i + k) % count) for i in range(count)]))
+    row_vals, col_vals = energies(place, partners, domains, occ_energy, vir_energy)
+    messages = relay(place, own, 2 * orbitals * depth)
+    near = [lax.ppermute(m, "aux", side) for m, side in zip(messages, sides)]
+    place, _ = lax.optimization_barrier((place, messages))
+    *sums, peak = own_pairs(place, own, orbitals)
+
+    peak = jnp.maximum(peak, lax.ppermute(peak, "pair", swap))
+    top = jnp.maximum(jnp.max(peak), 1e-17)
+    exponent = jnp.ceil(jnp.log2(top * top * (2 * count * depth))) - 15
+    to_half = jnp.exp2(-exponent)
+
+    def reduce(mine, other, give, more=()):
+        got = lax.ppermute(give, "pair", swap)
+        half = ((other + got[1]) * to_half).reshape(2 * domain, -1)
+        half = jnp.concatenate([half, *more]).astype(F16)
+        return mine, got[0], lax.ppermute(half, "pair", cross)
+
+    out = partners.shape + (domain, orbitals * domain)
+    parts = [reduce(*sums, [jnp.full((8, orbitals * domain), exponent)])]
+    from_half = jnp.exp2(parts[0][2][2 * domain, 0].astype(F32))
+    place, _ = lax.optimization_barrier((place, parts[0][2]))
+    sums = near_pairs(place, choice, own, (low_here, high_here), near, orbitals)
+    parts += [reduce(*sums[:3]), reduce(*sums[3:])]
+    amps, energy = [], []
+    for slot, (mine, got, across) in enumerate(parts):
+        across = across[: 2 * domain].astype(F32).reshape(mine.shape)
+        total = mine + got + across * from_half
+        *amps, part = finish(total, row_vals, col_vals, slot, amps, out)
+        energy.append(part)
+    amps = amps[0]
+    energy = jnp.concatenate(energy, axis=1).sum(axis=3)
+    energy = energy / (domain * domain)
+    mask = (jnp.arange(orbitals) == p)[None, None, :, None]
+    energy = jnp.where(mask, energy[:, :, None, :], 0.0)
+    others = [lax.ppermute(energy, "pair", [(i, i ^ k) for i in range(4)]) for k in (1, 2, 3)]
+    return amps, energy + others[0] + others[1] + others[2]
 
 
 def padded(shard, sides, width):
@@ -17,7 +328,7 @@
     return shard
 
 
-def on_device(half_ints, partners, domains, occ_energy, vir_energy):
+def general(half_ints, partners, domains, occ_energy, vir_energy):
     blocks_here, slots = partners.shape
     orbitals = half_ints.shape[2]
     domain = half_ints.shape[3]
@@ -64,6 +375,14 @@
     )
     pair_energy = lax.psum(partial_energy, "pair") / (domain * domain)
     return (amplitudes, pair_energy)
+
+
+def on_device(half_ints, partners, domains, occ_energy, vir_energy):
+    _, _, orbitals, domain = half_ints.shape
+    fits = partners.shape[0] == 2 and domain == 128 and vir_energy.shape[0] % domain == 0
+    fits &= lax.axis_size("pair") == orbitals == 4 and lax.axis_size("aux") % 2 == 0
+    step = fast if fits and half_ints.shape[0] % 16 == 0 else general
+    return step(half_ints, partners, domains, occ_energy, vir_energy)
 
 
 def solution(mesh):

time: 144 us -> 68.2 us (0.47)
  waiting for transfers between devices: 79.1 us -> 27.8 us
  local copies, waits for them, and re-layouts: 16.1 us -> 2.37 us
  between operations: 14.2 us -> 2.25 us
  Pallas kernels: 0 us -> 11.2 us
  blocking collectives: 10.1 us -> 0 us
  starting transfers between devices: 12.2 us -> 19.2 us
  matrix products: 6.4 us -> 0 us
    reduce_scatter x1 -> x0, waiting for transfers between devices: 50.7 us -> none  [on_device(): lax.psum_scatter(partial_terms, 'pair', scatter_dimension=2, tiled=True)]
    all_to_all x1 -> x0, waiting for transfers between devices: 17.3 us -> none  [on_device(): lax.all_to_all(half_ints, 'aux', split_axis=1, concat_axis=0, tiled=True)]
    ppermute x2 -> x15, waiting for transfers between devices: 11.1 us -> 27.8 us  [the longest x3 13.2 us: reduce(): return (mine, got[0], lax.ppermute(half, 'pair', cross))]
    ppermute x2 -> x15, starting transfers between devices: 5.88 us -> 19.2 us  [the longest x3 6.96 us: fast(): lax.ppermute(send, 'aux', [(i, (i + k) % count) for i in range(count)])]
    pallas_call x0 -> x8, Pallas kernels: none -> 11.2 us  [the longest x1 3.18 us: near_pairs(): pl.pallas_call(kernel, out_shape=tiles * 2, in_specs=[SMEM, SMEM] + [VMEM...]
    psum x1 -> x0, blocking collectives: 10.1 us -> none  [on_device(): pair_energy = lax.psum(partial_energy, 'pair') / (domain * domain)]
    gather x12 -> x0, local copies, waits for them, and re-layouts: 9.01 us -> none  [the longest x2 3.2 us: on_device(): jnp.take(vir_energy, jnp.take(domains, partners, axis=0), axis=0)]
    dot_general x2 -> x0, matrix products: 6.4 us -> none  [the longest x1 6.12 us: on_device(): jnp.einsum('qlr,qlsc->lsrc', own_blocks, partner_rows, preferred_element_...]
  transfers between devices with their start and end apart: 4 -> 15, of which waited for: 4 -> 8; matrix products, arithmetic and copies ran while one was open for 7% -> 6% of each run, Pallas kernels for 0% -> 4%
where the time goes in v1:
time: 68.2 us; the launch traced here: 67.4 us
  waiting for transfers between devices  27.8 us (41%)
  starting transfers between devices  19.2 us (28%)
  Pallas kernels  11.2 us (16%)
  other arithmetic  4.65 us (7%)
  local copies, waits for them, and re-layouts  2.37 us (3%)
  between operations  2.25 us (3%)
    ppermute x3, waiting for transfers between devices, reduce(): return (mine, got[0], lax.ppermute(half, 'pair', cross))  13.2 us
    ppermute x3, waiting for transfers between devices, fast(): lax.ppermute(send, 'aux', [(i, (i + k) % count) for i in range(count)])  9.66 us
    ppermute x3, starting transfers between devices, fast(): lax.ppermute(send, 'aux', [(i, (i + k) % count) for i in range(count)])  6.96 us
    ppermute x2, starting transfers between devices, fast(): near = [lax.ppermute(m, 'aux', side) for m, side in zip(messages, sides)]  5.51 us
    ppermute x3, starting transfers between devices, reduce(): return (mine, got[0], lax.ppermute(half, 'pair', cross))  3.71 us
    pallas_call x1, Pallas kernels, near_pairs(): pl.pallas_call(kernel, out_shape=tiles * 2, in_specs=[SMEM, SMEM] + [VMEM...  3.18 us
    ppermute x3, waiting for transfers between devices, fast(): lax.ppermute(energy, 'pair', [(i, i ^ k) for i in range(4)])  2.82 us
    pallas_call x3, Pallas kernels, finish(): pl.pallas_call(kernel, grid=(blocks,), out_shape=[shape(*out), shape(bloc...  2.61 us
  transfers between devices with their start and end apart: 15, of which 8 were waited for; matrix products, arithmetic and copies ran while one was open for 6% of the time, Pallas kernels for 4%

profile of v1, /device:TPU:0, one launch (start us, length us, event | category | flops | bytes accessed | tf_op | source)
XLA Modules:
  0.0 67.4 jit_solution(847256974307391839)
XLA Ops:
  0.7 1.1 %copy-done.4 = bf16[80,8,4,128]{3,2,1,0:T(4,128)(2,1)S(1)} copy-done((bf16[80,8,4,128]{3,2,1,0:T(4,128)(2,1)S(1)}, bf16[80,8,4,128]{3,2,1,0:T(4,128)(2,1)}, u32[]{:S(2)}) %copy-start.4) | copy-done | bytes 655384
  1.8 1.8 %shard_map.68 = (bf16[656,128]{1,0:T(8,128)(2,1)S(1)}, bf16[656,128]{1,0:T(8,128)(2,1)S(1)}, bf16[656,128]{1,0:T(8,128)(2,1)S(1)}, bf16[656,128]{1,0:T(8,128)(2,...) custom-call(s32[2]{0:T(128)S(1)} %pad_add_fusion.place_ref, bf16[2560,128]{1,0:T(8,128)(2,1)S(1)} %bitcast.56), custom_call_target="tpu_custom_call" | custom-call | flops 20000000000 | bytes 40000000 | tf_op jit(solution)/shard_map/pallas_call | solution.py:47
  4.3 3.0 %collective-permute-start = (bf16[656,128]{1,0:T(8,128)(2,1)S(1)}, bf16[656,128]{1,0:T(8,128)(2,1)S(1)}, u32[]{:S(2)}, u32[]{:S(2)}) collective-permute-start(bf16[656,128]{1,0:T(8,128)(2,1)S(1)} %get-tuple-element.31), channel_id=1, source_target_pairs={{0,4},{4,8},{8,12},{12,0},{1,5},{5,9},{9,13},{13,1},{2,6},{6,10},{... | collective-permute-start | bytes 503816 | tf_op jit(solution)/shard_map/ppermute | solution.py:279
  7.3 2.6 %collective-permute-start.1 = (bf16[656,128]{1,0:T(8,128)(2,1)S(1)}, bf16[656,128]{1,0:T(8,128)(2,1)S(1)}, u32[]{:S(2)}, u32[]{:S(2)}) collective-permute-start(bf16[656,128]{1,0:T(8,128)(2,1)S(1)} %get-tuple-element.32), channel_id=1, source_target_pairs={{0,8},{4,12},{8,0},{12,4},{1,9},{5,13},{9,1},{13,5},{2,10},{6,14},... | collective-permute-start | bytes 503816 | tf_op jit(solution)/shard_map/ppermute | solution.py:279
  9.9 1.3 %collective-permute-start.2 = (bf16[656,128]{1,0:T(8,128)(2,1)S(1)}, bf16[656,128]{1,0:T(8,128)(2,1)S(1)}, u32[]{:S(2)}, u32[]{:S(2)}) collective-permute-start(bf16[656,128]{1,0:T(8,128)(2,1)S(1)} %get-tuple-element.33), channel_id=1, source_target_pairs={{0,12},{4,0},{8,4},{12,8},{1,13},{5,1},{9,5},{13,9},{2,14},{6,2},{... | collective-permute-start | bytes 503816 | tf_op jit(solution)/shard_map/ppermute | solution.py:279
  11.3 3.3 %collective-permute-done.refs_1_ = bf16[656,128]{1,0:T(8,128)(2,1)S(1)} collective-permute-done((bf16[656,128]{1,0:T(8,128)(2,1)S(1)}, bf16[656,128]{1,0:T(8,128)(2,1)S(1)}, u32[]{:S(2)}, u32[]{:S(2)}) %collective-permute-start) | collective-permute-done | bytes 167968 | tf_op jit(solution)/shard_map/ppermute | solution.py:279
  14.6 6.4 %collective-permute-done.1.refs_2_ = bf16[656,128]{1,0:T(8,128)(2,1)S(1)} collective-permute-done((bf16[656,128]{1,0:T(8,128)(2,1)S(1)}, bf16[656,128]{1,0:T(8,128)(2,1)S(1)}, u32[]{:S(2)}, u32[]{:S(2)}) %collective-permute-start.1) | collective-permute-done | bytes 167968 | tf_op jit(solution)/shard_map/ppermute | solution.py:279
  20.9 1.5 %shard_map.69 = (bf16[1920,128]{1,0:T(8,128)(2,1)}, bf16[1920,128]{1,0:T(8,128)(2,1)S(1)}) custom-call(s32[2]{0:T(128)S(1)} %pad_add_fusion.place_ref, bf16[656,128]{1,0:T(8,128)(2,1)S(1)} %get-tuple-element.30.refs_0_, bf16[656,128]{1,0:T(8,128)(2,1)S(1)} %collective-permute-done.refs_1_, bf16[656,128]{1,0:T(8,128)(2,1)S(1)} %collective-permute-done.1.refs_2_, ...), custom_call_target="tpu_custom_call" | custom-call | flops 20000000000 | bytes 40000000 | tf_op jit(solution)/shard_map/pallas_call | solution.py:71
  22.4 1.3 %shard_map.70 = (f32[2,128,512]{2,1,0:T(8,128)S(1)}, f32[2,128,512]{2,1,0:T(8,128)S(1)}, f32[2,2,128,512]{3,2,1,0:T(8,128)S(1)}, f32[16,128]{1,0:T(8,128)S(1)}) custom-call(s32[2]{0:T(128)S(1)} %pad_add_fusion.place_ref, bf16[656,128]{1,0:T(8,128)(2,1)S(1)} %get-tuple-element.30.refs_0_, bf16[656,128]{1,0:T(8,128)(2,1)S(1)} %collective-permute-done.refs_1_, ...), custom_call_target="tpu_custom_call" | custom-call | flops 20000000000 | bytes 40000000 | tf_op jit(solution)/shard_map/pallas_call | solution.py:121
  24.3 4.1 %collective-permute-start.6 = (bf16[1920,128]{1,0:T(8,128)(2,1)}, bf16[1920,128]{1,0:T(8,128)(2,1)S(1)}, u32[]{:S(2)}, u32[]{:S(2)}) collective-permute-start(bf16[1920,128]{1,0:T(8,128)(2,1)} %get-tuple-element.34), channel_id=1, source_target_pairs={{0,4},{4,0},{8,12},{12,8},{1,5},{5,1},{9,13},{13,9},{2,6},{6,2},{1... | collective-permute-start | bytes 1474568 | tf_op jit(solution)/shard_map/ppermute | solution.py:282
  28.4 1.5 %collective-permute-start.7 = (bf16[1920,128]{1,0:T(8,128)(2,1)S(1)}, bf16[1920,128]{1,0:T(8,128)(2,1)}, u32[]{:S(2)}, u32[]{:S(2)}) collective-permute-start(bf16[1920,128]{1,0:T(8,128)(2,1)S(1)} %get-tuple-element.35), channel_id=1, source_target_pairs={{4,8},{8,4},{5,9},{9,5},{6,10},{10,6},{7,11},{11,7},{20,24},{24,20... | collective-permute-start | bytes 1474568 | tf_op jit(solution)/shard_map/ppermute | solution.py:282
  31.1 1.2 %fusion.14 = f16[2,128,512]{2,1,0:T(8,128)(2,1)S(1)} fusion(f32[2,128,512]{2,1,0:T(8,128)S(1)} %get-tuple-element.37, f32[2,2,128,512]{3,2,1,0:T(8,128)} %collective-permute-done.3, f32[]{:T(128)S(6)} %exp2.17), kind=kLoop, calls=%fused_computation.20 | loop fusion | flops 393216 | bytes 1310724 | tf_op jit(solution)/shard_map/convert.2
  32.4 1.6 %collective-permute-start.5 = (f16[264,512]{1,0:T(8,128)(2,1)S(1)}, f16[264,512]{1,0:T(8,128)(2,1)S(1)}, u32[]{:S(2)}, u32[]{:S(2)}) collective-permute-start(f16[264,512]{1,0:T(8,128)(2,1)S(1)} %concatenate.6), channel_id=1, source_target_pairs={{0,2},{1,3},{2,0},{3,1},{4,6},{5,7},{6,4},{7,5},{8,10},{9,11},{10,... | collective-permute-start | bytes 811016 | tf_op jit(solution)/shard_map/ppermute | solution.py:295
  34.0 6.7 %collective-permute-done.5 = f16[264,512]{1,0:T(8,128)(2,1)S(1)} collective-permute-done((f16[264,512]{1,0:T(8,128)(2,1)S(1)}, f16[264,512]{1,0:T(8,128)(2,1)S(1)}, u32[]{:S(2)}, u32[]{:S(2)}) %collective-permute-start.5) | collective-permute-done | bytes 270368 | tf_op jit(solution)/shard_map/ppermute | solution.py:295
  40.8 3.2 %shard_map.71 = (f32[2,128,512]{2,1,0:T(8,128)S(1)}, f32[2,128,512]{2,1,0:T(8,128)S(1)}, f32[2,2,128,512]{3,2,1,0:T(8,128)S(1)}, f32[2,128,512]{2,1,0:T(8,128)S(...) custom-call(s32[2]{0:T(128)S(1)} %pad_add_fusion.place_ref, s32[2,3]{1,0:T(2,128)S(1)} %subtract_add_fusion.choice_ref, ...), custom_call_target="tpu_custom_call" | custom-call | flops 20000000000 | bytes 40000000 | tf_op jit(solution)/shard_map/pallas_call | solution.py:184
  44.5 2.1 %collective-permute-done.10 = f32[2,2,128,512]{3,2,1,0:T(8,128)S(1)} collective-permute-done((f32[2,2,128,512]{3,2,1,0:T(8,128)S(1)}, f32[2,2,128,512]{3,2,1,0:T(8,128)S(1)}, u32[]{:S(2)}, u32[]{:S(2)}) %collective-permute-start.10) | collective-permute-done | bytes 1048608 | tf_op jit(solution)/shard_map/ppermute | solution.py:292
  46.8 1.6 %collective-permute-start.11 = (f16[256,512]{1,0:T(8,128)(2,1)S(1)}, f16[256,512]{1,0:T(8,128)(2,1)S(1)}, u32[]{:S(2)}, u32[]{:S(2)}) collective-permute-start(f16[256,512]{1,0:T(8,128)(2,1)S(1)} %bitcast.62), channel_id=1, source_target_pairs={{0,2},{1,3},{2,0},{3,1},{4,6},{5,7},{6,4},{7,5},{8,10},{9,11},{10,... | collective-permute-start | bytes 786440 | tf_op jit(solution)/shard_map/ppermute | solution.py:295
  51.1 4.9 %collective-permute-done.11 = f16[256,512]{1,0:T(8,128)(2,1)S(1)} collective-permute-done((f16[256,512]{1,0:T(8,128)(2,1)S(1)}, f16[256,512]{1,0:T(8,128)(2,1)S(1)}, u32[]{:S(2)}, u32[]{:S(2)}) %collective-permute-start.11) | collective-permute-done | bytes 262176 | tf_op jit(solution)/shard_map/ppermute | solution.py:295
  56.1 1.2 %fusion.1.total_ref = f32[2,128,512]{2,1,0:T(8,128)S(1)} fusion(f32[2,128,512]{2,1,0:T(8,128)S(1)} %bitcast.58, f32[2,128,512]{2,1,0:T(8,128)S(1)} %get-tuple-element.51, f32[2,2,128,512]{3,2,1,0:T(8,128)} %collective-permute-done.3), kind=kLoop, calls=%fused_computation.2 | loop fusion | flops 262144 | bytes 2097152 | tf_op jit(solution)/shard_map/add | solution.py:306
  58.3 0.9 %shard_map.74 = (f32[2,3,128,512]{3,2,1,0:T(8,128)}, f32[2,1,4,128]{3,2,1,0:T(4,128)S(1)}) custom-call(f32[2,128,512]{2,1,0:T(8,128)S(1)} %fusion.6.total_ref, f32[2,128,128]{2,1,0:T(8,128)S(1)} %get-tuple-element.46.row_ref, f32[2,3,4,128]{3,2,1,0:T(4,128)S(1)} %get-tuple-element.47.col_ref, ...), custom_call_target="tpu_custom_call", output_to_operand_aliasing={{0}: (3, {})} | custom-call | flops 20000000000 | bytes 40000000 | tf_op jit(solution)/shard_map/pallas_call | solution.py:209
  59.2 1.6 %collective-permute-done.9 = f16[256,512]{1,0:T(8,128)(2,1)S(1)} collective-permute-done((f16[256,512]{1,0:T(8,128)(2,1)S(1)}, f16[256,512]{1,0:T(8,128)(2,1)S(1)}, u32[]{:S(2)}, u32[]{:S(2)}) %collective-permute-start.9) | collective-permute-done | bytes 262176 | tf_op jit(solution)/shard_map/ppermute | solution.py:295
  62.1 1.6 %collective-permute-start.13 = (f32[2,3,4,4]{3,2,1,0:T(4,128)S(1)}, f32[2,3,4,4]{3,2,1,0:T(4,128)S(1)}, u32[]{:S(2)}, u32[]{:S(2)}) collective-permute-start(f32[2,3,4,4]{3,2,1,0:T(4,128)S(1)} %broadcast_select_fusion), channel_id=1, source_target_pairs={{0,2},{1,3},{2,0},{3,1},{4,6},{5,7},{6,4},{7,5},{8,10},{9,11},{10,... | collective-permute-start | bytes 1160 | tf_op jit(solution)/shard_map/ppermute | solution.py:314
  63.9 1.9 %collective-permute-done.13 = f32[2,3,4,4]{3,2,1,0:T(4,128)S(1)} collective-permute-done((f32[2,3,4,4]{3,2,1,0:T(4,128)S(1)}, f32[2,3,4,4]{3,2,1,0:T(4,128)S(1)}, u32[]{:S(2)}, u32[]{:S(2)}) %collective-permute-start.13) | collective-permute-done | bytes 416 | tf_op jit(solution)/shard_map/ppermute | solution.py:314
  65.8 0.9 %collective-permute-done.14 = f32[2,3,4,4]{3,2,1,0:T(4,128)S(1)} collective-permute-done((f32[2,3,4,4]{3,2,1,0:T(4,128)S(1)}, f32[2,3,4,4]{3,2,1,0:T(4,128)S(1)}, u32[]{:S(2)}, u32[]{:S(2)}) %collective-permute-start.14) | collective-permute-done | bytes 416 | tf_op jit(solution)/shard_map/ppermute | solution.py:314
  (58 shorter events, 8.1 us)
Async XLA Ops:
  4.3 18.1 %copy-start.11 = (bf16[656,128]{1,0:T(8,128)(2,1)}, bf16[656,128]{1,0:T(8,128)(2,1)S(1)}, u32[]{:S(2)}) copy-start(bf16[656,128]{1,0:T(8,128)(2,1)S(1)} %get-tuple-element.42.refs_5_) | copy-start | bytes 503812
  4.3 18.1 %copy-start.9 = (bf16[656,128]{1,0:T(8,128)(2,1)}, bf16[656,128]{1,0:T(8,128)(2,1)S(1)}, u32[]{:S(2)}) copy-start(bf16[656,128]{1,0:T(8,128)(2,1)S(1)} %get-tuple-element.30.refs_0_) | copy-start | bytes 503812
  4.3 10.3 %collective-permute-start = (bf16[656,128]{1,0:T(8,128)(2,1)S(1)}, bf16[656,128]{1,0:T(8,128)(2,1)S(1)}, u32[]{:S(2)}, u32[]{:S(2)}) collective-permute-start(bf16[656,128]{1,0:T(8,128)(2,1)S(1)} %get-tuple-element.31), channel_id=1, source_target_pairs={{0,4},{4,8},{8,12},{12,0},{1,5},{5,9},{9,13},{13,1},{2,6},{6,10},{... | collective-permute-start | bytes 503816 | tf_op jit(solution)/shard_map/ppermute | solution.py:279
  7.3 13.6 %collective-permute-start.1 = (bf16[656,128]{1,0:T(8,128)(2,1)S(1)}, bf16[656,128]{1,0:T(8,128)(2,1)S(1)}, u32[]{:S(2)}, u32[]{:S(2)}) collective-permute-start(bf16[656,128]{1,0:T(8,128)(2,1)S(1)} %get-tuple-element.32), channel_id=1, source_target_pairs={{0,8},{4,12},{8,0},{12,4},{1,9},{5,13},{9,1},{13,5},{2,10},{6,14},... | collective-permute-start | bytes 503816 | tf_op jit(solution)/shard_map/ppermute | solution.py:279
  9.9 11.0 %collective-permute-start.2 = (bf16[656,128]{1,0:T(8,128)(2,1)S(1)}, bf16[656,128]{1,0:T(8,128)(2,1)S(1)}, u32[]{:S(2)}, u32[]{:S(2)}) collective-permute-start(bf16[656,128]{1,0:T(8,128)(2,1)S(1)} %get-tuple-element.33), channel_id=1, source_target_pairs={{0,12},{4,0},{8,4},{12,8},{1,13},{5,1},{9,5},{13,9},{2,14},{6,2},{... | collective-permute-start | bytes 503816 | tf_op jit(solution)/shard_map/ppermute | solution.py:279
  23.7 10.3 %copy-start.2 = (s32[2,3]{1,0:T(2,128)S(1)}, s32[2,3]{1,0:T(2,128)}, u32[]{:S(2)}) copy-start(s32[2,3]{1,0:T(2,128)} %partners_ref.1) | copy-start | bytes 76
  23.7 7.4 %collective-permute-start.3 = (f32[2,2,128,512]{3,2,1,0:T(8,128)S(1)}, f32[2,2,128,512]{3,2,1,0:T(8,128)}, u32[]{:S(2)}, u32[]{:S(2)}) collective-permute-start(f32[2,2,128,512]{3,2,1,0:T(8,128)S(1)} %get-tuple-element.38), channel_id=1, source_target_pairs={{0,1},{1,0},{2,3},{3,2},{4,5},{5,4},{6,7},{7,6},{8,9},{9,8},{10,11... | collective-permute-start | bytes 3145736 | tf_op jit(solution)/shard_map/ppermute | solution.py:292
  23.8 6.0 %collective-permute-start.4 = (f32[16,128]{1,0:T(8,128)S(1)}, f32[16,128]{1,0:T(8,128)S(1)}, u32[]{:S(2)}, u32[]{:S(2)}) collective-permute-start(f32[16,128]{1,0:T(8,128)S(1)} %get-tuple-element.39), channel_id=1, source_target_pairs={{0,1},{1,0},{2,3},{3,2},{4,5},{5,4},{6,7},{7,6},{8,9},{9,8},{10,11... | collective-permute-start | bytes 24584 | tf_op jit(solution)/shard_map/ppermute | solution.py:286
  24.3 16.4 %collective-permute-start.6 = (bf16[1920,128]{1,0:T(8,128)(2,1)}, bf16[1920,128]{1,0:T(8,128)(2,1)S(1)}, u32[]{:S(2)}, u32[]{:S(2)}) collective-permute-start(bf16[1920,128]{1,0:T(8,128)(2,1)} %get-tuple-element.34), channel_id=1, source_target_pairs={{0,4},{4,0},{8,12},{12,8},{1,5},{5,1},{9,13},{13,9},{2,6},{6,2},{1... | collective-permute-start | bytes 1474568 | tf_op jit(solution)/shard_map/ppermute | solution.py:282
  28.4 12.3 %collective-permute-start.7 = (bf16[1920,128]{1,0:T(8,128)(2,1)S(1)}, bf16[1920,128]{1,0:T(8,128)(2,1)}, u32[]{:S(2)}, u32[]{:S(2)}) collective-permute-start(bf16[1920,128]{1,0:T(8,128)(2,1)S(1)} %get-tuple-element.35), channel_id=1, source_target_pairs={{4,8},{8,4},{5,9},{9,5},{6,10},{10,6},{7,11},{11,7},{20,24},{24,20... | collective-permute-start | bytes 1474568 | tf_op jit(solution)/shard_map/ppermute | solution.py:282
  31.1 9.6 %copy-start.6 = (bf16[656,128]{1,0:T(8,128)(2,1)S(1)}, bf16[656,128]{1,0:T(8,128)(2,1)}, u32[]{:S(2)}) copy-start(bf16[656,128]{1,0:T(8,128)(2,1)} %copy-done.5) | copy-start | bytes 503812
  31.1 9.6 %copy-start.8 = (bf16[656,128]{1,0:T(8,128)(2,1)S(1)}, bf16[656,128]{1,0:T(8,128)(2,1)}, u32[]{:S(2)}) copy-start(bf16[656,128]{1,0:T(8,128)(2,1)} %copy-done.7) | copy-start | bytes 503812
  31.1 9.6 %copy-start.10 = (bf16[656,128]{1,0:T(8,128)(2,1)S(1)}, bf16[656,128]{1,0:T(8,128)(2,1)}, u32[]{:S(2)}) copy-start(bf16[656,128]{1,0:T(8,128)(2,1)} %copy-done.9) | copy-start | bytes 503812
  31.1 9.6 %copy-start.12 = (bf16[656,128]{1,0:T(8,128)(2,1)S(1)}, bf16[656,128]{1,0:T(8,128)(2,1)}, u32[]{:S(2)}) copy-start(bf16[656,128]{1,0:T(8,128)(2,1)} %copy-done.11) | copy-start | bytes 503812
  32.4 8.3 %collective-permute-start.5 = (f16[264,512]{1,0:T(8,128)(2,1)S(1)}, f16[264,512]{1,0:T(8,128)(2,1)S(1)}, u32[]{:S(2)}, u32[]{:S(2)}) collective-permute-start(f16[264,512]{1,0:T(8,128)(2,1)S(1)} %concatenate.6), channel_id=1, source_target_pairs={{0,2},{1,3},{2,0},{3,1},{4,6},{5,7},{6,4},{7,5},{8,10},{9,11},{10,... | collective-permute-start | bytes 811016 | tf_op jit(solution)/shard_map/ppermute | solution.py:295
  40.7 7.6 %copy-start = (s32[8,128]{1,0:T(8,128)S(1)}, s32[8,128]{1,0:T(8,128)}, u32[]{:S(2)}) copy-start(s32[8,128]{1,0:T(8,128)} %domains_ref.1) | copy-start | bytes 12292
  40.7 7.6 %copy-start.1 = (f32[1024]{0:T(1024)S(1)}, f32[1024]{0:T(1024)}, u32[]{:S(2)}) copy-start(f32[1024]{0:T(1024)} %param.9) | copy-start | bytes 12292
  43.9 2.7 %collective-permute-start.10 = (f32[2,2,128,512]{3,2,1,0:T(8,128)S(1)}, f32[2,2,128,512]{3,2,1,0:T(8,128)S(1)}, u32[]{:S(2)}, u32[]{:S(2)}) collective-permute-start(f32[2,2,128,512]{3,2,1,0:T(8,128)S(1)} %get-tuple-element.49), channel_id=1, source_target_pairs={{0,1},{1,0},{2,3},{3,2},{4,5},{5,4},{6,7},{7,6},{8,9},{9,8},{10,11... | collective-permute-start | bytes 3145736 | tf_op jit(solution)/shard_map/ppermute | solution.py:292
  44.0 6.3 %collective-permute-start.8 = (f32[2,2,128,512]{3,2,1,0:T(8,128)S(1)}, f32[2,2,128,512]{3,2,1,0:T(8,128)S(1)}, u32[]{:S(2)}, u32[]{:S(2)}) collective-permute-start(f32[2,2,128,512]{3,2,1,0:T(8,128)S(1)} %get-tuple-element.44), channel_id=1, source_target_pairs={{0,1},{1,0},{2,3},{3,2},{4,5},{5,4},{6,7},{7,6},{8,9},{9,8},{10,11... | collective-permute-start | bytes 3145736 | tf_op jit(solution)/shard_map/ppermute | solution.py:292
  46.8 9.2 %collective-permute-start.11 = (f16[256,512]{1,0:T(8,128)(2,1)S(1)}, f16[256,512]{1,0:T(8,128)(2,1)S(1)}, u32[]{:S(2)}, u32[]{:S(2)}) collective-permute-start(f16[256,512]{1,0:T(8,128)(2,1)S(1)} %bitcast.62), channel_id=1, source_target_pairs={{0,2},{1,3},{2,0},{3,1},{4,6},{5,7},{6,4},{7,5},{8,10},{9,11},{10,... | collective-permute-start | bytes 786440 | tf_op jit(solution)/shard_map/ppermute | solution.py:295
  50.5 10.3 %collective-permute-start.9 = (f16[256,512]{1,0:T(8,128)(2,1)S(1)}, f16[256,512]{1,0:T(8,128)(2,1)S(1)}, u32[]{:S(2)}, u32[]{:S(2)}) collective-permute-start(f16[256,512]{1,0:T(8,128)(2,1)S(1)} %bitcast.61), channel_id=1, source_target_pairs={{0,2},{1,3},{2,0},{3,1},{4,6},{5,7},{6,4},{7,5},{8,10},{9,11},{10,... | collective-permute-start | bytes 786440 | tf_op jit(solution)/shard_map/ppermute | solution.py:295
  62.1 1.9 %collective-permute-start.12 = (f32[2,3,4,4]{3,2,1,0:T(4,128)S(1)}, f32[2,3,4,4]{3,2,1,0:T(4,128)S(1)}, u32[]{:S(2)}, u32[]{:S(2)}) collective-permute-start(f32[2,3,4,4]{3,2,1,0:T(4,128)S(1)} %broadcast_select_fusion), channel_id=1, source_target_pairs={{0,1},{1,0},{2,3},{3,2},{4,5},{5,4},{6,7},{7,6},{8,9},{9,8},{10,11... | collective-permute-start | bytes 1160 | tf_op jit(solution)/shard_map/ppermute | solution.py:314
  62.1 3.8 %collective-permute-start.13 = (f32[2,3,4,4]{3,2,1,0:T(4,128)S(1)}, f32[2,3,4,4]{3,2,1,0:T(4,128)S(1)}, u32[]{:S(2)}, u32[]{:S(2)}) collective-permute-start(f32[2,3,4,4]{3,2,1,0:T(4,128)S(1)} %broadcast_select_fusion), channel_id=1, source_target_pairs={{0,2},{1,3},{2,0},{3,1},{4,6},{5,7},{6,4},{7,5},{8,10},{9,11},{10,... | collective-permute-start | bytes 1160 | tf_op jit(solution)/shard_map/ppermute | solution.py:314
  63.6 3.1 %collective-permute-start.14 = (f32[2,3,4,4]{3,2,1,0:T(4,128)S(1)}, f32[2,3,4,4]{3,2,1,0:T(4,128)S(1)}, u32[]{:S(2)}, u32[]{:S(2)}) collective-permute-start(f32[2,3,4,4]{3,2,1,0:T(4,128)S(1)} %broadcast_select_fusion), channel_id=1, source_target_pairs={{0,3},{1,2},{2,1},{3,0},{4,7},{5,6},{6,5},{7,4},{8,11},{9,10},{10,... | collective-permute-start | bytes 1160 | tf_op jit(solution)/shard_map/ppermute | solution.py:314
  (4 other events, 10.8 us)

commit v2 on v0

--- a/solution.py
+++ b/solution.py
@@ -1,7 +1,351 @@
 import jax
 import jax.numpy as jnp
 from jax import lax
+from jax.experimental import pallas as pl
+from jax.experimental.pallas import tpu as pltpu
 from jax.sharding import PartitionSpec as P
+
+BF16, F16, F32 = jnp.bfloat16, jnp.float16, jnp.float32
+VMEM = pl.BlockSpec(memory_space=pltpu.VMEM)
+SMEM = pl.BlockSpec(memory_space=pltpu.SMEM)
+ANY = pl.BlockSpec(memory_space=pl.ANY)
+PARAMS = pltpu.CompilerParams(vmem_limit_bytes=8 * 2**20)
+PEAK_ROWS = 16
+
+def shape(*dims, dtype=F32):
+    return jax.ShapeDtypeStruct(dims, dtype)
+
+
+def call(kernel, name, **options):
+    return pl.pallas_call(kernel, compiler_params=PARAMS, name=name, **options)
+
+
+def after(value, *others):
+    return lax.optimization_barrier((value, *others))[0]
+
+
+def panel_at(depth, orbital, block):
+    return pl.ds((orbital * 2 + block) * depth, depth)
+
+
+def depth_of(one_set, orbitals):
+    return (one_set.shape[0] - PEAK_ROWS) // (2 * orbitals)
+
+
+def pack(raw, count):
+    depth, blocks, orbitals, domain = raw.shape
+    rows, parts = blocks * orbitals, 4
+    part = depth * rows // parts
+
+    def kernel(raw_ref, *refs):
+        outs, wide = refs[:count], refs[-1]
+        z = lax.axis_index("aux")
+        wide[...] = raw_ref[...].astype(F32)
+        peak = jnp.max(jnp.abs(wide[...]).reshape(-1, PEAK_ROWS, domain), axis=0)
+        for k in range(count):
+            out = outs[(k + 1) % count]
+            block = 2 * jnp.bitwise_xor(z, (k + 1) % count)
+            for r in range(2):
+                for i in range(orbitals):
+                    at = pl.ds((block + r) * orbitals + i, depth, stride=rows)
+                    out[panel_at(depth, i, r), :] = wide[at, :].astype(BF16)
+            out[2 * orbitals * depth :, :] = peak.astype(BF16)
+
+    one_set = shape(2 * orbitals * depth + PEAK_ROWS, domain, dtype=BF16)
+    return call(
+        kernel,
+        "pack",
+        out_shape=[one_set] * count,
+        in_specs=[VMEM],
+        out_specs=[VMEM] * count,
+        scratch_shapes=[
+            pltpu.VMEM((depth * rows, domain), F32),
+        ],
+    )(raw.reshape(depth * rows, domain))
+
+
+def relay(own, rows):
+    domain = own[0].shape[1]
+
+    def kernel(*refs):
+        own_refs, outs = refs[:4], refs[4:]
+        for out, partner in zip(outs, (1, 3)):
+            for k in (1, 2, 3):
+                out[(k - 1) * rows : k * rows] = own_refs[k ^ partner][:rows]
+
+    return call(
+        kernel,
+        "relay",
+        out_shape=[shape(3 * rows, domain, dtype=BF16)] * 2,
+        in_specs=[VMEM] * 4,
+        out_specs=[VMEM] * 2,
+    )(*own)
+
+
+def product(left, right):
+    return lax.dot_general(left, right, (((0,), (0,)), ((), ())), preferred_element_type=F32)
+
+
+def left_rows(own_refs, depth, r):
+    p = lax.axis_index("pair")
+    x, c = p // 2, lax.rem(p, 2)
+    order = (2 * x + c, 2 * (1 - x) + c, 2 * x + 1 - c, 2 * (1 - x) + 1 - c)
+    columns = [
+        jnp.concatenate([ref[panel_at(depth, i, r), :] for ref in own_refs], axis=0) for i in order
+    ]
+    return jnp.concatenate(columns, axis=1)
+
+
+def store_sums(sums, r, mine, other, give):
+    domain = sums.shape[0] // 4
+    mine[r] = sums[:domain]
+    other[r] = sums[domain : 2 * domain]
+    give[0, r] = sums[2 * domain : 3 * domain]
+    give[1, r] = sums[3 * domain :]
+
+
+def sum_shapes(orbitals, domain):
+    wide = orbitals * domain
+    return [shape(2, domain, wide), shape(2, domain, wide), shape(2, 2, domain, wide)]
+
+
+def own_pairs(own, orbitals):
+    count, domain = len(own), own[0].shape[1]
+    depth = depth_of(own[0], orbitals)
+
+    def kernel(*refs):
+        own_refs, (mine, other, give, peak) = refs[:count], refs[count:]
+        top = own_refs[0][-PEAK_ROWS:, :].astype(F32)
+        for ref in own_refs[1:]:
+            top = jnp.maximum(top, ref[-PEAK_ROWS:, :].astype(F32))
+        peak[...] = top
+        for r in range(2):
+            right = jnp.concatenate(
+                [
+                    jnp.concatenate([ref[panel_at(depth, j, r), :] for ref in own_refs], axis=0)
+                    for j in range(orbitals)
+                ],
+                axis=1,
+            )
+            store_sums(product(left_rows(own_refs, depth, r), right), r, mine, other, give)
+
+    return call(
+        kernel,
+        "own",
+        out_shape=sum_shapes(orbitals, domain) + [shape(PEAK_ROWS, domain)],
+        in_specs=[VMEM] * count,
+        out_specs=[VMEM] * 4,
+    )(*own)
+
+
+def near_pairs(partners, own, here, sides, orbitals, slot):
+    count, domain = len(own), own[0].shape[1]
+    depth = depth_of(own[0], orbitals)
+    rows = 2 * orbitals * depth
+
+    def kernel(partners_ref, *refs):
+        own_refs, here_refs, side_refs = refs[:count], refs[count : count + 2], refs[count + 2 :][:2]
+        z = lax.axis_index("aux")
+        even = lax.rem(z, 2) == 0
+
+        def panels(w, j):
+            from_first = (w > 3) == even
+            at = (2 * j + lax.rem(w, 2)) * depth
+            found = []
+            for k in range(count):
+                refs, start = (here_refs, at) if k == 0 else (side_refs, at + (k - 1) * rows)
+                rows_at = pl.ds(pl.multiple_of(start, 16), depth)
+                panel = jnp.where(from_first, refs[0][rows_at, :], refs[1][rows_at, :])
+                if slot > 1:
+                    own_at = pl.ds(pl.multiple_of(at, 16), depth)
+                    panel = jnp.where((w == 2) | (w == 3), own_refs[k][own_at, :], panel)
+                found.append(panel)
+            return jnp.concatenate(found, axis=0)
+
+        for r in range(2):
+            w = partners_ref[r, slot] - 2 * z + 2
+            right = jnp.concatenate([panels(w, j) for j in range(orbitals)], axis=1)
+            store_sums(product(left_rows(own_refs, depth, r), right), r, *refs[count + 4 :])
+
+    return call(
+        kernel,
+        f"near{slot}",
+        out_shape=sum_shapes(orbitals, domain),
+        in_specs=[SMEM] + [VMEM] * (count + 4),
+        out_specs=[VMEM] * 3,
+    )(partners, *own, *here, *sides)
+
+
+def scales(first, second, depth, wide):
+    def kernel(first_ref, second_ref, top_ref, down_ref, up_ref):
+        top = jnp.maximum(first_ref[...], second_ref[...])
+        top_ref[...] = top
+        top = jnp.maximum(jnp.max(top, axis=(0, 1), keepdims=True), 1e-17)
+        exponent = jnp.ceil(jnp.log2(top * top * depth)) - 15
+        exponent = jnp.broadcast_to(exponent, down_ref.shape)
+        down_ref[...] = jnp.exp2(-exponent)
+        up_ref[...] = jnp.exp2(exponent)
+
+    return call(
+        kernel,
+        "scales",
+        out_shape=[shape(*first.shape), shape(8, wide), shape(8, wide)],
+        in_specs=[VMEM] * 2,
+        out_specs=[VMEM] * 3,
+    )(first, second)
+
+
+def finish(totals, row_vals, col_vals, slot, before, out):
+    blocks, rows, width = totals.shape
+    orbitals = width // rows
+
+    def kernel(total_ref, row_ref, col_ref, *refs):
+        amp_ref, energy_ref, amp, sems = refs[-4:]
+        copies = []
+        for r in range(blocks):
+            row = row_ref[r]
+            for j in range(orbitals):
+                at = slice(j * rows, (j + 1) * rows)
+                total = total_ref[r, :, at]
+                tile = total / (row + col_ref[r, slot, j : j + 1, :])
+                amp[r, :, at] = tile
+                energy_ref[r, j : j + 1, :] = jnp.sum(total * tile, axis=0, keepdims=True)
+            copies.append(pltpu.make_async_copy(amp.at[r], amp_ref.at[r, slot], sems.at[r]))
+            copies[-1].start()
+        for started in copies:
+            started.wait()
+
+    return call(
+        kernel,
+        "finish",
+        out_shape=[shape(*out), shape(blocks, orbitals, rows)],
+        in_specs=[VMEM] * 3 + [ANY] * len(before),
+        out_specs=[ANY, VMEM],
+        input_output_aliases={3: 0} if before else {},
+        scratch_shapes=[pltpu.VMEM(totals.shape, F32), pltpu.SemaphoreType.DMA((blocks,))],
+    )(totals, row_vals, col_vals, *before)
+
+
+def share_out(shares):
+    blocks, orbitals, domain = shares[0].shape
+    slots = len(shares)
+
+    def kernel(*refs):
+        out = refs[-1]
+        p = lax.axis_index("pair")
+        row = lax.broadcasted_iota(jnp.int32, (orbitals, orbitals), 0)
+        column = lax.broadcasted_iota(jnp.int32, (orbitals, orbitals), 1)
+        for r in range(blocks):
+            for s in range(slots):
+                total = jnp.zeros((orbitals, orbitals), F32)
+                sums = jnp.sum(refs[s][r], axis=1, keepdims=True) * (1.0 / (domain * domain))
+                for j in range(orbitals):
+                    total = jnp.where((row == p) & (column == j), sums[j : j + 1, :], total)
+                out[r, s] = total
+
+    return call(
+        kernel,
+        "share",
+        out_shape=shape(blocks, slots, orbitals, orbitals),
+        in_specs=[VMEM] * slots,
+        out_specs=VMEM,
+    )(*shares)
+
+
+def last(shares):
+    def kernel(*refs):
+        refs[4][...] = (refs[0][...] + refs[1][...]) + (refs[2][...] + refs[3][...])
+
+    return call(
+        kernel,
+        "last",
+        out_shape=shape(*shares[0].shape),
+        in_specs=[VMEM] * 4,
+        out_specs=VMEM,
+    )(*shares)
+
+
+def energies(partners, domains, occ_energy, vir_energy):
+    blocks, domain = domains.shape
+    orbitals = occ_energy.shape[1]
+    here, slots = partners.shape
+    tables = vir_energy.shape[0] // domain
+
+    def kernel(partners_ref, occ_ref, domains_ref, vir_ref, row_ref, col_ref, picked):
+        at = domains_ref[...]
+        lane, table = lax.rem(at, domain), lax.div(at, domain)
+        vir = jnp.zeros(at.shape, F32)
+        for t in range(tables):
+            values = jnp.broadcast_to(vir_ref[t : t + 1, :], at.shape)
+            vir = jnp.where(table == t, jnp.take_along_axis(values, lane, axis=1), vir)
+        picked[...] = vir
+        z, p = lax.axis_index("aux"), lax.axis_index("pair")
+        for r in range(here):
+            block = here * z + r
+            value = occ_ref[p, block] - picked[pl.ds(block, 1), :]
+            row_ref[r] = jnp.broadcast_to(value, (domain, domain)).T
+            for s in range(slots):
+                other = partners_ref[r, s]
+                value = picked[pl.ds(other, 1), :]
+                for j in range(orbitals):
+                    col_ref[r, s, j : j + 1, :] = occ_ref[j, other] - value
+
+    return call(
+        kernel,
+        "energies",
+        out_shape=[shape(here, domain, domain), shape(here, slots, orbitals, domain)],
+        in_specs=[SMEM] * 2 + [VMEM] * 2,
+        out_specs=[VMEM] * 2,
+        scratch_shapes=[pltpu.VMEM((blocks, domain), F32)],
+    )(partners, occ_energy.T, domains, vir_energy.reshape(tables, domain))
+
+
+def fast(half_ints, partners, domains, occ_energy, vir_energy):
+    depth, _, orbitals, domain = half_ints.shape
+    count = lax.axis_size("aux")
+    wide = orbitals * domain
+    sides = [[(i, i ^ 4) for i in range(16)], [(i, i ^ (12 if 4 <= i < 12 else 1)) for i in range(16)]]
+    swap, cross, both = ([(i, i ^ k) for i in range(4)] for k in (1, 2, 3))
+
+    own_here, *sends = pack(half_ints, count)
+    here = [sends[0], sends[2]]
+    own = [own_here]
+    for k, send in enumerate(sends, 1):
+        own.append(lax.ppermute(send, "aux", [(i, i ^ k) for i in range(count)]))
+    row_vals, col_vals = energies(partners, domains, occ_energy, vir_energy)
+    messages = relay(own, 2 * orbitals * depth)
+    near = [lax.ppermute(m, ("aux", "pair"), side) for m, side in zip(messages, sides)]
+    own[0] = after(own[0], *messages)
+
+    def reduce(mine, other, give):
+        got = lax.ppermute(give, "pair", swap)
+        return mine, got[0], ((other + got[1]) * to_half[:1]).astype(F16)
+
+    def cross_over(half):
+        return lax.ppermute(half, "pair", cross)
+
+    *sums, peak = own_pairs(own, orbitals)
+    peak, to_half, _ = scales(peak, lax.ppermute(peak, "pair", swap), 2 * count * depth, wide)
+    peak = lax.ppermute(peak, "pair", cross)
+    _, _, from_half = scales(peak, peak, 2 * count * depth, wide)
+
+    parts = [reduce(*sums)]
+    across = [cross_over(parts[0][2])]
+    here[0] = after(here[0], across[0], from_half, row_vals)
+    parts.append(reduce(*near_pairs(partners, own, here, near, orbitals, 1)))
+    across.append(cross_over(parts[1][2]))
+    here[0] = after(here[0], parts[1][0])
+    mine, other, give = near_pairs(partners, own, here, near, orbitals, 2)
+    parts.append(reduce(mine, other, after(give, parts[1][2])))
+    across.append(cross_over(parts[2][2]))
+    amps, shares = [], []
+    for slot, (mine, got, _) in enumerate(parts):
+        back = after(from_half, shares[-1]) if slot else from_half
+        total = mine + got + across[slot].astype(F32) * back[:1]
+        *amps, share = finish(total, row_vals, col_vals, slot, amps, partners.shape + (domain, wide))
+        shares.append(share)
+    share = share_out(shares)
+    return amps[0], last([share] + [lax.ppermute(share, "pair", to) for to in (swap, cross, both)])
 
 
 def padded(shard, sides, width):
@@ -17,7 +361,7 @@
     return shard
 
 
-def on_device(half_ints, partners, domains, occ_energy, vir_energy):
+def general(half_ints, partners, domains, occ_energy, vir_energy):
     blocks_here, slots = partners.shape
     orbitals = half_ints.shape[2]
     domain = half_ints.shape[3]
@@ -64,6 +408,14 @@
     )
     pair_energy = lax.psum(partial_energy, "pair") / (domain * domain)
     return (amplitudes, pair_energy)
+
+
+def on_device(half_ints, partners, domains, occ_energy, vir_energy):
+    _, _, orbitals, domain = half_ints.shape
+    fits = partners.shape[0] == 2 and domain == 128 and vir_energy.shape[0] % domain == 0
+    fits &= lax.axis_size("pair") == lax.axis_size("aux") == orbitals == 4
+    step = fast if fits and half_ints.shape[0] % 16 == 0 else general
+    return step(half_ints, partners, domains, occ_energy, vir_energy)
 
 
 def solution(mesh):

time: 144 us -> 61.8 us (0.43)
  waiting for transfers between devices: 79.1 us -> 35.3 us
  local copies, waits for them, and re-layouts: 16.1 us -> 1.11 us
  between operations: 14.2 us -> 0.8 us
  blocking collectives: 10.1 us -> 0 us
  Pallas kernels: 0 us -> 9.99 us
  matrix products: 6.4 us -> 0 us
  other arithmetic: 5.1 us -> 0.74 us
  starting transfers between devices: 12.2 us -> 13.8 us
    reduce_scatter x1 -> x0, waiting for transfers between devices: 50.7 us -> none  [on_device(): lax.psum_scatter(partial_terms, 'pair', scatter_dimension=2, tiled=True)]
    ppermute x2 -> x16, waiting for transfers between devices: 11.1 us -> 35.3 us  [the longest x3 13.6 us: fast(): own.append(lax.ppermute(send, 'aux', [(i, i ^ k) for i in range(count)]))]
    all_to_all x1 -> x0, waiting for transfers between devices: 17.3 us -> none  [on_device(): lax.all_to_all(half_ints, 'aux', split_axis=1, concat_axis=0, tiled=True)]
    psum x1 -> x0, blocking collectives: 10.1 us -> none  [on_device(): pair_energy = lax.psum(partial_energy, 'pair') / (domain * domain)]
    pallas_call x0 -> x13, Pallas kernels: none -> 9.99 us  [the longest x2 2.7 us: near_pairs(): call(kernel, f'near{slot}', out_shape=sum_shapes(orbitals, domain), in_sp...]
    gather x12 -> x0, local copies, waits for them, and re-layouts: 9.01 us -> none  [the longest x2 3.2 us: on_device(): jnp.take(vir_energy, jnp.take(domains, partners, axis=0), axis=0)]
    ppermute x2 -> x16, starting transfers between devices: 5.88 us -> 13.8 us  [the longest x3 5.76 us: fast(): own.append(lax.ppermute(send, 'aux', [(i, i ^ k) for i in range(count)]))]
    dot_general x2 -> x0, matrix products: 6.4 us -> none  [the longest x1 6.12 us: on_device(): jnp.einsum('qlr,qlsc->lsrc', own_blocks, partner_rows, preferred_element_...]
  transfers between devices with their start and end apart: 4 -> 16, of which waited for: 4 -> 11; matrix products, arithmetic and copies ran while one was open for 7% -> 1% of each run, Pallas kernels for 0% -> 9%
where the time goes in v2:
time: 61.8 us; the launch traced here: 61.7 us
  waiting for transfers between devices  35.3 us (57%)
  starting transfers between devices  13.8 us (22%)
  Pallas kernels  9.99 us (16%)
  local copies, waits for them, and re-layouts  1.11 us (2%)
  between operations  0.8 us (1%)
  other arithmetic  0.74 us (1%)
    ppermute x3, waiting for transfers between devices, fast(): own.append(lax.ppermute(send, 'aux', [(i, i ^ k) for i in range(count)]))  13.6 us
    ppermute x3, waiting for transfers between devices, cross_over(): return lax.ppermute(half, 'pair', cross)  9 us
    ppermute x3, starting transfers between devices, fast(): own.append(lax.ppermute(send, 'aux', [(i, i ^ k) for i in range(count)]))  5.76 us
    ppermute x1, waiting for transfers between devices, fast(): peak = lax.ppermute(peak, 'pair', cross)  5.72 us
    ppermute x3, starting transfers between devices, cross_over(): return lax.ppermute(half, 'pair', cross)  4.64 us
    ppermute x3, waiting for transfers between devices, fast(): lax.ppermute(share, 'pair', to)  2.81 us
    pallas_call x2, Pallas kernels, near_pairs(): call(kernel, f'near{slot}', out_shape=sum_shapes(orbitals, domain), in_sp...  2.7 us
    pallas_call x3, Pallas kernels, finish(): call(kernel, 'finish', out_shape=[shape(*out), shape(blocks, orbitals, ro...  2.58 us
  transfers between devices with their start and end apart: 16, of which 11 were waited for; matrix products, arithmetic and copies ran while one was open for 1% of the time, Pallas kernels for 9%

profile of v2, /device:TPU:0, one launch (start us, length us, event | category | flops | bytes accessed | tf_op | source)
XLA Modules:
  0.0 61.7 jit_solution(1996579204129342911)
XLA Ops:
  0.6 1.1 %copy-done = bf16[80,8,4,128]{3,2,1,0:T(4,128)(2,1)S(1)} copy-done((bf16[80,8,4,128]{3,2,1,0:T(4,128)(2,1)S(1)}, bf16[80,8,4,128]{3,2,1,0:T(4,128)(2,1)}, u32[]{:S(2)}) %copy-start) | copy-done | bytes 655384
  1.7 0.9 %pack.1 = (bf16[656,128]{1,0:T(8,128)(2,1)S(1)}, bf16[656,128]{1,0:T(8,128)(2,1)S(1)}, bf16[656,128]{1,0:T(8,128)(2,1)S(1)}, bf16[656,128]{1,0:T(8,128)(2,1)S(1)}) custom-call(bf16[2560,128]{1,0:T(8,128)(2,1)S(1)} %bitcast.49), custom_call_target="tpu_custom_call" | custom-call | tf_op jit(solution)/shard_map/pack/pallas_call | solution.py:55
  2.7 5.1 %collective-permute-start.2 = (bf16[656,128]{1,0:T(8,128)(2,1)S(1)}, bf16[656,128]{1,0:T(8,128)(2,1)S(1)}, u32[]{:S(2)}, u32[]{:S(2)}) collective-permute-start(bf16[656,128]{1,0:T(8,128)(2,1)S(1)} %get-tuple-element.38.refs_5_), channel_id=1, source_target_pairs={{0,12},{4,8},{8,4},{12,0},{1,13},{5,9},{9,5},{13,1},{2,14},{6,10},... | collective-permute-start | bytes 503816 | tf_op jit(solution)/shard_map/ppermute | solution.py:314
  8.4 4.5 %collective-permute-done.2.refs_3_ = bf16[656,128]{1,0:T(8,128)(2,1)S(1)} collective-permute-done((bf16[656,128]{1,0:T(8,128)(2,1)S(1)}, bf16[656,128]{1,0:T(8,128)(2,1)S(1)}, u32[]{:S(2)}, u32[]{:S(2)}) %collective-permute-start.2) | collective-permute-done | bytes 167968 | tf_op jit(solution)/shard_map/ppermute | solution.py:314
  12.9 3.8 %collective-permute-done.refs_1_ = bf16[656,128]{1,0:T(8,128)(2,1)S(1)} collective-permute-done((bf16[656,128]{1,0:T(8,128)(2,1)S(1)}, bf16[656,128]{1,0:T(8,128)(2,1)S(1)}, u32[]{:S(2)}, u32[]{:S(2)}) %collective-permute-start) | collective-permute-done | bytes 167968 | tf_op jit(solution)/shard_map/ppermute | solution.py:314
  16.8 5.2 %collective-permute-done.1.refs_2_ = bf16[656,128]{1,0:T(8,128)(2,1)S(1)} collective-permute-done((bf16[656,128]{1,0:T(8,128)(2,1)S(1)}, bf16[656,128]{1,0:T(8,128)(2,1)S(1)}, u32[]{:S(2)}, u32[]{:S(2)}) %collective-permute-start.1) | collective-permute-done | bytes 167968 | tf_op jit(solution)/shard_map/ppermute | solution.py:314
  23.5 2.1 %collective-permute-done.4.second_ref = f32[16,128]{1,0:T(8,128)S(1)} collective-permute-done((f32[16,128]{1,0:T(8,128)S(1)}, f32[16,128]{1,0:T(8,128)S(1)}, u32[]{:S(2)}, u32[]{:S(2)}) %collective-permute-start.4) | collective-permute-done | bytes 8224 | tf_op jit(solution)/shard_map/ppermute | solution.py:328
  26.5 1.6 %collective-permute-start.5 = (f16[2,128,512]{2,1,0:T(8,128)(2,1)S(1)}, f16[2,128,512]{2,1,0:T(8,128)(2,1)S(1)}, u32[]{:S(2)}, u32[]{:S(2)}) collective-permute-start(f16[2,128,512]{2,1,0:T(8,128)(2,1)S(1)} %fusion.14), channel_id=1, source_target_pairs={{0,2},{1,3},{2,0},{3,1},{4,6},{5,7},{6,4},{7,5},{8,10},{9,11},{10,... | collective-permute-start | bytes 786440 | tf_op jit(solution)/shard_map/ppermute | solution.py:325
  28.6 0.8 %energies.1 = (f32[2,128,128]{2,1,0:T(8,128)S(1)}, f32[2,3,4,128]{3,2,1,0:T(4,128)S(1)}) custom-call(s32[2,3]{1,0:T(2,128)S(1)} %copy-done.1, f32[4,8]{1,0:T(4,128)S(1)} %bitcast.51, s32[8,128]{1,0:T(8,128)S(1)} %copy-done.2, f32[8,128]{1,0:T(8,128)S(1)} %bitcast.50), custom_call_target="tpu_custom_call" | custom-call | tf_op jit(solution)/shard_map/energies/pallas_call | solution.py:293
  29.3 5.7 %collective-permute-done.6.first_ref.second_ref = f32[16,128]{1,0:T(8,128)S(1)} collective-permute-done((f32[16,128]{1,0:T(8,128)S(1)}, f32[16,128]{1,0:T(8,128)S(1)}, u32[]{:S(2)}, u32[]{:S(2)}) %collective-permute-start.6) | collective-permute-done | bytes 8224 | tf_op jit(solution)/shard_map/ppermute | solution.py:329
  35.8 0.8 %collective-permute-done.7.refs_6_ = bf16[1920,128]{1,0:T(8,128)(2,1)S(1)} collective-permute-done((bf16[1920,128]{1,0:T(8,128)(2,1)S(1)}, bf16[1920,128]{1,0:T(8,128)(2,1)S(1)}, u32[]{:S(2)}, u32[]{:S(2)}) %collective-permute-start.7) | collective-permute-done | bytes 491552 | tf_op jit(solution)/shard_map/ppermute | solution.py:317
  36.6 1.3 %near1.1 = (f32[2,128,512]{2,1,0:T(8,128)S(1)}, f32[2,128,512]{2,1,0:T(8,128)S(1)}, f32[2,2,128,512]{3,2,1,0:T(8,128)S(1)}) custom-call(s32[2,3]{1,0:T(2,128)S(1)} %copy-done.1, bf16[656,128]{1,0:T(8,128)(2,1)S(1)} %get-tuple-element.41.refs_0_, bf16[656,128]{1,0:T(8,128)(2,1)S(1)} %collective-permute-done.refs_1_, ...), custom_call_target="tpu_custom_call" | custom-call | tf_op jit(solution)/shard_map/near1/pallas_call | solution.py:170
  38.1 1.4 %near2.1 = (f32[2,128,512]{2,1,0:T(8,128)S(1)}, f32[2,128,512]{2,1,0:T(8,128)S(1)}, f32[2,2,128,512]{3,2,1,0:T(8,128)S(1)}) custom-call(s32[2,3]{1,0:T(2,128)S(1)} %copy-done.1, bf16[656,128]{1,0:T(8,128)(2,1)S(1)} %get-tuple-element.41.refs_0_, bf16[656,128]{1,0:T(8,128)(2,1)S(1)} %collective-permute-done.refs_1_, ...), custom_call_target="tpu_custom_call" | custom-call | tf_op jit(solution)/shard_map/near2/pallas_call | solution.py:170
  39.4 1.3 %collective-permute-done.9 = f32[2,2,128,512]{3,2,1,0:T(8,128)S(1)} collective-permute-done((f32[2,2,128,512]{3,2,1,0:T(8,128)S(1)}, f32[2,2,128,512]{3,2,1,0:T(8,128)S(1)}, u32[]{:S(2)}, u32[]{:S(2)}) %collective-permute-start.9) | collective-permute-done | bytes 1048608 | tf_op jit(solution)/shard_map/ppermute | solution.py:321
  41.0 1.5 %collective-permute-start.12 = (f16[2,128,512]{2,1,0:T(8,128)(2,1)S(1)}, f16[2,128,512]{2,1,0:T(8,128)(2,1)S(1)}, u32[]{:S(2)}, u32[]{:S(2)}) collective-permute-start(f16[2,128,512]{2,1,0:T(8,128)(2,1)S(1)} %fusion.11), channel_id=1, source_target_pairs={{0,2},{1,3},{2,0},{3,1},{4,6},{5,7},{6,4},{7,5},{8,10},{9,11},{10,... | collective-permute-start | bytes 786440 | tf_op jit(solution)/shard_map/ppermute | solution.py:325
  42.7 0.9 %finish.3 = (f32[2,3,128,512]{3,2,1,0:T(8,128)}, f32[2,4,128]{2,1,0:T(4,128)S(1)}) custom-call(f32[2,128,512]{2,1,0:T(8,128)S(1)} %fusion.1.total_ref, f32[2,128,128]{2,1,0:T(8,128)S(1)} %get-tuple-element.48.row_ref, f32[2,3,4,128]{3,2,1,0:T(4,128)S(1)} %get-tuple-element.59.col_ref), custom_call_target="tpu_custom_call" | custom-call | tf_op jit(solution)/shard_map/finish/pallas_call | solution.py:218
  43.7 1.5 %collective-permute-start.11 = (f16[2,128,512]{2,1,0:T(8,128)(2,1)S(1)}, f16[2,128,512]{2,1,0:T(8,128)(2,1)S(1)}, u32[]{:S(2)}, u32[]{:S(2)}) collective-permute-start(f16[2,128,512]{2,1,0:T(8,128)(2,1)S(1)} %fusion.6), channel_id=1, source_target_pairs={{0,2},{1,3},{2,0},{3,1},{4,6},{5,7},{6,4},{7,5},{8,10},{9,11},{10,... | collective-permute-start | bytes 786440 | tf_op jit(solution)/shard_map/ppermute | solution.py:325
  45.2 4.9 %collective-permute-done.12 = f16[2,128,512]{2,1,0:T(8,128)(2,1)S(1)} collective-permute-done((f16[2,128,512]{2,1,0:T(8,128)(2,1)S(1)}, f16[2,128,512]{2,1,0:T(8,128)(2,1)S(1)}, u32[]{:S(2)}, u32[]{:S(2)}) %collective-permute-start.12) | collective-permute-done | bytes 262176 | tf_op jit(solution)/shard_map/ppermute | solution.py:325
  50.3 0.9 %finish.4 = (f32[2,3,128,512]{3,2,1,0:T(8,128)}, f32[2,4,128]{2,1,0:T(4,128)S(1)}) custom-call(f32[2,128,512]{2,1,0:T(8,128)S(1)} %fusion.3.total_ref, f32[2,128,128]{2,1,0:T(8,128)S(1)} %get-tuple-element.48.row_ref, f32[2,3,4,128]{3,2,1,0:T(4,128)S(1)} %get-tuple-element.59.col_ref, ...), custom_call_target="tpu_custom_call", output_to_operand_aliasing={{0}: (3, {})} | custom-call | tf_op jit(solution)/shard_map/finish/pallas_call | solution.py:218
  51.2 4.1 %collective-permute-done.11 = f16[2,128,512]{2,1,0:T(8,128)(2,1)S(1)} collective-permute-done((f16[2,128,512]{2,1,0:T(8,128)(2,1)S(1)}, f16[2,128,512]{2,1,0:T(8,128)(2,1)S(1)}, u32[]{:S(2)}, u32[]{:S(2)}) %collective-permute-start.11) | collective-permute-done | bytes 262176 | tf_op jit(solution)/shard_map/ppermute | solution.py:325
  55.4 0.9 %finish.5 = (f32[2,3,128,512]{3,2,1,0:T(8,128)}, f32[2,4,128]{2,1,0:T(4,128)S(1)}) custom-call(f32[2,128,512]{2,1,0:T(8,128)S(1)} %fusion.8.total_ref, f32[2,128,128]{2,1,0:T(8,128)S(1)} %get-tuple-element.48.row_ref, f32[2,3,4,128]{3,2,1,0:T(4,128)S(1)} %get-tuple-element.59.col_ref, ...), custom_call_target="tpu_custom_call", output_to_operand_aliasing={{0}: (3, {})} | custom-call | tf_op jit(solution)/shard_map/finish/pallas_call | solution.py:218
  56.4 1.6 %collective-permute-start.14 = (f32[2,3,4,4]{3,2,1,0:T(4,128)S(1)}, f32[2,3,4,4]{3,2,1,0:T(4,128)S(1)}, u32[]{:S(2)}, u32[]{:S(2)}) collective-permute-start(f32[2,3,4,4]{3,2,1,0:T(4,128)S(1)} %share.1.refs_0_), channel_id=1, source_target_pairs={{0,2},{1,3},{2,0},{3,1},{4,6},{5,7},{6,4},{7,5},{8,10},{9,11},{10,... | collective-permute-start | bytes 1160 | tf_op jit(solution)/shard_map/ppermute | solution.py:348
  58.3 1.9 %collective-permute-done.14.refs_2_ = f32[2,3,4,4]{3,2,1,0:T(4,128)S(1)} collective-permute-done((f32[2,3,4,4]{3,2,1,0:T(4,128)S(1)}, f32[2,3,4,4]{3,2,1,0:T(4,128)S(1)}, u32[]{:S(2)}, u32[]{:S(2)}) %collective-permute-start.14) | collective-permute-done | bytes 416 | tf_op jit(solution)/shard_map/ppermute | solution.py:348
  60.2 0.9 %collective-permute-done.15.refs_3_ = f32[2,3,4,4]{3,2,1,0:T(4,128)S(1)} collective-permute-done((f32[2,3,4,4]{3,2,1,0:T(4,128)S(1)}, f32[2,3,4,4]{3,2,1,0:T(4,128)S(1)}, u32[]{:S(2)}, u32[]{:S(2)}) %collective-permute-start.15) | collective-permute-done | bytes 416 | tf_op jit(solution)/shard_map/ppermute | solution.py:348
  (41 shorter events, 6.3 us)
Async XLA Ops:
  0.6 1.1 %copy-start = (bf16[80,8,4,128]{3,2,1,0:T(4,128)(2,1)S(1)}, bf16[80,8,4,128]{3,2,1,0:T(4,128)(2,1)}, u32[]{:S(2)}) copy-start(bf16[80,8,4,128]{3,2,1,0:T(4,128)(2,1)} %param.5) | copy-start | bytes 1966084
  1.7 26.9 %copy-start.1 = (s32[2,3]{1,0:T(2,128)S(1)}, s32[2,3]{1,0:T(2,128)}, u32[]{:S(2)}) copy-start(s32[2,3]{1,0:T(2,128)} %partners_ref.5) | copy-start | bytes 76
  1.7 26.9 %copy-start.2 = (s32[8,128]{1,0:T(8,128)S(1)}, s32[8,128]{1,0:T(8,128)}, u32[]{:S(2)}) copy-start(s32[8,128]{1,0:T(8,128)} %domains_ref.1) | copy-start | bytes 12292
  1.7 26.9 %copy-start.3 = (f32[1024]{0:T(1024)S(1)}, f32[1024]{0:T(1024)}, u32[]{:S(2)}) copy-start(f32[1024]{0:T(1024)} %param.9) | copy-start | bytes 12292
  1.7 26.9 %copy-start.4 = (f32[8,4]{0,1:T(4,128)S(1)}, f32[8,4]{0,1:T(4,128)}, u32[]{:S(2)}) copy-start(f32[8,4]{0,1:T(4,128)} %param.8) | copy-start | bytes 388
  2.7 10.3 %collective-permute-start.2 = (bf16[656,128]{1,0:T(8,128)(2,1)S(1)}, bf16[656,128]{1,0:T(8,128)(2,1)S(1)}, u32[]{:S(2)}, u32[]{:S(2)}) collective-permute-start(bf16[656,128]{1,0:T(8,128)(2,1)S(1)} %get-tuple-element.38.refs_5_), channel_id=1, source_target_pairs={{0,12},{4,8},{8,4},{12,0},{1,13},{5,9},{9,5},{13,1},{2,14},{6,10},... | collective-permute-start | bytes 503816 | tf_op jit(solution)/shard_map/ppermute | solution.py:314
  7.8 9.0 %collective-permute-start = (bf16[656,128]{1,0:T(8,128)(2,1)S(1)}, bf16[656,128]{1,0:T(8,128)(2,1)S(1)}, u32[]{:S(2)}, u32[]{:S(2)}) collective-permute-start(bf16[656,128]{1,0:T(8,128)(2,1)S(1)} %get-tuple-element.51.refs_4_), channel_id=1, source_target_pairs={{0,4},{4,0},{8,12},{12,8},{1,5},{5,1},{9,13},{13,9},{2,6},{6,2},{1... | collective-permute-start | bytes 503816 | tf_op jit(solution)/shard_map/ppermute | solution.py:314
  7.8 14.2 %collective-permute-start.1 = (bf16[656,128]{1,0:T(8,128)(2,1)S(1)}, bf16[656,128]{1,0:T(8,128)(2,1)S(1)}, u32[]{:S(2)}, u32[]{:S(2)}) collective-permute-start(bf16[656,128]{1,0:T(8,128)(2,1)S(1)} %get-tuple-element.37), channel_id=1, source_target_pairs={{0,8},{4,12},{8,0},{12,4},{1,9},{5,13},{9,1},{13,5},{2,10},{6,14},... | collective-permute-start | bytes 503816 | tf_op jit(solution)/shard_map/ppermute | solution.py:314
  22.9 3.5 %collective-permute-start.3 = (f32[2,2,128,512]{3,2,1,0:T(8,128)S(1)}, f32[2,2,128,512]{3,2,1,0:T(8,128)S(1)}, u32[]{:S(2)}, u32[]{:S(2)}) collective-permute-start(f32[2,2,128,512]{3,2,1,0:T(8,128)S(1)} %get-tuple-element.43), channel_id=1, source_target_pairs={{0,1},{1,0},{2,3},{3,2},{4,5},{5,4},{6,7},{7,6},{8,9},{9,8},{10,11... | collective-permute-start | bytes 3145736 | tf_op jit(solution)/shard_map/ppermute | solution.py:321
  22.9 2.7 %collective-permute-start.4 = (f32[16,128]{1,0:T(8,128)S(1)}, f32[16,128]{1,0:T(8,128)S(1)}, u32[]{:S(2)}, u32[]{:S(2)}) collective-permute-start(f32[16,128]{1,0:T(8,128)S(1)} %get-tuple-element.44.first_ref), channel_id=1, source_target_pairs={{0,1},{1,0},{2,3},{3,2},{4,5},{5,4},{6,7},{7,6},{8,9},{9,8},{10,11... | collective-permute-start | bytes 24584 | tf_op jit(solution)/shard_map/ppermute | solution.py:328
  23.4 13.2 %collective-permute-start.7 = (bf16[1920,128]{1,0:T(8,128)(2,1)S(1)}, bf16[1920,128]{1,0:T(8,128)(2,1)S(1)}, u32[]{:S(2)}, u32[]{:S(2)}) collective-permute-start(bf16[1920,128]{1,0:T(8,128)(2,1)S(1)} %get-tuple-element.39), channel_id=1, source_target_pairs={{0,4},{1,5},{2,6},{3,7},{4,0},{5,1},{6,2},{7,3},{8,12},{9,13},{10,... | collective-permute-start | bytes 1474568 | tf_op jit(solution)/shard_map/ppermute | solution.py:317
  23.4 13.2 %collective-permute-start.8 = (bf16[1920,128]{1,0:T(8,128)(2,1)S(1)}, bf16[1920,128]{1,0:T(8,128)(2,1)S(1)}, u32[]{:S(2)}, u32[]{:S(2)}) collective-permute-start(bf16[1920,128]{1,0:T(8,128)(2,1)S(1)} %get-tuple-element.40), channel_id=1, source_target_pairs={{0,1},{1,0},{2,3},{3,2},{4,8},{5,9},{6,10},{7,11},{8,4},{9,5},{10,... | collective-permute-start | bytes 1474568 | tf_op jit(solution)/shard_map/ppermute | solution.py:317
  26.5 9.3 %collective-permute-start.5 = (f16[2,128,512]{2,1,0:T(8,128)(2,1)S(1)}, f16[2,128,512]{2,1,0:T(8,128)(2,1)S(1)}, u32[]{:S(2)}, u32[]{:S(2)}) collective-permute-start(f16[2,128,512]{2,1,0:T(8,128)(2,1)S(1)} %fusion.14), channel_id=1, source_target_pairs={{0,2},{1,3},{2,0},{3,1},{4,6},{5,7},{6,4},{7,5},{8,10},{9,11},{10,... | collective-permute-start | bytes 786440 | tf_op jit(solution)/shard_map/ppermute | solution.py:325
  28.1 7.0 %collective-permute-start.6 = (f32[16,128]{1,0:T(8,128)S(1)}, f32[16,128]{1,0:T(8,128)S(1)}, u32[]{:S(2)}, u32[]{:S(2)}) collective-permute-start(f32[16,128]{1,0:T(8,128)S(1)} %get-tuple-element.46), channel_id=1, source_target_pairs={{0,2},{1,3},{2,0},{3,1},{4,6},{5,7},{6,4},{7,5},{8,10},{9,11},{10,... | collective-permute-start | bytes 24584 | tf_op jit(solution)/shard_map/ppermute | solution.py:329
  38.0 2.7 %collective-permute-start.9 = (f32[2,2,128,512]{3,2,1,0:T(8,128)S(1)}, f32[2,2,128,512]{3,2,1,0:T(8,128)S(1)}, u32[]{:S(2)}, u32[]{:S(2)}) collective-permute-start(f32[2,2,128,512]{3,2,1,0:T(8,128)S(1)} %get-tuple-element.55), channel_id=1, source_target_pairs={{0,1},{1,0},{2,3},{3,2},{4,5},{5,4},{6,7},{7,6},{8,9},{9,8},{10,11... | collective-permute-start | bytes 3145736 | tf_op jit(solution)/shard_map/ppermute | solution.py:321
  40.8 2.7 %collective-permute-start.10 = (f32[2,2,128,512]{3,2,1,0:T(8,128)S(1)}, f32[2,2,128,512]{3,2,1,0:T(8,128)S(1)}, u32[]{:S(2)}, u32[]{:S(2)}) collective-permute-start(f32[2,2,128,512]{3,2,1,0:T(8,128)S(1)} %get-tuple-element.56), channel_id=1, source_target_pairs={{0,1},{1,0},{2,3},{3,2},{4,5},{5,4},{6,7},{7,6},{8,9},{9,8},{10,11... | collective-permute-start | bytes 3145736 | tf_op jit(solution)/shard_map/ppermute | solution.py:321
  41.0 9.1 %collective-permute-start.12 = (f16[2,128,512]{2,1,0:T(8,128)(2,1)S(1)}, f16[2,128,512]{2,1,0:T(8,128)(2,1)S(1)}, u32[]{:S(2)}, u32[]{:S(2)}) collective-permute-start(f16[2,128,512]{2,1,0:T(8,128)(2,1)S(1)} %fusion.11), channel_id=1, source_target_pairs={{0,2},{1,3},{2,0},{3,1},{4,6},{5,7},{6,4},{7,5},{8,10},{9,11},{10,... | collective-permute-start | bytes 786440 | tf_op jit(solution)/shard_map/ppermute | solution.py:325
  43.7 11.6 %collective-permute-start.11 = (f16[2,128,512]{2,1,0:T(8,128)(2,1)S(1)}, f16[2,128,512]{2,1,0:T(8,128)(2,1)S(1)}, u32[]{:S(2)}, u32[]{:S(2)}) collective-permute-start(f16[2,128,512]{2,1,0:T(8,128)(2,1)S(1)} %fusion.6), channel_id=1, source_target_pairs={{0,2},{1,3},{2,0},{3,1},{4,6},{5,7},{6,4},{7,5},{8,10},{9,11},{10,... | collective-permute-start | bytes 786440 | tf_op jit(solution)/shard_map/ppermute | solution.py:325
  56.3 1.9 %collective-permute-start.13 = (f32[2,3,4,4]{3,2,1,0:T(4,128)S(1)}, f32[2,3,4,4]{3,2,1,0:T(4,128)S(1)}, u32[]{:S(2)}, u32[]{:S(2)}) collective-permute-start(f32[2,3,4,4]{3,2,1,0:T(4,128)S(1)} %share.1.refs_0_), channel_id=1, source_target_pairs={{0,1},{1,0},{2,3},{3,2},{4,5},{5,4},{6,7},{7,6},{8,9},{9,8},{10,11... | collective-permute-start | bytes 1160 | tf_op jit(solution)/shard_map/ppermute | solution.py:348
  56.4 3.8 %collective-permute-start.14 = (f32[2,3,4,4]{3,2,1,0:T(4,128)S(1)}, f32[2,3,4,4]{3,2,1,0:T(4,128)S(1)}, u32[]{:S(2)}, u32[]{:S(2)}) collective-permute-start(f32[2,3,4,4]{3,2,1,0:T(4,128)S(1)} %share.1.refs_0_), channel_id=1, source_target_pairs={{0,2},{1,3},{2,0},{3,1},{4,6},{5,7},{6,4},{7,5},{8,10},{9,11},{10,... | collective-permute-start | bytes 1160 | tf_op jit(solution)/shard_map/ppermute | solution.py:348
  58.0 3.1 %collective-permute-start.15 = (f32[2,3,4,4]{3,2,1,0:T(4,128)S(1)}, f32[2,3,4,4]{3,2,1,0:T(4,128)S(1)}, u32[]{:S(2)}, u32[]{:S(2)}) collective-permute-start(f32[2,3,4,4]{3,2,1,0:T(4,128)S(1)} %share.1.refs_0_), channel_id=1, source_target_pairs={{0,3},{1,2},{2,1},{3,0},{4,7},{5,6},{6,5},{7,4},{8,11},{9,10},{10,... | collective-permute-start | bytes 1160 | tf_op jit(solution)/shard_map/ppermute | solution.py:348

commit v3 on v2

--- a/solution.py
+++ b/solution.py
@@ -11,6 +11,7 @@
 ANY = pl.BlockSpec(memory_space=pl.ANY)
 PARAMS = pltpu.CompilerParams(vmem_limit_bytes=8 * 2**20)
 PEAK_ROWS = 16
+GROUPS = ([[(0, 1)]], [[(1, 1), (0, 2), (1, 2)]])
 
 def shape(*dims, dtype=F32):
     return jax.ShapeDtypeStruct(dims, dtype)
@@ -96,29 +97,28 @@
     return jnp.concatenate(columns, axis=1)
 
 
-def store_sums(sums, r, mine, other, give):
+def store_sums(sums, at, mine, other, give):
     domain = sums.shape[0] // 4
-    mine[r] = sums[:domain]
-    other[r] = sums[domain : 2 * domain]
-    give[0, r] = sums[2 * domain : 3 * domain]
-    give[1, r] = sums[3 * domain :]
-
-
-def sum_shapes(orbitals, domain):
-    wide = orbitals * domain
-    return [shape(2, domain, wide), shape(2, domain, wide), shape(2, 2, domain, wide)]
+    mine[at] = sums[:domain]
+    other[at] = sums[domain : 2 * domain]
+    give[0, at] = sums[2 * domain : 3 * domain]
+    give[1, at] = sums[3 * domain :]
 
 
 def own_pairs(own, orbitals):
     count, domain = len(own), own[0].shape[1]
     depth = depth_of(own[0], orbitals)
+    wide = orbitals * domain
 
     def kernel(*refs):
         own_refs, (mine, other, give, peak) = refs[:count], refs[count:]
         top = own_refs[0][-PEAK_ROWS:, :].astype(F32)
         for ref in own_refs[1:]:
             top = jnp.maximum(top, ref[-PEAK_ROWS:, :].astype(F32))
-        peak[...] = top
+        top = jnp.maximum(top[:8], top[8:])
+        peak[...] = jnp.concatenate([top] * orbitals, axis=1)
+        for n in range(2):
+            give[n, 2 * domain :] = peak[...]
         for r in range(2):
             right = jnp.concatenate(
                 [
@@ -127,28 +127,34 @@
                 ],
                 axis=1,
             )
-            store_sums(product(left_rows(own_refs, depth, r), right), r, mine, other, give)
+            at = slice(r * domain, (r + 1) * domain)
+            store_sums(product(left_rows(own_refs, depth, r), right), at, mine, other, give)
 
     return call(
         kernel,
         "own",
-        out_shape=sum_shapes(orbitals, domain) + [shape(PEAK_ROWS, domain)],
+        out_shape=[
+            shape(2 * domain, wide),
+            shape(2 * domain, wide),
+            shape(2, 2 * domain + 8, wide),
+            shape(8, wide),
+        ],
         in_specs=[VMEM] * count,
         out_specs=[VMEM] * 4,
     )(*own)
 
 
-def near_pairs(partners, own, here, sides, orbitals, slot):
+def near_pairs(partners, own, here, sides, orbitals, groups):
     count, domain = len(own), own[0].shape[1]
     depth = depth_of(own[0], orbitals)
-    rows = 2 * orbitals * depth
+    rows, wide = 2 * orbitals * depth, orbitals * domain
 
     def kernel(partners_ref, *refs):
         own_refs, here_refs, side_refs = refs[:count], refs[count : count + 2], refs[count + 2 :][:2]
         z = lax.axis_index("aux")
         even = lax.rem(z, 2) == 0
 
-        def panels(w, j):
+        def panels(w, j, slot):
             from_first = (w > 3) == even
             at = (2 * j + lax.rem(w, 2)) * depth
             found = []
@@ -162,94 +168,143 @@
                 found.append(panel)
             return jnp.concatenate(found, axis=0)
 
-        for r in range(2):
-            w = partners_ref[r, slot] - 2 * z + 2
-            right = jnp.concatenate([panels(w, j) for j in range(orbitals)], axis=1)
-            store_sums(product(left_rows(own_refs, depth, r), right), r, *refs[count + 4 :])
-
-    return call(
-        kernel,
-        f"near{slot}",
-        out_shape=sum_shapes(orbitals, domain),
+        for n, tiles in enumerate(groups):
+            for t, (r, slot) in enumerate(tiles):
+                w = partners_ref[r, slot] - 2 * z + 2
+                right = jnp.concatenate([panels(w, j, slot) for j in range(orbitals)], axis=1)
+                sums = product(left_rows(own_refs, depth, r), right)
+                at = slice(t * domain, (t + 1) * domain)
+                store_sums(sums, at, *refs[count + 4 + 3 * n :][:3])
+
+    outs = []
+    for tiles in groups:
+        height = len(tiles) * domain
+        outs += [shape(height, wide), shape(height, wide), shape(2, height, wide)]
+    return call(
+        kernel,
+        "near",
+        out_shape=outs,
         in_specs=[SMEM] + [VMEM] * (count + 4),
-        out_specs=[VMEM] * 3,
+        out_specs=[VMEM] * len(outs),
     )(partners, *own, *here, *sides)
 
 
-def scales(first, second, depth, wide):
-    def kernel(first_ref, second_ref, top_ref, down_ref, up_ref):
-        top = jnp.maximum(first_ref[...], second_ref[...])
+def scale_down(peak, got, depth):
+    def kernel(peak_ref, got_ref, top_ref, down_ref):
+        top = jnp.maximum(peak_ref[...], got_ref[0, -8:])
         top_ref[...] = top
-        top = jnp.maximum(jnp.max(top, axis=(0, 1), keepdims=True), 1e-17)
-        exponent = jnp.ceil(jnp.log2(top * top * depth)) - 15
-        exponent = jnp.broadcast_to(exponent, down_ref.shape)
-        down_ref[...] = jnp.exp2(-exponent)
-        up_ref[...] = jnp.exp2(exponent)
-
-    return call(
-        kernel,
-        "scales",
-        out_shape=[shape(*first.shape), shape(8, wide), shape(8, wide)],
+        top = jnp.maximum(jnp.max(top[:, :128], axis=(0, 1), keepdims=True), 1e-17)
+        down_ref[...] = jnp.broadcast_to(32768.0 / (top * top * depth), down_ref.shape)
+
+    return call(
+        kernel,
+        "scale_down",
+        out_shape=[shape(*peak.shape)] * 2,
         in_specs=[VMEM] * 2,
-        out_specs=[VMEM] * 3,
-    )(first, second)
-
-
-def finish(totals, row_vals, col_vals, slot, before, out):
-    blocks, rows, width = totals.shape
-    orbitals = width // rows
+        out_specs=[VMEM] * 2,
+    )(peak, got)
+
+
+def scale_up(top, depth):
+    def kernel(top_ref, up_ref):
+        top = jnp.maximum(jnp.max(top_ref[:, :128], axis=(0, 1), keepdims=True), 1e-17)
+        up_ref[...] = jnp.broadcast_to((top * top * depth) * (1.0 / 32768.0), up_ref.shape)
+
+    return call(
+        kernel, "scale_up", out_shape=shape(*top.shape), in_specs=[VMEM], out_specs=VMEM
+    )(top)
+
+
+def amplitude_tiles(total_ref, row_ref, col_ref, amp, energy_ref, tiles, done):
+    rows, wide = amp.shape[1:]
+    for t, (r, slot) in enumerate(tiles):
+        row = row_ref[r]
+        for j in range(wide // rows):
+            at = slice(j * rows, (j + 1) * rows)
+            total = total_ref[t * rows : (t + 1) * rows, at]
+            tile = total / (row + col_ref[r, slot, j : j + 1, :])
+            amp[t, :, at] = tile
+            energy_ref[t, j : j + 1, :] = jnp.sum(total * tile, axis=0, keepdims=True)
+        done(t)
+
+
+def finish(totals, row_vals, col_vals, tiles, before, out):
+    rows, wide = out[2:]
+    count = len(tiles)
 
     def kernel(total_ref, row_ref, col_ref, *refs):
         amp_ref, energy_ref, amp, sems = refs[-4:]
         copies = []
-        for r in range(blocks):
-            row = row_ref[r]
-            for j in range(orbitals):
-                at = slice(j * rows, (j + 1) * rows)
-                total = total_ref[r, :, at]
-                tile = total / (row + col_ref[r, slot, j : j + 1, :])
-                amp[r, :, at] = tile
-                energy_ref[r, j : j + 1, :] = jnp.sum(total * tile, axis=0, keepdims=True)
-            copies.append(pltpu.make_async_copy(amp.at[r], amp_ref.at[r, slot], sems.at[r]))
+
+        def done(t):
+            r, slot = tiles[t]
+            copies.append(pltpu.make_async_copy(amp.at[t], amp_ref.at[r, slot], sems.at[t]))
+            copies[-1].start()
+
+        amplitude_tiles(total_ref, row_ref, col_ref, amp, energy_ref, tiles, done)
+        for started in copies:
+            started.wait()
+
+    return call(
+        kernel,
+        "finish",
+        out_shape=[shape(*out), shape(count, wide // rows, rows)],
+        in_specs=[VMEM] * 3 + [ANY] * len(before),
+        out_specs=[ANY, VMEM],
+        input_output_aliases={3: 0} if before else {},
+        scratch_shapes=[pltpu.VMEM((count, rows, wide), F32), pltpu.SemaphoreType.DMA((count,))],
+    )(totals, row_vals, col_vals, *before)
+
+
+def finish_last(totals, row_vals, col_vals, tiles, before, shares):
+    orbitals, domain = col_vals.shape[2:]
+    wide = orbitals * domain
+    blocks, slots = col_vals.shape[:2]
+    count = len(tiles)
+    known = len(shares)
+
+    def kernel(total_ref, row_ref, col_ref, *refs):
+        share_refs, (amp_ref, out, energy) = refs[:known], refs[known:]
+        amplitude_tiles(total_ref, row_ref, col_ref, amp_ref, energy, tiles, lambda t: None)
+        p = lax.axis_index("pair")
+        row = lax.broadcasted_iota(jnp.int32, (orbitals, orbitals), 0)
+        column = lax.broadcasted_iota(jnp.int32, (orbitals, orbitals), 1)
+        for ref, places in zip((*share_refs, energy), (*before, tiles)):
+            for t, (r, slot) in enumerate(places):
+                sums = jnp.sum(ref[t], axis=1, keepdims=True) * (1.0 / (domain * domain))
+                value = jnp.zeros((orbitals, orbitals), F32)
+                for j in range(orbitals):
+                    value = jnp.where((row == p) & (column == j), sums[j : j + 1, :], value)
+                out[r, slot] = value
+
+    return call(
+        kernel,
+        "finish_last",
+        out_shape=[shape(count, domain, wide), shape(blocks, slots, orbitals, orbitals)],
+        in_specs=[VMEM] * (3 + known),
+        out_specs=[VMEM] * 2,
+        scratch_shapes=[pltpu.VMEM((count, orbitals, domain), F32)],
+    )(totals, row_vals, col_vals, *shares)
+
+
+def put(tiles_at, values, amps):
+    def kernel(values_ref, _, amp_ref, sems):
+        copies = []
+        for t, (r, slot) in enumerate(tiles_at):
+            copies.append(pltpu.make_async_copy(values_ref.at[t], amp_ref.at[r, slot], sems.at[t]))
             copies[-1].start()
         for started in copies:
             started.wait()
 
     return call(
         kernel,
-        "finish",
-        out_shape=[shape(*out), shape(blocks, orbitals, rows)],
-        in_specs=[VMEM] * 3 + [ANY] * len(before),
-        out_specs=[ANY, VMEM],
-        input_output_aliases={3: 0} if before else {},
-        scratch_shapes=[pltpu.VMEM(totals.shape, F32), pltpu.SemaphoreType.DMA((blocks,))],
-    )(totals, row_vals, col_vals, *before)
-
-
-def share_out(shares):
-    blocks, orbitals, domain = shares[0].shape
-    slots = len(shares)
-
-    def kernel(*refs):
-        out = refs[-1]
-        p = lax.axis_index("pair")
-        row = lax.broadcasted_iota(jnp.int32, (orbitals, orbitals), 0)
-        column = lax.broadcasted_iota(jnp.int32, (orbitals, orbitals), 1)
-        for r in range(blocks):
-            for s in range(slots):
-                total = jnp.zeros((orbitals, orbitals), F32)
-                sums = jnp.sum(refs[s][r], axis=1, keepdims=True) * (1.0 / (domain * domain))
-                for j in range(orbitals):
-                    total = jnp.where((row == p) & (column == j), sums[j : j + 1, :], total)
-                out[r, s] = total
-
-    return call(
-        kernel,
-        "share",
-        out_shape=shape(blocks, slots, orbitals, orbitals),
-        in_specs=[VMEM] * slots,
-        out_specs=VMEM,
-    )(*shares)
+        "put",
+        out_shape=shape(*amps.shape),
+        in_specs=[VMEM, ANY],
+        out_specs=ANY,
+        input_output_aliases={1: 0},
+        scratch_shapes=[pltpu.SemaphoreType.DMA((len(tiles_at),))],
+    )(values, amps)
 
 
 def last(shares):
@@ -317,35 +372,44 @@
     near = [lax.ppermute(m, ("aux", "pair"), side) for m, side in zip(messages, sides)]
     own[0] = after(own[0], *messages)
 
-    def reduce(mine, other, give):
+    def across_cores(mine, other, give):
         got = lax.ppermute(give, "pair", swap)
-        return mine, got[0], ((other + got[1]) * to_half[:1]).astype(F16)
-
-    def cross_over(half):
-        return lax.ppermute(half, "pair", cross)
+        height = mine.shape[0]
+        return mine, got, other + got[1, :height]
+
+    def across_chips(other):
+        return lax.ppermute((other * to_half[:1]).astype(F16), "pair", cross)
 
     *sums, peak = own_pairs(own, orbitals)
-    peak, to_half, _ = scales(peak, lax.ppermute(peak, "pair", swap), 2 * count * depth, wide)
-    peak = lax.ppermute(peak, "pair", cross)
-    _, _, from_half = scales(peak, peak, 2 * count * depth, wide)
-
-    parts = [reduce(*sums)]
-    across = [cross_over(parts[0][2])]
-    here[0] = after(here[0], across[0], from_half, row_vals)
-    parts.append(reduce(*near_pairs(partners, own, here, near, orbitals, 1)))
-    across.append(cross_over(parts[1][2]))
-    here[0] = after(here[0], parts[1][0])
-    mine, other, give = near_pairs(partners, own, here, near, orbitals, 2)
-    parts.append(reduce(mine, other, after(give, parts[1][2])))
-    across.append(cross_over(parts[2][2]))
+    mine, got, other = across_cores(*sums)
+    top, to_half = scale_down(peak, got, 2 * count * depth)
+    parts = [(mine, got, across_chips(other))]
+    from_half = scale_up(lax.ppermute(top, "pair", cross), 2 * count * depth)
+    here[0] = after(here[0], parts[0][2], from_half, row_vals)
+
+    groups = [[(0, 0), (1, 0)], *GROUPS[0], *GROUPS[1]]
+    sums = near_pairs(partners, own, here, near, orbitals, GROUPS[0])
+    here[0] = after(here[0], sums[0])
+    sums += near_pairs(partners, own, here, near, orbitals, GROUPS[1])
+    for n in range(0, len(sums), 3):
+        mine, other, give = sums[n : n + 3]
+        if n:
+            give = after(give, half)
+        mine, got, other = across_cores(mine, other, give)
+        half = (other * to_half[:1]).astype(F16)
+        parts.append((mine, got, lax.ppermute(half, "pair", cross)))
+
+    out = partners.shape + (domain, wide)
     amps, shares = [], []
-    for slot, (mine, got, _) in enumerate(parts):
-        back = after(from_half, shares[-1]) if slot else from_half
-        total = mine + got + across[slot].astype(F32) * back[:1]
-        *amps, share = finish(total, row_vals, col_vals, slot, amps, partners.shape + (domain, wide))
-        shares.append(share)
-    share = share_out(shares)
-    return amps[0], last([share] + [lax.ppermute(share, "pair", to) for to in (swap, cross, both)])
+    for at, (mine, got, across) in enumerate(parts):
+        back = after(from_half, shares[-1]) if at else from_half
+        total = mine + got[0, : mine.shape[0]] + across.astype(F32) * back[:1]
+        if at < len(parts) - 1:
+            *amps, share = finish(total, row_vals, col_vals, groups[at], amps, out)
+            shares.append(share)
+    values, share = finish_last(total, row_vals, col_vals, groups[-1], groups[:-1], shares)
+    others = [lax.ppermute(share, "pair", to) for to in (swap, cross, both)]
+    return put(groups[-1], values, amps[0]), last([share, *others])
 
 
 def padded(shard, sides, width):

time: 61.8 us -> 59 us (0.955)
  waiting for transfers between devices: 35.3 us -> 30.7 us
  starting transfers between devices: 13.8 us -> 16.5 us
  Pallas kernels: 9.99 us -> 8.84 us
    ppermute x11 -> x10, waiting for transfers between devices: 20.9 us -> 17.4 us  [the longest x2 7.88 us: fast(): parts.append((mine, got, lax.ppermute(half, 'pair', cross)))]
    ppermute x2, starting transfers between devices: 0.08 us -> 3.34 us  [fast(): lax.ppermute(m, ('aux', 'pair'), side)]
    ppermute x3, waiting for transfers between devices: 13.6 us -> 11.1 us  [fast(): own.append(lax.ppermute(send, 'aux', [(i, i ^ k) for i in range(count)]))]
    ppermute x2, waiting for transfers between devices: 0.84 us -> 2.26 us  [fast(): lax.ppermute(m, ('aux', 'pair'), side)]
    pallas_call x9, Pallas kernels: 7.6 us -> 6.46 us  [the longest x2 2.66 us: near_pairs(): call(kernel, 'near', out_shape=outs, in_specs=[SMEM] + [VMEM] * (count +...]
    ppermute x11 -> x10, starting transfers between devices: 7.91 us -> 7.47 us  [the longest x2 3.04 us: fast(): parts.append((mine, got, lax.ppermute(half, 'pair', cross)))]
  transfers between devices with their start and end apart: 16 -> 15, of which waited for: 11 -> 9; matrix products, arithmetic and copies ran while one was open for 1% -> 1% of each run, Pallas kernels for 9% -> 9%
where the time goes in v3:
time: 59 us; the launch traced here: 58.8 us
  waiting for transfers between devices  30.7 us (52%)
  starting transfers between devices  16.5 us (28%)
  Pallas kernels  8.84 us (15%)
  local copies, waits for them, and re-layouts  1.13 us (2%)
  between operations  0.85 us (1%)
  other arithmetic  0.76 us (1%)
    ppermute x3, waiting for transfers between devices, fast(): own.append(lax.ppermute(send, 'aux', [(i, i ^ k) for i in range(count)]))  11.1 us
    ppermute x2, waiting for transfers between devices, fast(): parts.append((mine, got, lax.ppermute(half, 'pair', cross)))  7.88 us
    ppermute x1, waiting for transfers between devices, fast(): from_half = scale_up(lax.ppermute(top, 'pair', cross), 2 * count * depth)  6.1 us
    ppermute x3, starting transfers between devices, fast(): own.append(lax.ppermute(send, 'aux', [(i, i ^ k) for i in range(count)]))  5.68 us
    ppermute x2, starting transfers between devices, fast(): lax.ppermute(m, ('aux', 'pair'), side)  3.34 us
    ppermute x2, starting transfers between devices, fast(): parts.append((mine, got, lax.ppermute(half, 'pair', cross)))  3.04 us
    pallas_call x2, Pallas kernels, near_pairs(): call(kernel, 'near', out_shape=outs, in_specs=[SMEM] + [VMEM] * (count +...  2.66 us
    ppermute x2, waiting for transfers between devices, fast(): lax.ppermute(m, ('aux', 'pair'), side)  2.26 us
  transfers between devices with their start and end apart: 15, of which 9 were waited for; matrix products, arithmetic and copies ran while one was open for 1% of the time, Pallas kernels for 9%

profile of v3, /device:TPU:0, one launch (start us, length us, event | category | flops | bytes accessed | tf_op | source)
XLA Modules:
  0.0 58.8 jit_solution(158936736057059263)
XLA Ops:
  0.6 1.1 %copy-done = bf16[80,8,4,128]{3,2,1,0:T(4,128)(2,1)S(1)} copy-done((bf16[80,8,4,128]{3,2,1,0:T(4,128)(2,1)S(1)}, bf16[80,8,4,128]{3,2,1,0:T(4,128)(2,1)}, u32[]{:S(2)}) %copy-start) | copy-done | bytes 655384
  1.7 0.9 %pack.1 = (bf16[656,128]{1,0:T(8,128)(2,1)S(1)}, bf16[656,128]{1,0:T(8,128)(2,1)S(1)}, bf16[656,128]{1,0:T(8,128)(2,1)S(1)}, bf16[656,128]{1,0:T(8,128)(2,1)S(1)}) custom-call(bf16[2560,128]{1,0:T(8,128)(2,1)S(1)} %bitcast.49), custom_call_target="tpu_custom_call" | custom-call | tf_op jit(solution)/shard_map/pack/pallas_call | solution.py:56
  2.6 4.1 %collective-permute-start.1 = (bf16[656,128]{1,0:T(8,128)(2,1)S(1)}, bf16[656,128]{1,0:T(8,128)(2,1)S(1)}, u32[]{:S(2)}, u32[]{:S(2)}) collective-permute-start(bf16[656,128]{1,0:T(8,128)(2,1)S(1)} %get-tuple-element.36), channel_id=1, source_target_pairs={{0,8},{4,12},{8,0},{12,4},{1,9},{5,13},{9,1},{13,5},{2,10},{6,14},... | collective-permute-start | bytes 503816 | tf_op jit(solution)/shard_map/ppermute | solution.py:369
  6.8 1.6 %collective-permute-start = (bf16[656,128]{1,0:T(8,128)(2,1)S(1)}, bf16[656,128]{1,0:T(8,128)(2,1)S(1)}, u32[]{:S(2)}, u32[]{:S(2)}) collective-permute-start(bf16[656,128]{1,0:T(8,128)(2,1)S(1)} %get-tuple-element.49.refs_4_), channel_id=1, source_target_pairs={{0,4},{4,0},{8,12},{12,8},{1,5},{5,1},{9,13},{13,9},{2,6},{6,2},{1... | collective-permute-start | bytes 503816 | tf_op jit(solution)/shard_map/ppermute | solution.py:369
  8.3 8.0 %collective-permute-done.1.refs_2_ = bf16[656,128]{1,0:T(8,128)(2,1)S(1)} collective-permute-done((bf16[656,128]{1,0:T(8,128)(2,1)S(1)}, bf16[656,128]{1,0:T(8,128)(2,1)S(1)}, u32[]{:S(2)}, u32[]{:S(2)}) %collective-permute-start.1) | collective-permute-done | bytes 167968 | tf_op jit(solution)/shard_map/ppermute | solution.py:369
  16.3 3.2 %collective-permute-done.2.refs_3_ = bf16[656,128]{1,0:T(8,128)(2,1)S(1)} collective-permute-done((bf16[656,128]{1,0:T(8,128)(2,1)S(1)}, bf16[656,128]{1,0:T(8,128)(2,1)S(1)}, u32[]{:S(2)}, u32[]{:S(2)}) %collective-permute-start.2) | collective-permute-done | bytes 167968 | tf_op jit(solution)/shard_map/ppermute | solution.py:369
  19.6 0.8 %own.1 = (f32[256,512]{1,0:T(8,128)S(1)}, f32[256,512]{1,0:T(8,128)S(1)}, f32[2,264,512]{2,1,0:T(8,128)S(1)}, f32[8,512]{1,0:T(8,128)S(1)}) custom-call(bf16[656,128]{1,0:T(8,128)(2,1)S(1)} %get-tuple-element.40.refs_0_, bf16[656,128]{1,0:T(8,128)(2,1)S(1)} %collective-permute-done.refs_1_, bf16[656,128]{1,0:T(8,128)(2,1)S(1)} %collective-permute-done.1.refs_2_, ...), custom_call_target="tpu_custom_call" | custom-call | tf_op jit(solution)/shard_map/own/pallas_call | solution.py:133
  20.4 3.2 %collective-permute-start.6 = (bf16[1920,128]{1,0:T(8,128)(2,1)S(1)}, bf16[1920,128]{1,0:T(8,128)(2,1)S(1)}, u32[]{:S(2)}, u32[]{:S(2)}) collective-permute-start(bf16[1920,128]{1,0:T(8,128)(2,1)S(1)} %get-tuple-element.38), channel_id=1, source_target_pairs={{0,4},{1,5},{2,6},{3,7},{4,0},{5,1},{6,2},{7,3},{8,12},{9,13},{10,... | collective-permute-start | bytes 1474568 | tf_op jit(solution)/shard_map/ppermute | solution.py:372
  24.0 1.6 %collective-permute-start.4 = (f16[256,512]{1,0:T(8,128)(2,1)S(1)}, f16[256,512]{1,0:T(8,128)(2,1)S(1)}, u32[]{:S(2)}, u32[]{:S(2)}) collective-permute-start(f16[256,512]{1,0:T(8,128)(2,1)S(1)} %fusion.9), channel_id=1, source_target_pairs={{0,2},{1,3},{2,0},{3,1},{4,6},{5,7},{6,4},{7,5},{8,10},{9,11},{10,... | collective-permute-start | bytes 786440 | tf_op jit(solution)/shard_map/ppermute | solution.py:381
  26.1 0.8 %energies.1 = (f32[2,128,128]{2,1,0:T(8,128)S(1)}, f32[2,3,4,128]{3,2,1,0:T(4,128)S(1)}) custom-call(s32[2,3]{1,0:T(2,128)S(1)} %copy-done.2, f32[4,8]{1,0:T(4,128)S(1)} %bitcast.54, s32[8,128]{1,0:T(8,128)S(1)} %copy-done.3, f32[8,128]{1,0:T(8,128)S(1)} %bitcast.53), custom_call_target="tpu_custom_call" | custom-call | tf_op jit(solution)/shard_map/energies/pallas_call | solution.py:348
  26.9 6.1 %collective-permute-done.5.top_ref = f32[8,512]{1,0:T(8,128)S(1)} collective-permute-done((f32[8,512]{1,0:T(8,128)S(1)}, f32[8,512]{1,0:T(8,128)S(1)}, u32[]{:S(2)}, u32[]{:S(2)}) %collective-permute-start.5) | collective-permute-done | bytes 16416 | tf_op jit(solution)/shard_map/ppermute | solution.py:387
  33.2 2.3 %collective-permute-done.6.refs_6_ = bf16[1920,128]{1,0:T(8,128)(2,1)S(1)} collective-permute-done((bf16[1920,128]{1,0:T(8,128)(2,1)S(1)}, bf16[1920,128]{1,0:T(8,128)(2,1)S(1)}, u32[]{:S(2)}, u32[]{:S(2)}) %collective-permute-start.6) | collective-permute-done | bytes 491552 | tf_op jit(solution)/shard_map/ppermute | solution.py:372
  35.4 1.0 %near.2 = (f32[128,512]{1,0:T(8,128)S(1)}, f32[128,512]{1,0:T(8,128)S(1)}, f32[2,128,512]{2,1,0:T(8,128)S(1)}) custom-call(s32[2,3]{1,0:T(2,128)S(1)} %copy-done.2, bf16[656,128]{1,0:T(8,128)(2,1)S(1)} %get-tuple-element.40.refs_0_, bf16[656,128]{1,0:T(8,128)(2,1)S(1)} %collective-permute-done.refs_1_, bf16[656,128]{1,0:T(8,128)(2,1)S(1)} %collective-permute-done.1.refs_2_, ...), custom_call_target="tpu_custom_call" | custom-call | tf_op jit(solution)/shard_map/near/pallas_call | solution.py:183
  36.6 1.6 %near.3 = (f32[384,512]{1,0:T(8,128)S(1)}, f32[384,512]{1,0:T(8,128)S(1)}, f32[2,384,512]{2,1,0:T(8,128)S(1)}) custom-call(s32[2,3]{1,0:T(2,128)S(1)} %copy-done.2, bf16[656,128]{1,0:T(8,128)(2,1)S(1)} %get-tuple-element.40.refs_0_, bf16[656,128]{1,0:T(8,128)(2,1)S(1)} %collective-permute-done.refs_1_, bf16[656,128]{1,0:T(8,128)(2,1)S(1)} %collective-permute-done.1.refs_2_, ...), custom_call_target="tpu_custom_call" | custom-call | tf_op jit(solution)/shard_map/near/pallas_call | solution.py:183
  38.8 1.5 %collective-permute-start.11 = (f16[128,512]{1,0:T(8,128)(2,1)S(1)}, f16[128,512]{1,0:T(8,128)(2,1)S(1)}, u32[]{:S(2)}, u32[]{:S(2)}) collective-permute-start(f16[128,512]{1,0:T(8,128)(2,1)S(1)} %fusion.14), channel_id=1, source_target_pairs={{0,2},{1,3},{2,0},{3,1},{4,6},{5,7},{6,4},{7,5},{8,10},{9,11},{10,... | collective-permute-start | bytes 393224 | tf_op jit(solution)/shard_map/ppermute | solution.py:400
  40.3 1.7 %collective-permute-done.9 = f32[2,384,512]{2,1,0:T(8,128)S(1)} collective-permute-done((f32[2,384,512]{2,1,0:T(8,128)S(1)}, f32[2,384,512]{2,1,0:T(8,128)S(1)}, u32[]{:S(2)}, u32[]{:S(2)}) %collective-permute-start.9) | collective-permute-done | bytes 1572896 | tf_op jit(solution)/shard_map/ppermute | solution.py:376
  42.2 1.6 %collective-permute-start.10 = (f16[384,512]{1,0:T(8,128)(2,1)S(1)}, f16[384,512]{1,0:T(8,128)(2,1)S(1)}, u32[]{:S(2)}, u32[]{:S(2)}) collective-permute-start(f16[384,512]{1,0:T(8,128)(2,1)S(1)} %fusion.2), channel_id=1, source_target_pairs={{0,2},{1,3},{2,0},{3,1},{4,6},{5,7},{6,4},{7,5},{8,10},{9,11},{10,... | collective-permute-start | bytes 1179656 | tf_op jit(solution)/shard_map/ppermute | solution.py:400
  43.9 0.9 %finish.2 = (f32[2,3,128,512]{3,2,1,0:T(8,128)}, f32[2,4,128]{2,1,0:T(4,128)S(1)}) custom-call(f32[256,512]{1,0:T(8,128)S(1)} %fusion.6.total_ref, f32[2,128,128]{2,1,0:T(8,128)S(1)} %get-tuple-element.46.row_ref, f32[2,3,4,128]{3,2,1,0:T(4,128)S(1)} %get-tuple-element.57.col_ref), custom_call_target="tpu_custom_call" | custom-call | tf_op jit(solution)/shard_map/finish/pallas_call | solution.py:248
  44.8 0.8 %finish.3 = (f32[2,3,128,512]{3,2,1,0:T(8,128)}, f32[1,4,128]{2,1,0:T(4,128)S(1)}) custom-call(f32[128,512]{1,0:T(8,128)S(1)} %fusion.11.total_ref, f32[2,128,128]{2,1,0:T(8,128)S(1)} %get-tuple-element.46.row_ref, f32[2,3,4,128]{3,2,1,0:T(4,128)S(1)} %get-tuple-element.57.col_ref, ...), custom_call_target="tpu_custom_call", output_to_operand_aliasing={{0}: (3, {})} | custom-call | tf_op jit(solution)/shard_map/finish/pallas_call | solution.py:248
  45.6 7.9 %collective-permute-done.10 = f16[384,512]{1,0:T(8,128)(2,1)S(1)} collective-permute-done((f16[384,512]{1,0:T(8,128)(2,1)S(1)}, f16[384,512]{1,0:T(8,128)(2,1)S(1)}, u32[]{:S(2)}, u32[]{:S(2)}) %collective-permute-start.10) | collective-permute-done | bytes 393248 | tf_op jit(solution)/shard_map/ppermute | solution.py:400
  54.5 1.1 %collective-permute-start.13 = (f32[2,3,4,4]{3,2,1,0:T(4,128)S(1)}, f32[2,3,4,4]{3,2,1,0:T(4,128)S(1)}, u32[]{:S(2)}, u32[]{:S(2)}) collective-permute-start(f32[2,3,4,4]{3,2,1,0:T(4,128)S(1)} %get-tuple-element.65.refs_0_), channel_id=1, source_target_pairs={{0,2},{1,3},{2,0},{3,1},{4,6},{5,7},{6,4},{7,5},{8,10},{9,11},{10,... | collective-permute-start | bytes 1160 | tf_op jit(solution)/shard_map/ppermute | solution.py:411
  55.9 0.9 %put.1 = f32[2,3,128,512]{3,2,1,0:T(8,128)} custom-call(f32[3,128,512]{2,1,0:T(8,128)S(1)} %get-tuple-element.63.values_ref, f32[2,3,128,512]{3,2,1,0:T(8,128)} %get-tuple-element.64._), custom_call_target="tpu_custom_call", output_to_operand_aliasing={{}: (1, {})} | custom-call | tf_op jit(solution)/shard_map/put/pallas_call | solution.py:299
  57.2 1.0 %collective-permute-done.13.refs_2_ = f32[2,3,4,4]{3,2,1,0:T(4,128)S(1)} collective-permute-done((f32[2,3,4,4]{3,2,1,0:T(4,128)S(1)}, f32[2,3,4,4]{3,2,1,0:T(4,128)S(1)}, u32[]{:S(2)}, u32[]{:S(2)}) %collective-permute-start.13) | collective-permute-done | bytes 416 | tf_op jit(solution)/shard_map/ppermute | solution.py:411
  58.2 0.6 %last.1 = f32[2,3,4,4]{3,2,1,0:T(4,128)} custom-call(f32[2,3,4,4]{3,2,1,0:T(4,128)S(1)} %get-tuple-element.65.refs_0_, f32[2,3,4,4]{3,2,1,0:T(4,128)S(1)} %collective-permute-done.12.refs_1_, f32[2,3,4,4]{3,2,1,0:T(4,128)S(1)} %collective-permute-done.13.refs_2_, f32[2,3,4,4]{3,2,1,0:T(4,128)S(1)} %collective-permute-done.14.refs_3_), custom_call_target="tpu_custom_call" | custom-call | tf_op jit(solution)/shard_map/last/pallas_call | solution.py:314
  (44 shorter events, 4.1 us)
Async XLA Ops:
  0.6 1.1 %copy-start = (bf16[80,8,4,128]{3,2,1,0:T(4,128)(2,1)S(1)}, bf16[80,8,4,128]{3,2,1,0:T(4,128)(2,1)}, u32[]{:S(2)}) copy-start(bf16[80,8,4,128]{3,2,1,0:T(4,128)(2,1)} %param.5) | copy-start | bytes 1966084
  2.6 13.6 %collective-permute-start.1 = (bf16[656,128]{1,0:T(8,128)(2,1)S(1)}, bf16[656,128]{1,0:T(8,128)(2,1)S(1)}, u32[]{:S(2)}, u32[]{:S(2)}) collective-permute-start(bf16[656,128]{1,0:T(8,128)(2,1)S(1)} %get-tuple-element.36), channel_id=1, source_target_pairs={{0,8},{4,12},{8,0},{12,4},{1,9},{5,13},{9,1},{13,5},{2,10},{6,14},... | collective-permute-start | bytes 503816 | tf_op jit(solution)/shard_map/ppermute | solution.py:369
  6.8 9.5 %collective-permute-start = (bf16[656,128]{1,0:T(8,128)(2,1)S(1)}, bf16[656,128]{1,0:T(8,128)(2,1)S(1)}, u32[]{:S(2)}, u32[]{:S(2)}) collective-permute-start(bf16[656,128]{1,0:T(8,128)(2,1)S(1)} %get-tuple-element.49.refs_4_), channel_id=1, source_target_pairs={{0,4},{4,0},{8,12},{12,8},{1,5},{5,1},{9,13},{13,9},{2,6},{6,2},{1... | collective-permute-start | bytes 503816 | tf_op jit(solution)/shard_map/ppermute | solution.py:369
  8.3 11.1 %collective-permute-start.2 = (bf16[656,128]{1,0:T(8,128)(2,1)S(1)}, bf16[656,128]{1,0:T(8,128)(2,1)S(1)}, u32[]{:S(2)}, u32[]{:S(2)}) collective-permute-start(bf16[656,128]{1,0:T(8,128)(2,1)S(1)} %get-tuple-element.37.refs_5_), channel_id=1, source_target_pairs={{0,12},{4,8},{8,4},{12,0},{1,13},{5,9},{9,5},{13,1},{2,14},{6,10},... | collective-permute-start | bytes 503816 | tf_op jit(solution)/shard_map/ppermute | solution.py:369
  19.5 6.6 %copy-start.2 = (s32[2,3]{1,0:T(2,128)S(1)}, s32[2,3]{1,0:T(2,128)}, u32[]{:S(2)}) copy-start(s32[2,3]{1,0:T(2,128)} %partners_ref.5) | copy-start | bytes 76
  19.6 6.6 %copy-start.3 = (s32[8,128]{1,0:T(8,128)S(1)}, s32[8,128]{1,0:T(8,128)}, u32[]{:S(2)}) copy-start(s32[8,128]{1,0:T(8,128)} %domains_ref.1) | copy-start | bytes 12292
  19.6 6.6 %copy-start.4 = (f32[1024]{0:T(1024)S(1)}, f32[1024]{0:T(1024)}, u32[]{:S(2)}) copy-start(f32[1024]{0:T(1024)} %param.9) | copy-start | bytes 12292
  19.6 6.6 %copy-start.5 = (f32[8,4]{0,1:T(4,128)S(1)}, f32[8,4]{0,1:T(4,128)}, u32[]{:S(2)}) copy-start(f32[8,4]{0,1:T(4,128)} %param.8) | copy-start | bytes 388
  20.4 3.4 %collective-permute-start.3 = (f32[2,264,512]{2,1,0:T(8,128)S(1)}, f32[2,264,512]{2,1,0:T(8,128)S(1)}, u32[]{:S(2)}, u32[]{:S(2)}) collective-permute-start(f32[2,264,512]{2,1,0:T(8,128)S(1)} %get-tuple-element.42), channel_id=1, source_target_pairs={{0,1},{1,0},{2,3},{3,2},{4,5},{5,4},{6,7},{7,6},{8,9},{9,8},{10,11... | collective-permute-start | bytes 3244040 | tf_op jit(solution)/shard_map/ppermute | solution.py:376
  20.4 15.0 %collective-permute-start.6 = (bf16[1920,128]{1,0:T(8,128)(2,1)S(1)}, bf16[1920,128]{1,0:T(8,128)(2,1)S(1)}, u32[]{:S(2)}, u32[]{:S(2)}) collective-permute-start(bf16[1920,128]{1,0:T(8,128)(2,1)S(1)} %get-tuple-element.38), channel_id=1, source_target_pairs={{0,4},{1,5},{2,6},{3,7},{4,0},{5,1},{6,2},{7,3},{8,12},{9,13},{10,... | collective-permute-start | bytes 1474568 | tf_op jit(solution)/shard_map/ppermute | solution.py:372
  23.6 11.8 %collective-permute-start.7 = (bf16[1920,128]{1,0:T(8,128)(2,1)S(1)}, bf16[1920,128]{1,0:T(8,128)(2,1)S(1)}, u32[]{:S(2)}, u32[]{:S(2)}) collective-permute-start(bf16[1920,128]{1,0:T(8,128)(2,1)S(1)} %get-tuple-element.39), channel_id=1, source_target_pairs={{0,1},{1,0},{2,3},{3,2},{4,8},{5,9},{6,10},{7,11},{8,4},{9,5},{10,... | collective-permute-start | bytes 1474568 | tf_op jit(solution)/shard_map/ppermute | solution.py:372
  24.0 9.1 %collective-permute-start.4 = (f16[256,512]{1,0:T(8,128)(2,1)S(1)}, f16[256,512]{1,0:T(8,128)(2,1)S(1)}, u32[]{:S(2)}, u32[]{:S(2)}) collective-permute-start(f16[256,512]{1,0:T(8,128)(2,1)S(1)} %fusion.9), channel_id=1, source_target_pairs={{0,2},{1,3},{2,0},{3,1},{4,6},{5,7},{6,4},{7,5},{8,10},{9,11},{10,... | collective-permute-start | bytes 786440 | tf_op jit(solution)/shard_map/ppermute | solution.py:381
  25.6 7.4 %collective-permute-start.5 = (f32[8,512]{1,0:T(8,128)S(1)}, f32[8,512]{1,0:T(8,128)S(1)}, u32[]{:S(2)}, u32[]{:S(2)}) collective-permute-start(f32[8,512]{1,0:T(8,128)S(1)} %get-tuple-element.45), channel_id=1, source_target_pairs={{0,2},{1,3},{2,0},{3,1},{4,6},{5,7},{6,4},{7,5},{8,10},{9,11},{10,... | collective-permute-start | bytes 49160 | tf_op jit(solution)/shard_map/ppermute | solution.py:387
  33.1 5.7 %copy-start.1 = (f32[8,512]{1,0:T(8,128)}, f32[8,512]{1,0:T(8,128)S(1)}, u32[]{:S(2)}) copy-start(f32[8,512]{1,0:T(8,128)S(1)} %scale_up.1) | copy-start | bytes 49156
  36.5 2.0 %collective-permute-start.8 = (f32[2,128,512]{2,1,0:T(8,128)S(1)}, f32[2,128,512]{2,1,0:T(8,128)S(1)}, u32[]{:S(2)}, u32[]{:S(2)}) collective-permute-start(f32[2,128,512]{2,1,0:T(8,128)S(1)} %get-tuple-element.53), channel_id=1, source_target_pairs={{0,1},{1,0},{2,3},{3,2},{4,5},{5,4},{6,7},{7,6},{8,9},{9,8},{10,11... | collective-permute-start | bytes 1572872 | tf_op jit(solution)/shard_map/ppermute | solution.py:376
  38.5 3.5 %collective-permute-start.9 = (f32[2,384,512]{2,1,0:T(8,128)S(1)}, f32[2,384,512]{2,1,0:T(8,128)S(1)}, u32[]{:S(2)}, u32[]{:S(2)}) collective-permute-start(f32[2,384,512]{2,1,0:T(8,128)S(1)} %get-tuple-element.54), channel_id=1, source_target_pairs={{0,1},{1,0},{2,3},{3,2},{4,5},{5,4},{6,7},{7,6},{8,9},{9,8},{10,11... | collective-permute-start | bytes 4718600 | tf_op jit(solution)/shard_map/ppermute | solution.py:376
  38.8 4.9 %slice-start = ((f32[8,512]{1,0:T(8,128)}), f32[1,512]{1,0:T(1,128)S(1)}, s32[]{:S(2)}) async-start(f32[8,512]{1,0:T(8,128)} %copy-done.1), calls=%async_computation | async-start | bytes 4096 | tf_op jit(solution)/shard_map/slice | solution.py:406
  38.8 5.9 %collective-permute-start.11 = (f16[128,512]{1,0:T(8,128)(2,1)S(1)}, f16[128,512]{1,0:T(8,128)(2,1)S(1)}, u32[]{:S(2)}, u32[]{:S(2)}) collective-permute-start(f16[128,512]{1,0:T(8,128)(2,1)S(1)} %fusion.14), channel_id=1, source_target_pairs={{0,2},{1,3},{2,0},{3,1},{4,6},{5,7},{6,4},{7,5},{8,10},{9,11},{10,... | collective-permute-start | bytes 393224 | tf_op jit(solution)/shard_map/ppermute | solution.py:400
  42.2 2.6 %slice-start.1 = ((f32[8,512]{1,0:T(8,128)}), f32[1,512]{1,0:T(1,128)S(1)}, s32[]{:S(2)}) async-start(f32[8,512]{1,0:T(8,128)} %copy-done.1), calls=%async_computation.1 | async-start | bytes 4096 | tf_op jit(solution)/shard_map/slice | solution.py:406
  42.2 11.3 %collective-permute-start.10 = (f16[384,512]{1,0:T(8,128)(2,1)S(1)}, f16[384,512]{1,0:T(8,128)(2,1)S(1)}, u32[]{:S(2)}, u32[]{:S(2)}) collective-permute-start(f16[384,512]{1,0:T(8,128)(2,1)S(1)} %fusion.2), channel_id=1, source_target_pairs={{0,2},{1,3},{2,0},{3,1},{4,6},{5,7},{6,4},{7,5},{8,10},{9,11},{10,... | collective-permute-start | bytes 1179656 | tf_op jit(solution)/shard_map/ppermute | solution.py:400
  44.7 8.8 %slice-start.2 = ((f32[8,512]{1,0:T(8,128)}), f32[1,512]{1,0:T(1,128)S(1)}, s32[]{:S(2)}) async-start(f32[8,512]{1,0:T(8,128)} %copy-done.1), calls=%async_computation.2 | async-start | bytes 4096 | tf_op jit(solution)/shard_map/slice | solution.py:406
  54.0 3.2 %collective-permute-start.14 = (f32[2,3,4,4]{3,2,1,0:T(4,128)S(1)}, f32[2,3,4,4]{3,2,1,0:T(4,128)S(1)}, u32[]{:S(2)}, u32[]{:S(2)}) collective-permute-start(f32[2,3,4,4]{3,2,1,0:T(4,128)S(1)} %get-tuple-element.65.refs_0_), channel_id=1, source_target_pairs={{0,3},{1,2},{2,1},{3,0},{4,7},{5,6},{6,5},{7,4},{8,11},{9,10},{10,... | collective-permute-start | bytes 1160 | tf_op jit(solution)/shard_map/ppermute | solution.py:411
  54.5 3.7 %collective-permute-start.13 = (f32[2,3,4,4]{3,2,1,0:T(4,128)S(1)}, f32[2,3,4,4]{3,2,1,0:T(4,128)S(1)}, u32[]{:S(2)}, u32[]{:S(2)}) collective-permute-start(f32[2,3,4,4]{3,2,1,0:T(4,128)S(1)} %get-tuple-element.65.refs_0_), channel_id=1, source_target_pairs={{0,2},{1,3},{2,0},{3,1},{4,6},{5,7},{6,4},{7,5},{8,10},{9,11},{10,... | collective-permute-start | bytes 1160 | tf_op jit(solution)/shard_map/ppermute | solution.py:411
  55.6 2.6 %collective-permute-start.12 = (f32[2,3,4,4]{3,2,1,0:T(4,128)S(1)}, f32[2,3,4,4]{3,2,1,0:T(4,128)S(1)}, u32[]{:S(2)}, u32[]{:S(2)}) collective-permute-start(f32[2,3,4,4]{3,2,1,0:T(4,128)S(1)} %get-tuple-element.65.refs_0_), channel_id=1, source_target_pairs={{0,1},{1,0},{2,3},{3,2},{4,5},{5,4},{6,7},{7,6},{8,9},{9,8},{10,11... | collective-permute-start | bytes 1160 | tf_op jit(solution)/shard_map/ppermute | solution.py:411

commit v4 on v3

--- a/solution.py
+++ b/solution.py
@@ -152,11 +152,17 @@
     def kernel(partners_ref, *refs):
         own_refs, here_refs, side_refs = refs[:count], refs[count : count + 2], refs[count + 2 :][:2]
         z = lax.axis_index("aux")
-        even = lax.rem(z, 2) == 0
-
-        def panels(w, j, slot):
-            from_first = (w > 3) == even
-            at = (2 * j + lax.rem(w, 2)) * depth
+
+        def panels(r, j, slot):
+            if slot == 1:
+                w = (partners_ref[r : r + 1, slot : slot + 1] if only_first else partners_ref[r, slot]) - 2 * z + 2
+                from_first = jnp.where(w > 3, 1, 0) != lax.rem(z, 2)
+                from_first = jnp.broadcast_to(from_first, (depth, domain))
+                at = (2 * j + r) * depth
+            else:
+                w = partners_ref[r, slot] - 2 * z + 2
+                from_first = (w > 3) == (lax.rem(z, 2) == 0)
+                at = (2 * j + lax.rem(w, 2)) * depth
             found = []
             for k in range(count):
                 refs, start = (here_refs, at) if k == 0 else (side_refs, at + (k - 1) * rows)
@@ -170,12 +176,12 @@
 
         for n, tiles in enumerate(groups):
             for t, (r, slot) in enumerate(tiles):
-                w = partners_ref[r, slot] - 2 * z + 2
-                right = jnp.concatenate([panels(w, j, slot) for j in range(orbitals)], axis=1)
+                right = jnp.concatenate([panels(r, j, slot) for j in range(orbitals)], axis=1)
                 sums = product(left_rows(own_refs, depth, r), right)
                 at = slice(t * domain, (t + 1) * domain)
                 store_sums(sums, at, *refs[count + 4 + 3 * n :][:3])
 
+    only_first = all(slot == 1 for tiles in groups for _, slot in tiles)
     outs = []
     for tiles in groups:
         height = len(tiles) * domain
@@ -184,7 +190,7 @@
         kernel,
         "near",
         out_shape=outs,
-        in_specs=[SMEM] + [VMEM] * (count + 4),
+        in_specs=[VMEM if only_first else SMEM] + [VMEM] * (count + 4),
         out_specs=[VMEM] * len(outs),
     )(partners, *own, *here, *sides)
 

time: 59 us -> 58.5 us (level)
  no operation moved by 1% of the time
where the time goes in v4:
time: 58.5 us; the launch traced here: 58.3 us
  waiting for transfers between devices  30.7 us (52%)
  starting transfers between devices  16.5 us (28%)
  Pallas kernels  8.37 us (14%)
  local copies, waits for them, and re-layouts  1.13 us (2%)
  between operations  0.84 us (1%)
  other arithmetic  0.76 us (1%)
    ppermute x3, waiting for transfers between devices, fast(): own.append(lax.ppermute(send, 'aux', [(i, i ^ k) for i in range(count)]))  11.1 us
    ppermute x2, waiting for transfers between devices, fast(): parts.append((mine, got, lax.ppermute(half, 'pair', cross)))  7.86 us
    ppermute x1, waiting for transfers between devices, fast(): from_half = scale_up(lax.ppermute(top, 'pair', cross), 2 * count * depth)  6.1 us
    ppermute x3, starting transfers between devices, fast(): own.append(lax.ppermute(send, 'aux', [(i, i ^ k) for i in range(count)]))  5.68 us
    ppermute x2, starting transfers between devices, fast(): lax.ppermute(m, ('aux', 'pair'), side)  3.34 us
    ppermute x2, starting transfers between devices, fast(): parts.append((mine, got, lax.ppermute(half, 'pair', cross)))  3.04 us
    ppermute x2, waiting for transfers between devices, fast(): lax.ppermute(m, ('aux', 'pair'), side)  2.26 us
    pallas_call x2, Pallas kernels, near_pairs(): call(kernel, 'near', out_shape=outs, in_specs=[VMEM if only_first else SM...  2.19 us
  transfers between devices with their start and end apart: 15, of which 9 were waited for; matrix products, arithmetic and copies ran while one was open for 1% of the time, Pallas kernels for 9%

profile of v4, /device:TPU:0, one launch (start us, length us, event | category | flops | bytes accessed | tf_op | source)
XLA Modules:
  0.0 58.3 jit_solution(16726269532502903173)
XLA Ops:
  0.6 1.1 %copy-done = bf16[80,8,4,128]{3,2,1,0:T(4,128)(2,1)S(1)} copy-done((bf16[80,8,4,128]{3,2,1,0:T(4,128)(2,1)S(1)}, bf16[80,8,4,128]{3,2,1,0:T(4,128)(2,1)}, u32[]{:S(2)}) %copy-start) | copy-done | bytes 655384
  1.7 0.9 %pack.1 = (bf16[656,128]{1,0:T(8,128)(2,1)S(1)}, bf16[656,128]{1,0:T(8,128)(2,1)S(1)}, bf16[656,128]{1,0:T(8,128)(2,1)S(1)}, bf16[656,128]{1,0:T(8,128)(2,1)S(1)}) custom-call(bf16[2560,128]{1,0:T(8,128)(2,1)S(1)} %bitcast.49), custom_call_target="tpu_custom_call" | custom-call | tf_op jit(solution)/shard_map/pack/pallas_call | solution.py:56
  2.6 4.1 %collective-permute-start.1 = (bf16[656,128]{1,0:T(8,128)(2,1)S(1)}, bf16[656,128]{1,0:T(8,128)(2,1)S(1)}, u32[]{:S(2)}, u32[]{:S(2)}) collective-permute-start(bf16[656,128]{1,0:T(8,128)(2,1)S(1)} %get-tuple-element.36), channel_id=1, source_target_pairs={{0,8},{4,12},{8,0},{12,4},{1,9},{5,13},{9,1},{13,5},{2,10},{6,14},... | collective-permute-start | bytes 503816 | tf_op jit(solution)/shard_map/ppermute | solution.py:375
  6.8 1.6 %collective-permute-start = (bf16[656,128]{1,0:T(8,128)(2,1)S(1)}, bf16[656,128]{1,0:T(8,128)(2,1)S(1)}, u32[]{:S(2)}, u32[]{:S(2)}) collective-permute-start(bf16[656,128]{1,0:T(8,128)(2,1)S(1)} %get-tuple-element.49.refs_4_), channel_id=1, source_target_pairs={{0,4},{4,0},{8,12},{12,8},{1,5},{5,1},{9,13},{13,9},{2,6},{6,2},{1... | collective-permute-start | bytes 503816 | tf_op jit(solution)/shard_map/ppermute | solution.py:375
  8.3 8.0 %collective-permute-done.1.refs_2_ = bf16[656,128]{1,0:T(8,128)(2,1)S(1)} collective-permute-done((bf16[656,128]{1,0:T(8,128)(2,1)S(1)}, bf16[656,128]{1,0:T(8,128)(2,1)S(1)}, u32[]{:S(2)}, u32[]{:S(2)}) %collective-permute-start.1) | collective-permute-done | bytes 167968 | tf_op jit(solution)/shard_map/ppermute | solution.py:375
  16.3 3.2 %collective-permute-done.2.refs_3_ = bf16[656,128]{1,0:T(8,128)(2,1)S(1)} collective-permute-done((bf16[656,128]{1,0:T(8,128)(2,1)S(1)}, bf16[656,128]{1,0:T(8,128)(2,1)S(1)}, u32[]{:S(2)}, u32[]{:S(2)}) %collective-permute-start.2) | collective-permute-done | bytes 167968 | tf_op jit(solution)/shard_map/ppermute | solution.py:375
  19.6 0.8 %own.1 = (f32[256,512]{1,0:T(8,128)S(1)}, f32[256,512]{1,0:T(8,128)S(1)}, f32[2,264,512]{2,1,0:T(8,128)S(1)}, f32[8,512]{1,0:T(8,128)S(1)}) custom-call(bf16[656,128]{1,0:T(8,128)(2,1)S(1)} %get-tuple-element.40.refs_0_, bf16[656,128]{1,0:T(8,128)(2,1)S(1)} %collective-permute-done.refs_1_, bf16[656,128]{1,0:T(8,128)(2,1)S(1)} %collective-permute-done.1.refs_2_, ...), custom_call_target="tpu_custom_call" | custom-call | tf_op jit(solution)/shard_map/own/pallas_call | solution.py:133
  20.4 3.2 %collective-permute-start.6 = (bf16[1920,128]{1,0:T(8,128)(2,1)S(1)}, bf16[1920,128]{1,0:T(8,128)(2,1)S(1)}, u32[]{:S(2)}, u32[]{:S(2)}) collective-permute-start(bf16[1920,128]{1,0:T(8,128)(2,1)S(1)} %get-tuple-element.38), channel_id=1, source_target_pairs={{0,4},{1,5},{2,6},{3,7},{4,0},{5,1},{6,2},{7,3},{8,12},{9,13},{10,... | collective-permute-start | bytes 1474568 | tf_op jit(solution)/shard_map/ppermute | solution.py:378
  24.0 1.6 %collective-permute-start.4 = (f16[256,512]{1,0:T(8,128)(2,1)S(1)}, f16[256,512]{1,0:T(8,128)(2,1)S(1)}, u32[]{:S(2)}, u32[]{:S(2)}) collective-permute-start(f16[256,512]{1,0:T(8,128)(2,1)S(1)} %fusion.9), channel_id=1, source_target_pairs={{0,2},{1,3},{2,0},{3,1},{4,6},{5,7},{6,4},{7,5},{8,10},{9,11},{10,... | collective-permute-start | bytes 786440 | tf_op jit(solution)/shard_map/ppermute | solution.py:387
  26.1 0.8 %energies.1 = (f32[2,128,128]{2,1,0:T(8,128)S(1)}, f32[2,3,4,128]{3,2,1,0:T(4,128)S(1)}) custom-call(s32[2,3]{1,0:T(2,128)S(1)} %copy-done.2, f32[4,8]{1,0:T(4,128)S(1)} %bitcast.54, s32[8,128]{1,0:T(8,128)S(1)} %copy-done.3, f32[8,128]{1,0:T(8,128)S(1)} %bitcast.53), custom_call_target="tpu_custom_call" | custom-call | tf_op jit(solution)/shard_map/energies/pallas_call | solution.py:354
  26.9 6.1 %collective-permute-done.5.top_ref = f32[8,512]{1,0:T(8,128)S(1)} collective-permute-done((f32[8,512]{1,0:T(8,128)S(1)}, f32[8,512]{1,0:T(8,128)S(1)}, u32[]{:S(2)}, u32[]{:S(2)}) %collective-permute-start.5) | collective-permute-done | bytes 16416 | tf_op jit(solution)/shard_map/ppermute | solution.py:393
  33.2 2.3 %collective-permute-done.6.refs_6_ = bf16[1920,128]{1,0:T(8,128)(2,1)S(1)} collective-permute-done((bf16[1920,128]{1,0:T(8,128)(2,1)S(1)}, bf16[1920,128]{1,0:T(8,128)(2,1)S(1)}, u32[]{:S(2)}, u32[]{:S(2)}) %collective-permute-start.6) | collective-permute-done | bytes 491552 | tf_op jit(solution)/shard_map/ppermute | solution.py:378
  35.4 0.6 near.2
  36.1 1.6 %near.3 = (f32[384,512]{1,0:T(8,128)S(1)}, f32[384,512]{1,0:T(8,128)S(1)}, f32[2,384,512]{2,1,0:T(8,128)S(1)}) custom-call(s32[2,3]{1,0:T(2,128)S(1)} %copy-done.2, bf16[656,128]{1,0:T(8,128)(2,1)S(1)} %get-tuple-element.40.refs_0_, bf16[656,128]{1,0:T(8,128)(2,1)S(1)} %collective-permute-done.refs_1_, bf16[656,128]{1,0:T(8,128)(2,1)S(1)} %collective-permute-done.1.refs_2_, ...), custom_call_target="tpu_custom_call" | custom-call | tf_op jit(solution)/shard_map/near/pallas_call | solution.py:189
  38.3 1.5 %collective-permute-start.11 = (f16[128,512]{1,0:T(8,128)(2,1)S(1)}, f16[128,512]{1,0:T(8,128)(2,1)S(1)}, u32[]{:S(2)}, u32[]{:S(2)}) collective-permute-start(f16[128,512]{1,0:T(8,128)(2,1)S(1)} %fusion.14), channel_id=1, source_target_pairs={{0,2},{1,3},{2,0},{3,1},{4,6},{5,7},{6,4},{7,5},{8,10},{9,11},{10,... | collective-permute-start | bytes 393224 | tf_op jit(solution)/shard_map/ppermute | solution.py:406
  39.8 1.7 %collective-permute-done.9 = f32[2,384,512]{2,1,0:T(8,128)S(1)} collective-permute-done((f32[2,384,512]{2,1,0:T(8,128)S(1)}, f32[2,384,512]{2,1,0:T(8,128)S(1)}, u32[]{:S(2)}, u32[]{:S(2)}) %collective-permute-start.9) | collective-permute-done | bytes 1572896 | tf_op jit(solution)/shard_map/ppermute | solution.py:382
  41.7 1.6 %collective-permute-start.10 = (f16[384,512]{1,0:T(8,128)(2,1)S(1)}, f16[384,512]{1,0:T(8,128)(2,1)S(1)}, u32[]{:S(2)}, u32[]{:S(2)}) collective-permute-start(f16[384,512]{1,0:T(8,128)(2,1)S(1)} %fusion.2), channel_id=1, source_target_pairs={{0,2},{1,3},{2,0},{3,1},{4,6},{5,7},{6,4},{7,5},{8,10},{9,11},{10,... | collective-permute-start | bytes 1179656 | tf_op jit(solution)/shard_map/ppermute | solution.py:406
  43.4 0.9 %finish.2 = (f32[2,3,128,512]{3,2,1,0:T(8,128)}, f32[2,4,128]{2,1,0:T(4,128)S(1)}) custom-call(f32[256,512]{1,0:T(8,128)S(1)} %fusion.6.total_ref, f32[2,128,128]{2,1,0:T(8,128)S(1)} %get-tuple-element.46.row_ref, f32[2,3,4,128]{3,2,1,0:T(4,128)S(1)} %get-tuple-element.57.col_ref), custom_call_target="tpu_custom_call" | custom-call | tf_op jit(solution)/shard_map/finish/pallas_call | solution.py:254
  44.4 0.8 %finish.3 = (f32[2,3,128,512]{3,2,1,0:T(8,128)}, f32[1,4,128]{2,1,0:T(4,128)S(1)}) custom-call(f32[128,512]{1,0:T(8,128)S(1)} %fusion.11.total_ref, f32[2,128,128]{2,1,0:T(8,128)S(1)} %get-tuple-element.46.row_ref, f32[2,3,4,128]{3,2,1,0:T(4,128)S(1)} %get-tuple-element.57.col_ref, ...), custom_call_target="tpu_custom_call", output_to_operand_aliasing={{0}: (3, {})} | custom-call | tf_op jit(solution)/shard_map/finish/pallas_call | solution.py:254
  45.1 7.9 %collective-permute-done.10 = f16[384,512]{1,0:T(8,128)(2,1)S(1)} collective-permute-done((f16[384,512]{1,0:T(8,128)(2,1)S(1)}, f16[384,512]{1,0:T(8,128)(2,1)S(1)}, u32[]{:S(2)}, u32[]{:S(2)}) %collective-permute-start.10) | collective-permute-done | bytes 393248 | tf_op jit(solution)/shard_map/ppermute | solution.py:406
  54.0 1.1 %collective-permute-start.13 = (f32[2,3,4,4]{3,2,1,0:T(4,128)S(1)}, f32[2,3,4,4]{3,2,1,0:T(4,128)S(1)}, u32[]{:S(2)}, u32[]{:S(2)}) collective-permute-start(f32[2,3,4,4]{3,2,1,0:T(4,128)S(1)} %get-tuple-element.65.refs_0_), channel_id=1, source_target_pairs={{0,2},{1,3},{2,0},{3,1},{4,6},{5,7},{6,4},{7,5},{8,10},{9,11},{10,... | collective-permute-start | bytes 1160 | tf_op jit(solution)/shard_map/ppermute | solution.py:417
  55.4 0.9 %put.1 = f32[2,3,128,512]{3,2,1,0:T(8,128)} custom-call(f32[3,128,512]{2,1,0:T(8,128)S(1)} %get-tuple-element.63.values_ref, f32[2,3,128,512]{3,2,1,0:T(8,128)} %get-tuple-element.64._), custom_call_target="tpu_custom_call", output_to_operand_aliasing={{}: (1, {})} | custom-call | tf_op jit(solution)/shard_map/put/pallas_call | solution.py:305
  56.7 1.0 %collective-permute-done.13.refs_2_ = f32[2,3,4,4]{3,2,1,0:T(4,128)S(1)} collective-permute-done((f32[2,3,4,4]{3,2,1,0:T(4,128)S(1)}, f32[2,3,4,4]{3,2,1,0:T(4,128)S(1)}, u32[]{:S(2)}, u32[]{:S(2)}) %collective-permute-start.13) | collective-permute-done | bytes 416 | tf_op jit(solution)/shard_map/ppermute | solution.py:417
  57.7 0.6 %last.1 = f32[2,3,4,4]{3,2,1,0:T(4,128)} custom-call(f32[2,3,4,4]{3,2,1,0:T(4,128)S(1)} %get-tuple-element.65.refs_0_, f32[2,3,4,4]{3,2,1,0:T(4,128)S(1)} %collective-permute-done.12.refs_1_, f32[2,3,4,4]{3,2,1,0:T(4,128)S(1)} %collective-permute-done.13.refs_2_, f32[2,3,4,4]{3,2,1,0:T(4,128)S(1)} %collective-permute-done.14.refs_3_), custom_call_target="tpu_custom_call" | custom-call | tf_op jit(solution)/shard_map/last/pallas_call | solution.py:320
  (44 shorter events, 4.1 us)
Async XLA Ops:
  0.6 1.1 %copy-start = (bf16[80,8,4,128]{3,2,1,0:T(4,128)(2,1)S(1)}, bf16[80,8,4,128]{3,2,1,0:T(4,128)(2,1)}, u32[]{:S(2)}) copy-start(bf16[80,8,4,128]{3,2,1,0:T(4,128)(2,1)} %param.5) | copy-start | bytes 1966084
  2.6 13.6 %collective-permute-start.1 = (bf16[656,128]{1,0:T(8,128)(2,1)S(1)}, bf16[656,128]{1,0:T(8,128)(2,1)S(1)}, u32[]{:S(2)}, u32[]{:S(2)}) collective-permute-start(bf16[656,128]{1,0:T(8,128)(2,1)S(1)} %get-tuple-element.36), channel_id=1, source_target_pairs={{0,8},{4,12},{8,0},{12,4},{1,9},{5,13},{9,1},{13,5},{2,10},{6,14},... | collective-permute-start | bytes 503816 | tf_op jit(solution)/shard_map/ppermute | solution.py:375
  6.8 9.5 %collective-permute-start = (bf16[656,128]{1,0:T(8,128)(2,1)S(1)}, bf16[656,128]{1,0:T(8,128)(2,1)S(1)}, u32[]{:S(2)}, u32[]{:S(2)}) collective-permute-start(bf16[656,128]{1,0:T(8,128)(2,1)S(1)} %get-tuple-element.49.refs_4_), channel_id=1, source_target_pairs={{0,4},{4,0},{8,12},{12,8},{1,5},{5,1},{9,13},{13,9},{2,6},{6,2},{1... | collective-permute-start | bytes 503816 | tf_op jit(solution)/shard_map/ppermute | solution.py:375
  8.3 11.1 %collective-permute-start.2 = (bf16[656,128]{1,0:T(8,128)(2,1)S(1)}, bf16[656,128]{1,0:T(8,128)(2,1)S(1)}, u32[]{:S(2)}, u32[]{:S(2)}) collective-permute-start(bf16[656,128]{1,0:T(8,128)(2,1)S(1)} %get-tuple-element.37.refs_5_), channel_id=1, source_target_pairs={{0,12},{4,8},{8,4},{12,0},{1,13},{5,9},{9,5},{13,1},{2,14},{6,10},... | collective-permute-start | bytes 503816 | tf_op jit(solution)/shard_map/ppermute | solution.py:375
  19.5 6.6 %copy-start.2 = (s32[2,3]{1,0:T(2,128)S(1)}, s32[2,3]{1,0:T(2,128)}, u32[]{:S(2)}) copy-start(s32[2,3]{1,0:T(2,128)} %partners_ref.5) | copy-start | bytes 76
  19.6 6.6 %copy-start.3 = (s32[8,128]{1,0:T(8,128)S(1)}, s32[8,128]{1,0:T(8,128)}, u32[]{:S(2)}) copy-start(s32[8,128]{1,0:T(8,128)} %domains_ref.1) | copy-start | bytes 12292
  19.6 6.6 %copy-start.4 = (f32[1024]{0:T(1024)S(1)}, f32[1024]{0:T(1024)}, u32[]{:S(2)}) copy-start(f32[1024]{0:T(1024)} %param.9) | copy-start | bytes 12292
  19.6 6.6 %copy-start.5 = (f32[8,4]{0,1:T(4,128)S(1)}, f32[8,4]{0,1:T(4,128)}, u32[]{:S(2)}) copy-start(f32[8,4]{0,1:T(4,128)} %param.8) | copy-start | bytes 388
  20.4 3.4 %collective-permute-start.3 = (f32[2,264,512]{2,1,0:T(8,128)S(1)}, f32[2,264,512]{2,1,0:T(8,128)S(1)}, u32[]{:S(2)}, u32[]{:S(2)}) collective-permute-start(f32[2,264,512]{2,1,0:T(8,128)S(1)} %get-tuple-element.42), channel_id=1, source_target_pairs={{0,1},{1,0},{2,3},{3,2},{4,5},{5,4},{6,7},{7,6},{8,9},{9,8},{10,11... | collective-permute-start | bytes 3244040 | tf_op jit(solution)/shard_map/ppermute | solution.py:382
  20.4 15.0 %collective-permute-start.6 = (bf16[1920,128]{1,0:T(8,128)(2,1)S(1)}, bf16[1920,128]{1,0:T(8,128)(2,1)S(1)}, u32[]{:S(2)}, u32[]{:S(2)}) collective-permute-start(bf16[1920,128]{1,0:T(8,128)(2,1)S(1)} %get-tuple-element.38), channel_id=1, source_target_pairs={{0,4},{1,5},{2,6},{3,7},{4,0},{5,1},{6,2},{7,3},{8,12},{9,13},{10,... | collective-permute-start | bytes 1474568 | tf_op jit(solution)/shard_map/ppermute | solution.py:378
  23.6 11.8 %collective-permute-start.7 = (bf16[1920,128]{1,0:T(8,128)(2,1)S(1)}, bf16[1920,128]{1,0:T(8,128)(2,1)S(1)}, u32[]{:S(2)}, u32[]{:S(2)}) collective-permute-start(bf16[1920,128]{1,0:T(8,128)(2,1)S(1)} %get-tuple-element.39), channel_id=1, source_target_pairs={{0,1},{1,0},{2,3},{3,2},{4,8},{5,9},{6,10},{7,11},{8,4},{9,5},{10,... | collective-permute-start | bytes 1474568 | tf_op jit(solution)/shard_map/ppermute | solution.py:378
  24.0 9.1 %collective-permute-start.4 = (f16[256,512]{1,0:T(8,128)(2,1)S(1)}, f16[256,512]{1,0:T(8,128)(2,1)S(1)}, u32[]{:S(2)}, u32[]{:S(2)}) collective-permute-start(f16[256,512]{1,0:T(8,128)(2,1)S(1)} %fusion.9), channel_id=1, source_target_pairs={{0,2},{1,3},{2,0},{3,1},{4,6},{5,7},{6,4},{7,5},{8,10},{9,11},{10,... | collective-permute-start | bytes 786440 | tf_op jit(solution)/shard_map/ppermute | solution.py:387
  25.6 7.4 %collective-permute-start.5 = (f32[8,512]{1,0:T(8,128)S(1)}, f32[8,512]{1,0:T(8,128)S(1)}, u32[]{:S(2)}, u32[]{:S(2)}) collective-permute-start(f32[8,512]{1,0:T(8,128)S(1)} %get-tuple-element.45), channel_id=1, source_target_pairs={{0,2},{1,3},{2,0},{3,1},{4,6},{5,7},{6,4},{7,5},{8,10},{9,11},{10,... | collective-permute-start | bytes 49160 | tf_op jit(solution)/shard_map/ppermute | solution.py:393
  33.1 5.2 %copy-start.1 = (f32[8,512]{1,0:T(8,128)}, f32[8,512]{1,0:T(8,128)S(1)}, u32[]{:S(2)}) copy-start(f32[8,512]{1,0:T(8,128)S(1)} %scale_up.1) | copy-start | bytes 49156
  36.0 2.0 %collective-permute-start.8 = (f32[2,128,512]{2,1,0:T(8,128)S(1)}, f32[2,128,512]{2,1,0:T(8,128)S(1)}, u32[]{:S(2)}, u32[]{:S(2)}) collective-permute-start(f32[2,128,512]{2,1,0:T(8,128)S(1)} %get-tuple-element.53), channel_id=1, source_target_pairs={{0,1},{1,0},{2,3},{3,2},{4,5},{5,4},{6,7},{7,6},{8,9},{9,8},{10,11... | collective-permute-start | bytes 1572872 | tf_op jit(solution)/shard_map/ppermute | solution.py:382
  38.0 3.5 %collective-permute-start.9 = (f32[2,384,512]{2,1,0:T(8,128)S(1)}, f32[2,384,512]{2,1,0:T(8,128)S(1)}, u32[]{:S(2)}, u32[]{:S(2)}) collective-permute-start(f32[2,384,512]{2,1,0:T(8,128)S(1)} %get-tuple-element.54), channel_id=1, source_target_pairs={{0,1},{1,0},{2,3},{3,2},{4,5},{5,4},{6,7},{7,6},{8,9},{9,8},{10,11... | collective-permute-start | bytes 4718600 | tf_op jit(solution)/shard_map/ppermute | solution.py:382
  38.3 5.0 %slice-start = ((f32[8,512]{1,0:T(8,128)}), f32[1,512]{1,0:T(1,128)S(1)}, s32[]{:S(2)}) async-start(f32[8,512]{1,0:T(8,128)} %copy-done.1), calls=%async_computation | async-start | bytes 4096 | tf_op jit(solution)/shard_map/slice | solution.py:412
  38.3 6.0 %collective-permute-start.11 = (f16[128,512]{1,0:T(8,128)(2,1)S(1)}, f16[128,512]{1,0:T(8,128)(2,1)S(1)}, u32[]{:S(2)}, u32[]{:S(2)}) collective-permute-start(f16[128,512]{1,0:T(8,128)(2,1)S(1)} %fusion.14), channel_id=1, source_target_pairs={{0,2},{1,3},{2,0},{3,1},{4,6},{5,7},{6,4},{7,5},{8,10},{9,11},{10,... | collective-permute-start | bytes 393224 | tf_op jit(solution)/shard_map/ppermute | solution.py:406
  41.7 2.6 %slice-start.1 = ((f32[8,512]{1,0:T(8,128)}), f32[1,512]{1,0:T(1,128)S(1)}, s32[]{:S(2)}) async-start(f32[8,512]{1,0:T(8,128)} %copy-done.1), calls=%async_computation.1 | async-start | bytes 4096 | tf_op jit(solution)/shard_map/slice | solution.py:412
  41.7 11.3 %collective-permute-start.10 = (f16[384,512]{1,0:T(8,128)(2,1)S(1)}, f16[384,512]{1,0:T(8,128)(2,1)S(1)}, u32[]{:S(2)}, u32[]{:S(2)}) collective-permute-start(f16[384,512]{1,0:T(8,128)(2,1)S(1)} %fusion.2), channel_id=1, source_target_pairs={{0,2},{1,3},{2,0},{3,1},{4,6},{5,7},{6,4},{7,5},{8,10},{9,11},{10,... | collective-permute-start | bytes 1179656 | tf_op jit(solution)/shard_map/ppermute | solution.py:406
  44.3 8.7 %slice-start.2 = ((f32[8,512]{1,0:T(8,128)}), f32[1,512]{1,0:T(1,128)S(1)}, s32[]{:S(2)}) async-start(f32[8,512]{1,0:T(8,128)} %copy-done.1), calls=%async_computation.2 | async-start | bytes 4096 | tf_op jit(solution)/shard_map/slice | solution.py:412
  53.5 3.2 %collective-permute-start.14 = (f32[2,3,4,4]{3,2,1,0:T(4,128)S(1)}, f32[2,3,4,4]{3,2,1,0:T(4,128)S(1)}, u32[]{:S(2)}, u32[]{:S(2)}) collective-permute-start(f32[2,3,4,4]{3,2,1,0:T(4,128)S(1)} %get-tuple-element.65.refs_0_), channel_id=1, source_target_pairs={{0,3},{1,2},{2,1},{3,0},{4,7},{5,6},{6,5},{7,4},{8,11},{9,10},{10,... | collective-permute-start | bytes 1160 | tf_op jit(solution)/shard_map/ppermute | solution.py:417
  54.0 3.7 %collective-permute-start.13 = (f32[2,3,4,4]{3,2,1,0:T(4,128)S(1)}, f32[2,3,4,4]{3,2,1,0:T(4,128)S(1)}, u32[]{:S(2)}, u32[]{:S(2)}) collective-permute-start(f32[2,3,4,4]{3,2,1,0:T(4,128)S(1)} %get-tuple-element.65.refs_0_), channel_id=1, source_target_pairs={{0,2},{1,3},{2,0},{3,1},{4,6},{5,7},{6,4},{7,5},{8,10},{9,11},{10,... | collective-permute-start | bytes 1160 | tf_op jit(solution)/shard_map/ppermute | solution.py:417
  55.1 2.6 %collective-permute-start.12 = (f32[2,3,4,4]{3,2,1,0:T(4,128)S(1)}, f32[2,3,4,4]{3,2,1,0:T(4,128)S(1)}, u32[]{:S(2)}, u32[]{:S(2)}) collective-permute-start(f32[2,3,4,4]{3,2,1,0:T(4,128)S(1)} %get-tuple-element.65.refs_0_), channel_id=1, source_target_pairs={{0,1},{1,0},{2,3},{3,2},{4,5},{5,4},{6,7},{7,6},{8,9},{9,8},{10,11... | collective-permute-start | bytes 1160 | tf_op jit(solution)/shard_map/ppermute | solution.py:417

commit v5 on v3

--- a/solution.py
+++ b/solution.py
@@ -35,21 +35,32 @@
 
 def pack(raw, count):
     depth, blocks, orbitals, domain = raw.shape
-    rows, parts = blocks * orbitals, 4
-    part = depth * rows // parts
+    rows = blocks * orbitals
+    group = rows // 2
 
     def kernel(raw_ref, *refs):
-        outs, wide = refs[:count], refs[-1]
+        outs, (narrow, wide, sems) = refs[:count], refs[count:]
         z = lax.axis_index("aux")
-        wide[...] = raw_ref[...].astype(F32)
-        peak = jnp.max(jnp.abs(wide[...]).reshape(-1, PEAK_ROWS, domain), axis=0)
-        for k in range(count):
-            out = outs[(k + 1) % count]
-            block = 2 * jnp.bitwise_xor(z, (k + 1) % count)
-            for r in range(2):
-                for i in range(orbitals):
-                    at = pl.ds((block + r) * orbitals + i, depth, stride=rows)
-                    out[panel_at(depth, i, r), :] = wide[at, :].astype(BF16)
+        copies = []
+        for n in range(2):
+            start = pl.multiple_of((lax.div(z, 2) ^ (1 - n)) * group, 16)
+            part = raw_ref.at[:, pl.ds(start, group), :]
+            copies.append(pltpu.make_async_copy(part, narrow.at[n], sems.at[n]))
+            copies[-1].start()
+        peak = jnp.zeros((PEAK_ROWS, domain), F32)
+        for n, ks in enumerate(((2, 3), (0, 1))):
+            copies[n].wait()
+            values = narrow[n].astype(F32).reshape(depth * group, domain)
+            wide[n] = values
+            values = jnp.max(jnp.abs(values).reshape(-1, PEAK_ROWS, domain), axis=0)
+            peak = jnp.maximum(peak, values)
+            for k in ks:
+                first = lax.rem(z ^ k, 2) * 2 * orbitals
+                for r in range(2):
+                    for i in range(orbitals):
+                        at = pl.ds(first + r * orbitals + i, depth, stride=group)
+                        outs[k][panel_at(depth, i, r), :] = wide[n, at, :].astype(BF16)
+        for out in outs:
             out[2 * orbitals * depth :, :] = peak.astype(BF16)
 
     one_set = shape(2 * orbitals * depth + PEAK_ROWS, domain, dtype=BF16)
@@ -57,12 +68,14 @@
         kernel,
         "pack",
         out_shape=[one_set] * count,
-        in_specs=[VMEM],
+        in_specs=[pl.BlockSpec(memory_space=pltpu.HBM)],
         out_specs=[VMEM] * count,
         scratch_shapes=[
-            pltpu.VMEM((depth * rows, domain), F32),
+            pltpu.VMEM((2, depth, group, domain), BF16),
+            pltpu.VMEM((2, depth * group, domain), F32),
+            pltpu.SemaphoreType.DMA((2,)),
         ],
-    )(raw.reshape(depth * rows, domain))
+    )(pltpu.with_memory_space_constraint(raw.reshape(depth, rows, domain), pltpu.HBM))
 
 
 def relay(own, rows):
@@ -97,12 +110,10 @@
     return jnp.concatenate(columns, axis=1)
 
 
-def store_sums(sums, at, mine, other, give):
+def store_sums(sums, at, *outs):
     domain = sums.shape[0] // 4
-    mine[at] = sums[:domain]
-    other[at] = sums[domain : 2 * domain]
-    give[0, at] = sums[2 * domain : 3 * domain]
-    give[1, at] = sums[3 * domain :]
+    for n, out in enumerate(outs):
+        out[at] = sums[n * domain : (n + 1) * domain]
 
 
 def own_pairs(own, orbitals):
@@ -128,7 +139,7 @@
                 axis=1,
             )
             at = slice(r * domain, (r + 1) * domain)
-            store_sums(product(left_rows(own_refs, depth, r), right), at, mine, other, give)
+            store_sums(product(left_rows(own_refs, depth, r), right), at, mine, other, give.at[0], give.at[1])
 
     return call(
         kernel,
@@ -151,41 +162,50 @@
 
     def kernel(partners_ref, *refs):
         own_refs, here_refs, side_refs = refs[:count], refs[count : count + 2], refs[count + 2 :][:2]
+        outs = refs[count + 4 :]
         z = lax.axis_index("aux")
-        even = lax.rem(z, 2) == 0
-
-        def panels(w, j, slot):
-            from_first = (w > 3) == even
-            at = (2 * j + lax.rem(w, 2)) * depth
+
+        def flag(value):
+            return jnp.broadcast_to(value, (depth, domain))
+
+        def panels(r, j, slot, w):
+            from_first = flag(jnp.where(w > 3, 1, 0) != lax.rem(z, 2))
+            is_own, is_second = flag((w == 2) | (w == 3)), flag(lax.rem(w, 2) == 1)
+
+            def either(first, second, start):
+                rows_at = slice(start, start + depth)
+                return jnp.where(from_first, first[rows_at, :], second[rows_at, :])
+
             found = []
             for k in range(count):
-                refs, start = (here_refs, at) if k == 0 else (side_refs, at + (k - 1) * rows)
-                rows_at = pl.ds(pl.multiple_of(start, 16), depth)
-                panel = jnp.where(from_first, refs[0][rows_at, :], refs[1][rows_at, :])
-                if slot > 1:
-                    own_at = pl.ds(pl.multiple_of(at, 16), depth)
-                    panel = jnp.where((w == 2) | (w == 3), own_refs[k][own_at, :], panel)
+                refs, start = (here_refs, 0) if k == 0 else (side_refs, (k - 1) * rows)
+                start += 2 * j * depth
+                if slot == 1:
+                    panel = either(*refs, start + r * depth)
+                else:
+                    panel = jnp.where(is_second, either(*refs, start + depth), either(*refs, start))
+                    mine = [own_refs[k][panel_at(depth, j, block), :] for block in range(2)]
+                    panel = jnp.where(is_own, jnp.where(is_second, mine[1], mine[0]), panel)
                 found.append(panel)
             return jnp.concatenate(found, axis=0)
 
         for n, tiles in enumerate(groups):
             for t, (r, slot) in enumerate(tiles):
-                w = partners_ref[r, slot] - 2 * z + 2
-                right = jnp.concatenate([panels(w, j, slot) for j in range(orbitals)], axis=1)
+                w = partners_ref[r : r + 1, slot : slot + 1] - 2 * z + 2
+                right = jnp.concatenate([panels(r, j, slot, w) for j in range(orbitals)], axis=1)
                 sums = product(left_rows(own_refs, depth, r), right)
                 at = slice(t * domain, (t + 1) * domain)
-                store_sums(sums, at, *refs[count + 4 + 3 * n :][:3])
-
-    outs = []
+                store_sums(sums, at, *outs[4 * n : 4 * n + 4])
+
+    shapes = []
     for tiles in groups:
-        height = len(tiles) * domain
-        outs += [shape(height, wide), shape(height, wide), shape(2, height, wide)]
+        shapes += [shape(len(tiles) * domain, wide)] * 4
     return call(
         kernel,
         "near",
-        out_shape=outs,
-        in_specs=[SMEM] + [VMEM] * (count + 4),
-        out_specs=[VMEM] * len(outs),
+        out_shape=shapes,
+        in_specs=[VMEM] * (count + 5),
+        out_specs=[VMEM] * len(shapes),
     )(partners, *own, *here, *sides)
 
 
@@ -372,38 +392,34 @@
     near = [lax.ppermute(m, ("aux", "pair"), side) for m, side in zip(messages, sides)]
     own[0] = after(own[0], *messages)
 
-    def across_cores(mine, other, give):
-        got = lax.ppermute(give, "pair", swap)
-        height = mine.shape[0]
-        return mine, got, other + got[1, :height]
-
-    def across_chips(other):
-        return lax.ppermute((other * to_half[:1]).astype(F16), "pair", cross)
-
-    *sums, peak = own_pairs(own, orbitals)
-    mine, got, other = across_cores(*sums)
+    def across(sums, axis_pairs):
+        return lax.ppermute(sums, "pair", axis_pairs)
+
+    mine, other, give, peak = own_pairs(own, orbitals)
+    got = across(give, swap)
     top, to_half = scale_down(peak, got, 2 * count * depth)
-    parts = [(mine, got, across_chips(other))]
-    from_half = scale_up(lax.ppermute(top, "pair", cross), 2 * count * depth)
+    half = ((other + got[1, : 2 * domain]) * to_half[:1]).astype(F16)
+    parts = [(mine, got[0, : 2 * domain], across(half, cross))]
+    from_half = scale_up(across(top, cross), 2 * count * depth)
     here[0] = after(here[0], parts[0][2], from_half, row_vals)
 
     groups = [[(0, 0), (1, 0)], *GROUPS[0], *GROUPS[1]]
     sums = near_pairs(partners, own, here, near, orbitals, GROUPS[0])
     here[0] = after(here[0], sums[0])
     sums += near_pairs(partners, own, here, near, orbitals, GROUPS[1])
-    for n in range(0, len(sums), 3):
-        mine, other, give = sums[n : n + 3]
+    for n in range(0, len(sums), 4):
+        mine, other, give, give_on = sums[n : n + 4]
         if n:
-            give = after(give, half)
-        mine, got, other = across_cores(mine, other, give)
-        half = (other * to_half[:1]).astype(F16)
-        parts.append((mine, got, lax.ppermute(half, "pair", cross)))
+            give_on = after(give_on, half)
+        half = ((other + across(give_on, swap)) * to_half[:1]).astype(F16)
+        got = across(give, swap)
+        parts.append((mine, got, across(half, cross)))
 
     out = partners.shape + (domain, wide)
     amps, shares = [], []
-    for at, (mine, got, across) in enumerate(parts):
+    for at, (mine, got, arrived) in enumerate(parts):
         back = after(from_half, shares[-1]) if at else from_half
-        total = mine + got[0, : mine.shape[0]] + across.astype(F32) * back[:1]
+        total = mine + got + arrived.astype(F32) * back[:1]
         if at < len(parts) - 1:
             *amps, share = finish(total, row_vals, col_vals, groups[at], amps, out)
             shares.append(share)

time: 59 us -> 57.4 us (0.973)
  local copies, waits for them, and re-layouts: 1.13 us -> 0.04 us
  waiting for transfers between devices: 30.7 us -> 29.9 us
    unnamed x12 -> x10, local copies, waits for them, and re-layouts: 1.11 us -> 0.02 us
    ppermute x7 -> x9, waiting for transfers between devices: 15.9 us -> 15.2 us  [across(): return lax.ppermute(sums, 'pair', axis_pairs)]
    ppermute x7 -> x9, starting transfers between devices: 5.57 us -> 6.13 us  [across(): return lax.ppermute(sums, 'pair', axis_pairs)]
  transfers between devices with their start and end apart: 15 -> 17, of which waited for: 9 -> 9; matrix products, arithmetic and copies ran while one was open for 1% -> 1% of each run, Pallas kernels for 9% -> 9%
where the time goes in v5:
time: 57.4 us; the launch traced here: 57.3 us
  waiting for transfers between devices  29.9 us (52%)
  starting transfers between devices  17 us (30%)
  Pallas kernels  8.68 us (15%)
  between operations  0.82 us (1%)
  other arithmetic  0.78 us (1%)
    ppermute x9, waiting for transfers between devices, across(): return lax.ppermute(sums, 'pair', axis_pairs)  15.2 us
    ppermute x3, waiting for transfers between devices, fast(): own.append(lax.ppermute(send, 'aux', [(i, i ^ k) for i in range(count)]))  11.1 us
    ppermute x9, starting transfers between devices, across(): return lax.ppermute(sums, 'pair', axis_pairs)  6.13 us
    ppermute x3, starting transfers between devices, fast(): own.append(lax.ppermute(send, 'aux', [(i, i ^ k) for i in range(count)]))  5.67 us
    ppermute x2, starting transfers between devices, fast(): lax.ppermute(m, ('aux', 'pair'), side)  3.35 us
    ppermute x2, waiting for transfers between devices, fast(): lax.ppermute(m, ('aux', 'pair'), side)  2.24 us
    pallas_call x2, Pallas kernels, near_pairs(): call(kernel, 'near', out_shape=shapes, in_specs=[VMEM] * (count + 5), out...  1.94 us
    ppermute x3, starting transfers between devices, fast(): others = [lax.ppermute(share, 'pair', to) for to in (swap, cross, both)]  1.89 us
  transfers between devices with their start and end apart: 17, of which 9 were waited for; matrix products, arithmetic and copies ran while one was open for 1% of the time, Pallas kernels for 9%

profile of v5, /device:TPU:0, one launch (start us, length us, event | category | flops | bytes accessed | tf_op | source)
XLA Modules:
  0.0 57.3 jit_solution(6517841785689672270)
XLA Ops:
  0.6 1.5 %pack.1 = (bf16[656,128]{1,0:T(8,128)(2,1)S(1)}, bf16[656,128]{1,0:T(8,128)(2,1)S(1)}, bf16[656,128]{1,0:T(8,128)(2,1)S(1)}, bf16[656,128]{1,0:T(8,128)(2,1)S(1)}) custom-call(bf16[80,32,128]{2,1,0:T(8,128)(2,1)} %bitcast.26), custom_call_target="tpu_custom_call" | custom-call | tf_op jit(solution)/shard_map/pack/pallas_call | solution.py:67
  2.1 4.1 %collective-permute-start.1 = (bf16[656,128]{1,0:T(8,128)(2,1)S(1)}, bf16[656,128]{1,0:T(8,128)(2,1)S(1)}, u32[]{:S(2)}, u32[]{:S(2)}) collective-permute-start(bf16[656,128]{1,0:T(8,128)(2,1)S(1)} %get-tuple-element.38), channel_id=1, source_target_pairs={{0,8},{4,12},{8,0},{12,4},{1,9},{5,13},{9,1},{13,5},{2,10},{6,14},... | collective-permute-start | bytes 503816 | tf_op jit(solution)/shard_map/ppermute | solution.py:389
  6.2 1.6 %collective-permute-start = (bf16[656,128]{1,0:T(8,128)(2,1)S(1)}, bf16[656,128]{1,0:T(8,128)(2,1)S(1)}, u32[]{:S(2)}, u32[]{:S(2)}) collective-permute-start(bf16[656,128]{1,0:T(8,128)(2,1)S(1)} %get-tuple-element.51.refs_4_), channel_id=1, source_target_pairs={{0,4},{4,0},{8,12},{12,8},{1,5},{5,1},{9,13},{13,9},{2,6},{6,2},{1... | collective-permute-start | bytes 503816 | tf_op jit(solution)/shard_map/ppermute | solution.py:389
  7.8 8.0 %collective-permute-done.1.refs_2_ = bf16[656,128]{1,0:T(8,128)(2,1)S(1)} collective-permute-done((bf16[656,128]{1,0:T(8,128)(2,1)S(1)}, bf16[656,128]{1,0:T(8,128)(2,1)S(1)}, u32[]{:S(2)}, u32[]{:S(2)}) %collective-permute-start.1) | collective-permute-done | bytes 167968 | tf_op jit(solution)/shard_map/ppermute | solution.py:389
  15.8 3.1 %collective-permute-done.2.refs_3_ = bf16[656,128]{1,0:T(8,128)(2,1)S(1)} collective-permute-done((bf16[656,128]{1,0:T(8,128)(2,1)S(1)}, bf16[656,128]{1,0:T(8,128)(2,1)S(1)}, u32[]{:S(2)}, u32[]{:S(2)}) %collective-permute-start.2) | collective-permute-done | bytes 167968 | tf_op jit(solution)/shard_map/ppermute | solution.py:389
  19.0 0.8 %own.1 = (f32[256,512]{1,0:T(8,128)S(1)}, f32[256,512]{1,0:T(8,128)S(1)}, f32[2,264,512]{2,1,0:T(8,128)S(1)}, f32[8,512]{1,0:T(8,128)S(1)}) custom-call(bf16[656,128]{1,0:T(8,128)(2,1)S(1)} %get-tuple-element.42.refs_0_, bf16[656,128]{1,0:T(8,128)(2,1)S(1)} %collective-permute-done.refs_1_, bf16[656,128]{1,0:T(8,128)(2,1)S(1)} %collective-permute-done.1.refs_2_, ...), custom_call_target="tpu_custom_call" | custom-call | tf_op jit(solution)/shard_map/own/pallas_call | solution.py:144
  19.9 3.2 %collective-permute-start.6 = (bf16[1920,128]{1,0:T(8,128)(2,1)S(1)}, bf16[1920,128]{1,0:T(8,128)(2,1)S(1)}, u32[]{:S(2)}, u32[]{:S(2)}) collective-permute-start(bf16[1920,128]{1,0:T(8,128)(2,1)S(1)} %get-tuple-element.40), channel_id=1, source_target_pairs={{0,4},{1,5},{2,6},{3,7},{4,0},{5,1},{6,2},{7,3},{8,12},{9,13},{10,... | collective-permute-start | bytes 1474568 | tf_op jit(solution)/shard_map/ppermute | solution.py:392
  23.5 1.6 %collective-permute-start.4 = (f16[256,512]{1,0:T(8,128)(2,1)S(1)}, f16[256,512]{1,0:T(8,128)(2,1)S(1)}, u32[]{:S(2)}, u32[]{:S(2)}) collective-permute-start(f16[256,512]{1,0:T(8,128)(2,1)S(1)} %fusion.4), channel_id=1, source_target_pairs={{0,2},{1,3},{2,0},{3,1},{4,6},{5,7},{6,4},{7,5},{8,10},{9,11},{10,... | collective-permute-start | bytes 786440 | tf_op jit(solution)/shard_map/ppermute | solution.py:396
  25.1 0.5 collective-permute-start.5
  25.6 0.8 %energies.1 = (f32[2,128,128]{2,1,0:T(8,128)S(1)}, f32[2,3,4,128]{3,2,1,0:T(4,128)S(1)}) custom-call(s32[2,3]{1,0:T(2,128)S(1)} %copy-done.1, f32[4,8]{1,0:T(4,128)S(1)} %bitcast.25, s32[8,128]{1,0:T(8,128)S(1)} %copy-done.2, f32[8,128]{1,0:T(8,128)S(1)} %bitcast.24), custom_call_target="tpu_custom_call" | custom-call | tf_op jit(solution)/shard_map/energies/pallas_call | solution.py:368
  26.4 6.1 %collective-permute-done.5.top_ref = f32[8,512]{1,0:T(8,128)S(1)} collective-permute-done((f32[8,512]{1,0:T(8,128)S(1)}, f32[8,512]{1,0:T(8,128)S(1)}, u32[]{:S(2)}, u32[]{:S(2)}) %collective-permute-start.5) | collective-permute-done | bytes 16416 | tf_op jit(solution)/shard_map/ppermute | solution.py:396
  32.6 2.2 %collective-permute-done.6.refs_6_ = bf16[1920,128]{1,0:T(8,128)(2,1)S(1)} collective-permute-done((bf16[1920,128]{1,0:T(8,128)(2,1)S(1)}, bf16[1920,128]{1,0:T(8,128)(2,1)S(1)}, u32[]{:S(2)}, u32[]{:S(2)}) %collective-permute-start.6) | collective-permute-done | bytes 491552 | tf_op jit(solution)/shard_map/ppermute | solution.py:392
  34.9 0.6 near.2
  35.5 1.4 %near.3 = (f32[384,512]{1,0:T(8,128)S(1)}, f32[384,512]{1,0:T(8,128)S(1)}, f32[384,512]{1,0:T(8,128)S(1)}, f32[384,512]{1,0:T(8,128)S(1)}) custom-call(s32[2,3]{1,0:T(2,128)S(1)} %copy-done.1, bf16[656,128]{1,0:T(8,128)(2,1)S(1)} %get-tuple-element.42.refs_0_, bf16[656,128]{1,0:T(8,128)(2,1)S(1)} %collective-permute-done.refs_1_, ...), custom_call_target="tpu_custom_call" | custom-call | tf_op jit(solution)/shard_map/near/pallas_call | solution.py:203
  38.0 1.5 %collective-permute-start.13 = (f16[128,512]{1,0:T(8,128)(2,1)S(1)}, f16[128,512]{1,0:T(8,128)(2,1)S(1)}, u32[]{:S(2)}, u32[]{:S(2)}) collective-permute-start(f16[128,512]{1,0:T(8,128)(2,1)S(1)} %multiply_convert_fusion.1), channel_id=1, source_target_pairs={{0,2},{1,3},{2,0},{3,1},{4,6},{5,7},{6,4},{7,5},{8,10},{9,11},{10,... | collective-permute-start | bytes 393224 | tf_op jit(solution)/shard_map/ppermute | solution.py:396
  39.7 1.5 %collective-permute-start.11 = (f16[384,512]{1,0:T(8,128)(2,1)S(1)}, f16[384,512]{1,0:T(8,128)(2,1)S(1)}, u32[]{:S(2)}, u32[]{:S(2)}) collective-permute-start(f16[384,512]{1,0:T(8,128)(2,1)S(1)} %multiply_convert_fusion), channel_id=1, source_target_pairs={{0,2},{1,3},{2,0},{3,1},{4,6},{5,7},{6,4},{7,5},{8,10},{9,11},{10,... | collective-permute-start | bytes 1179656 | tf_op jit(solution)/shard_map/ppermute | solution.py:396
  41.3 0.9 %finish.2 = (f32[2,3,128,512]{3,2,1,0:T(8,128)}, f32[2,4,128]{2,1,0:T(4,128)S(1)}) custom-call(f32[256,512]{1,0:T(8,128)S(1)} %fusion.1.total_ref, f32[2,128,128]{2,1,0:T(8,128)S(1)} %get-tuple-element.48.row_ref, f32[2,3,4,128]{3,2,1,0:T(4,128)S(1)} %get-tuple-element.61.col_ref), custom_call_target="tpu_custom_call" | custom-call | tf_op jit(solution)/shard_map/finish/pallas_call | solution.py:268
  42.2 2.2 %collective-permute-done.13 = f16[128,512]{1,0:T(8,128)(2,1)S(1)} collective-permute-done((f16[128,512]{1,0:T(8,128)(2,1)S(1)}, f16[128,512]{1,0:T(8,128)(2,1)S(1)}, u32[]{:S(2)}, u32[]{:S(2)}) %collective-permute-start.13) | collective-permute-done | bytes 131104 | tf_op jit(solution)/shard_map/ppermute | solution.py:396
  44.4 0.8 %finish.3 = (f32[2,3,128,512]{3,2,1,0:T(8,128)}, f32[1,4,128]{2,1,0:T(4,128)S(1)}) custom-call(f32[128,512]{1,0:T(8,128)S(1)} %multiply_add_fusion.1.total_ref, f32[2,128,128]{2,1,0:T(8,128)S(1)} %get-tuple-element.48.row_ref, f32[2,3,4,128]{3,2,1,0:T(4,128)S(1)} %get-tuple-element.61.col_ref, ...), custom_call_target="tpu_custom_call", output_to_operand_aliasing={{0}: (3, {})} | custom-call | tf_op jit(solution)/shard_map/finish/pallas_call | solution.py:268
  45.2 6.8 %collective-permute-done.11 = f16[384,512]{1,0:T(8,128)(2,1)S(1)} collective-permute-done((f16[384,512]{1,0:T(8,128)(2,1)S(1)}, f16[384,512]{1,0:T(8,128)(2,1)S(1)}, u32[]{:S(2)}, u32[]{:S(2)}) %collective-permute-start.11) | collective-permute-done | bytes 393248 | tf_op jit(solution)/shard_map/ppermute | solution.py:396
  53.0 1.1 %collective-permute-start.15 = (f32[2,3,4,4]{3,2,1,0:T(4,128)S(1)}, f32[2,3,4,4]{3,2,1,0:T(4,128)S(1)}, u32[]{:S(2)}, u32[]{:S(2)}) collective-permute-start(f32[2,3,4,4]{3,2,1,0:T(4,128)S(1)} %get-tuple-element.69.refs_0_), channel_id=1, source_target_pairs={{0,2},{1,3},{2,0},{3,1},{4,6},{5,7},{6,4},{7,5},{8,10},{9,11},{10,... | collective-permute-start | bytes 1160 | tf_op jit(solution)/shard_map/ppermute | solution.py:427
  54.4 0.9 %put.1 = f32[2,3,128,512]{3,2,1,0:T(8,128)} custom-call(f32[3,128,512]{2,1,0:T(8,128)S(1)} %get-tuple-element.67.values_ref, f32[2,3,128,512]{3,2,1,0:T(8,128)} %get-tuple-element.68._), custom_call_target="tpu_custom_call", output_to_operand_aliasing={{}: (1, {})} | custom-call | tf_op jit(solution)/shard_map/put/pallas_call | solution.py:319
  55.7 0.9 %collective-permute-done.15.refs_2_ = f32[2,3,4,4]{3,2,1,0:T(4,128)S(1)} collective-permute-done((f32[2,3,4,4]{3,2,1,0:T(4,128)S(1)}, f32[2,3,4,4]{3,2,1,0:T(4,128)S(1)}, u32[]{:S(2)}, u32[]{:S(2)}) %collective-permute-start.15) | collective-permute-done | bytes 416 | tf_op jit(solution)/shard_map/ppermute | solution.py:427
  56.7 0.6 %last.1 = f32[2,3,4,4]{3,2,1,0:T(4,128)} custom-call(f32[2,3,4,4]{3,2,1,0:T(4,128)S(1)} %get-tuple-element.69.refs_0_, f32[2,3,4,4]{3,2,1,0:T(4,128)S(1)} %collective-permute-done.14.refs_1_, f32[2,3,4,4]{3,2,1,0:T(4,128)S(1)} %collective-permute-done.15.refs_2_, f32[2,3,4,4]{3,2,1,0:T(4,128)S(1)} %collective-permute-done.16.refs_3_), custom_call_target="tpu_custom_call" | custom-call | tf_op jit(solution)/shard_map/last/pallas_call | solution.py:334
  (46 shorter events, 4.0 us)
Async XLA Ops:
  2.1 13.6 %collective-permute-start.1 = (bf16[656,128]{1,0:T(8,128)(2,1)S(1)}, bf16[656,128]{1,0:T(8,128)(2,1)S(1)}, u32[]{:S(2)}, u32[]{:S(2)}) collective-permute-start(bf16[656,128]{1,0:T(8,128)(2,1)S(1)} %get-tuple-element.38), channel_id=1, source_target_pairs={{0,8},{4,12},{8,0},{12,4},{1,9},{5,13},{9,1},{13,5},{2,10},{6,14},... | collective-permute-start | bytes 503816 | tf_op jit(solution)/shard_map/ppermute | solution.py:389
  6.2 9.5 %collective-permute-start = (bf16[656,128]{1,0:T(8,128)(2,1)S(1)}, bf16[656,128]{1,0:T(8,128)(2,1)S(1)}, u32[]{:S(2)}, u32[]{:S(2)}) collective-permute-start(bf16[656,128]{1,0:T(8,128)(2,1)S(1)} %get-tuple-element.51.refs_4_), channel_id=1, source_target_pairs={{0,4},{4,0},{8,12},{12,8},{1,5},{5,1},{9,13},{13,9},{2,6},{6,2},{1... | collective-permute-start | bytes 503816 | tf_op jit(solution)/shard_map/ppermute | solution.py:389
  7.8 11.1 %collective-permute-start.2 = (bf16[656,128]{1,0:T(8,128)(2,1)S(1)}, bf16[656,128]{1,0:T(8,128)(2,1)S(1)}, u32[]{:S(2)}, u32[]{:S(2)}) collective-permute-start(bf16[656,128]{1,0:T(8,128)(2,1)S(1)} %get-tuple-element.39.refs_5_), channel_id=1, source_target_pairs={{0,12},{4,8},{8,4},{12,0},{1,13},{5,9},{9,5},{13,1},{2,14},{6,10},... | collective-permute-start | bytes 503816 | tf_op jit(solution)/shard_map/ppermute | solution.py:389
  19.8 3.4 %collective-permute-start.3 = (f32[2,264,512]{2,1,0:T(8,128)S(1)}, f32[2,264,512]{2,1,0:T(8,128)S(1)}, u32[]{:S(2)}, u32[]{:S(2)}) collective-permute-start(f32[2,264,512]{2,1,0:T(8,128)S(1)} %get-tuple-element.44), channel_id=1, source_target_pairs={{0,1},{1,0},{2,3},{3,2},{4,5},{5,4},{6,7},{7,6},{8,9},{9,8},{10,11... | collective-permute-start | bytes 3244040 | tf_op jit(solution)/shard_map/ppermute | solution.py:396
  19.9 15.0 %collective-permute-start.6 = (bf16[1920,128]{1,0:T(8,128)(2,1)S(1)}, bf16[1920,128]{1,0:T(8,128)(2,1)S(1)}, u32[]{:S(2)}, u32[]{:S(2)}) collective-permute-start(bf16[1920,128]{1,0:T(8,128)(2,1)S(1)} %get-tuple-element.40), channel_id=1, source_target_pairs={{0,4},{1,5},{2,6},{3,7},{4,0},{5,1},{6,2},{7,3},{8,12},{9,13},{10,... | collective-permute-start | bytes 1474568 | tf_op jit(solution)/shard_map/ppermute | solution.py:392
  23.0 11.8 %collective-permute-start.7 = (bf16[1920,128]{1,0:T(8,128)(2,1)S(1)}, bf16[1920,128]{1,0:T(8,128)(2,1)S(1)}, u32[]{:S(2)}, u32[]{:S(2)}) collective-permute-start(bf16[1920,128]{1,0:T(8,128)(2,1)S(1)} %get-tuple-element.41), channel_id=1, source_target_pairs={{0,1},{1,0},{2,3},{3,2},{4,8},{5,9},{6,10},{7,11},{8,4},{9,5},{10,... | collective-permute-start | bytes 1474568 | tf_op jit(solution)/shard_map/ppermute | solution.py:392
  23.2 2.4 %copy-start.1 = (s32[2,3]{1,0:T(2,128)S(1)}, s32[2,3]{1,0:T(2,128)}, u32[]{:S(2)}) copy-start(s32[2,3]{1,0:T(2,128)} %partners_ref.5) | copy-start | bytes 76
  23.2 2.4 %copy-start.2 = (s32[8,128]{1,0:T(8,128)S(1)}, s32[8,128]{1,0:T(8,128)}, u32[]{:S(2)}) copy-start(s32[8,128]{1,0:T(8,128)} %domains_ref.1) | copy-start | bytes 12292
  23.2 2.4 %copy-start.3 = (f32[1024]{0:T(1024)S(1)}, f32[1024]{0:T(1024)}, u32[]{:S(2)}) copy-start(f32[1024]{0:T(1024)} %param.9) | copy-start | bytes 12292
  23.5 9.1 %collective-permute-start.4 = (f16[256,512]{1,0:T(8,128)(2,1)S(1)}, f16[256,512]{1,0:T(8,128)(2,1)S(1)}, u32[]{:S(2)}, u32[]{:S(2)}) collective-permute-start(f16[256,512]{1,0:T(8,128)(2,1)S(1)} %fusion.4), channel_id=1, source_target_pairs={{0,2},{1,3},{2,0},{3,1},{4,6},{5,7},{6,4},{7,5},{8,10},{9,11},{10,... | collective-permute-start | bytes 786440 | tf_op jit(solution)/shard_map/ppermute | solution.py:396
  25.1 7.4 %collective-permute-start.5 = (f32[8,512]{1,0:T(8,128)S(1)}, f32[8,512]{1,0:T(8,128)S(1)}, u32[]{:S(2)}, u32[]{:S(2)}) collective-permute-start(f32[8,512]{1,0:T(8,128)S(1)} %get-tuple-element.47), channel_id=1, source_target_pairs={{0,2},{1,3},{2,0},{3,1},{4,6},{5,7},{6,4},{7,5},{8,10},{9,11},{10,... | collective-permute-start | bytes 49160 | tf_op jit(solution)/shard_map/ppermute | solution.py:396
  32.6 4.9 %copy-start = (f32[8,512]{1,0:T(8,128)}, f32[8,512]{1,0:T(8,128)S(1)}, u32[]{:S(2)}) copy-start(f32[8,512]{1,0:T(8,128)S(1)} %scale_up.1) | copy-start | bytes 49156
  35.4 1.6 %collective-permute-start.9 = (f32[128,512]{1,0:T(8,128)S(1)}, f32[128,512]{1,0:T(8,128)S(1)}, u32[]{:S(2)}, u32[]{:S(2)}) collective-permute-start(f32[128,512]{1,0:T(8,128)S(1)} %get-tuple-element.57), channel_id=1, source_target_pairs={{0,1},{1,0},{2,3},{3,2},{4,5},{5,4},{6,7},{7,6},{8,9},{9,8},{10,11... | collective-permute-start | bytes 786440 | tf_op jit(solution)/shard_map/ppermute | solution.py:396
  37.1 2.4 %collective-permute-start.10 = (f32[384,512]{1,0:T(8,128)S(1)}, f32[384,512]{1,0:T(8,128)S(1)}, u32[]{:S(2)}, u32[]{:S(2)}) collective-permute-start(f32[384,512]{1,0:T(8,128)S(1)} %get-tuple-element.58), channel_id=1, source_target_pairs={{0,1},{1,0},{2,3},{3,2},{4,5},{5,4},{6,7},{7,6},{8,9},{9,8},{10,11... | collective-permute-start | bytes 2359304 | tf_op jit(solution)/shard_map/ppermute | solution.py:396
  37.5 3.7 %slice-start = ((f32[8,512]{1,0:T(8,128)}), f32[1,512]{1,0:T(1,128)S(1)}, s32[]{:S(2)}) async-start(f32[8,512]{1,0:T(8,128)} %copy-done), calls=%async_computation | async-start | bytes 4096 | tf_op jit(solution)/shard_map/slice | solution.py:422
  37.5 4.7 %collective-permute-start.12 = (f32[128,512]{1,0:T(8,128)S(1)}, f32[128,512]{1,0:T(8,128)S(1)}, u32[]{:S(2)}, u32[]{:S(2)}) collective-permute-start(f32[128,512]{1,0:T(8,128)S(1)} %get-tuple-element.59), channel_id=1, source_target_pairs={{0,1},{1,0},{2,3},{3,2},{4,5},{5,4},{6,7},{7,6},{8,9},{9,8},{10,11... | collective-permute-start | bytes 786440 | tf_op jit(solution)/shard_map/ppermute | solution.py:396
  37.7 7.6 %collective-permute-start.8 = (f32[384,512]{1,0:T(8,128)S(1)}, f32[384,512]{1,0:T(8,128)S(1)}, u32[]{:S(2)}, u32[]{:S(2)}) collective-permute-start(f32[384,512]{1,0:T(8,128)S(1)} %get-tuple-element.53), channel_id=1, source_target_pairs={{0,1},{1,0},{2,3},{3,2},{4,5},{5,4},{6,7},{7,6},{8,9},{9,8},{10,11... | collective-permute-start | bytes 2359304 | tf_op jit(solution)/shard_map/ppermute | solution.py:396
  38.0 6.3 %collective-permute-start.13 = (f16[128,512]{1,0:T(8,128)(2,1)S(1)}, f16[128,512]{1,0:T(8,128)(2,1)S(1)}, u32[]{:S(2)}, u32[]{:S(2)}) collective-permute-start(f16[128,512]{1,0:T(8,128)(2,1)S(1)} %multiply_convert_fusion.1), channel_id=1, source_target_pairs={{0,2},{1,3},{2,0},{3,1},{4,6},{5,7},{6,4},{7,5},{8,10},{9,11},{10,... | collective-permute-start | bytes 393224 | tf_op jit(solution)/shard_map/ppermute | solution.py:396
  39.7 12.3 %collective-permute-start.11 = (f16[384,512]{1,0:T(8,128)(2,1)S(1)}, f16[384,512]{1,0:T(8,128)(2,1)S(1)}, u32[]{:S(2)}, u32[]{:S(2)}) collective-permute-start(f16[384,512]{1,0:T(8,128)(2,1)S(1)} %multiply_convert_fusion), channel_id=1, source_target_pairs={{0,2},{1,3},{2,0},{3,1},{4,6},{5,7},{6,4},{7,5},{8,10},{9,11},{10,... | collective-permute-start | bytes 1179656 | tf_op jit(solution)/shard_map/ppermute | solution.py:396
  41.2 3.2 %slice-start.1 = ((f32[8,512]{1,0:T(8,128)}), f32[1,512]{1,0:T(1,128)S(1)}, s32[]{:S(2)}) async-start(f32[8,512]{1,0:T(8,128)} %copy-done), calls=%async_computation.1 | async-start | bytes 4096 | tf_op jit(solution)/shard_map/slice | solution.py:422
  44.4 7.6 %slice-start.2 = ((f32[8,512]{1,0:T(8,128)}), f32[1,512]{1,0:T(1,128)S(1)}, s32[]{:S(2)}) async-start(f32[8,512]{1,0:T(8,128)} %copy-done), calls=%async_computation.2 | async-start | bytes 4096 | tf_op jit(solution)/shard_map/slice | solution.py:422
  52.5 3.2 %collective-permute-start.16 = (f32[2,3,4,4]{3,2,1,0:T(4,128)S(1)}, f32[2,3,4,4]{3,2,1,0:T(4,128)S(1)}, u32[]{:S(2)}, u32[]{:S(2)}) collective-permute-start(f32[2,3,4,4]{3,2,1,0:T(4,128)S(1)} %get-tuple-element.69.refs_0_), channel_id=1, source_target_pairs={{0,3},{1,2},{2,1},{3,0},{4,7},{5,6},{6,5},{7,4},{8,11},{9,10},{10,... | collective-permute-start | bytes 1160 | tf_op jit(solution)/shard_map/ppermute | solution.py:427
  53.0 3.7 %collective-permute-start.15 = (f32[2,3,4,4]{3,2,1,0:T(4,128)S(1)}, f32[2,3,4,4]{3,2,1,0:T(4,128)S(1)}, u32[]{:S(2)}, u32[]{:S(2)}) collective-permute-start(f32[2,3,4,4]{3,2,1,0:T(4,128)S(1)} %get-tuple-element.69.refs_0_), channel_id=1, source_target_pairs={{0,2},{1,3},{2,0},{3,1},{4,6},{5,7},{6,4},{7,5},{8,10},{9,11},{10,... | collective-permute-start | bytes 1160 | tf_op jit(solution)/shard_map/ppermute | solution.py:427
  54.1 2.5 %collective-permute-start.14 = (f32[2,3,4,4]{3,2,1,0:T(4,128)S(1)}, f32[2,3,4,4]{3,2,1,0:T(4,128)S(1)}, u32[]{:S(2)}, u32[]{:S(2)}) collective-permute-start(f32[2,3,4,4]{3,2,1,0:T(4,128)S(1)} %get-tuple-element.69.refs_0_), channel_id=1, source_target_pairs={{0,1},{1,0},{2,3},{3,2},{4,5},{5,4},{6,7},{7,6},{8,9},{9,8},{10,11... | collective-permute-start | bytes 1160 | tf_op jit(solution)/shard_map/ppermute | solution.py:427
  (1 other events, 2.4 us)

commit v6 on v5

--- a/solution.py
+++ b/solution.py
@@ -407,13 +407,14 @@
     sums = near_pairs(partners, own, here, near, orbitals, GROUPS[0])
     here[0] = after(here[0], sums[0])
     sums += near_pairs(partners, own, here, near, orbitals, GROUPS[1])
-    for n in range(0, len(sums), 4):
-        mine, other, give, give_on = sums[n : n + 4]
-        if n:
-            give_on = after(give_on, half)
-        half = ((other + across(give_on, swap)) * to_half[:1]).astype(F16)
-        got = across(give, swap)
-        parts.append((mine, got, across(half, cross)))
+    mine_a, other_a, give_a, on_a, mine_b, other_b, give_b, on_b = sums
+    half_a = ((other_a + across(on_a, swap)) * to_half[:1]).astype(F16)
+    x_a = across(half_a, cross)
+    on_b = after(on_b, half_a)
+    half_b = ((other_b + across(on_b, swap)) * to_half[:1]).astype(F16)
+    x_b = across(half_b, cross)
+    parts.append((mine_a, across(after(give_a, half_a), swap), x_a))
+    parts.append((mine_b, across(after(give_b, half_a), swap), x_b))
 
     out = partners.shape + (domain, wide)
     amps, shares = [], []

time: 57.4 us -> 57.3 us (level)
  no operation moved by 1% of the time
where the time goes in v6:
time: 57.3 us; the launch traced here: 57.2 us
  waiting for transfers between devices  29.8 us (52%)
  starting transfers between devices  17 us (30%)
  Pallas kernels  8.68 us (15%)
  between operations  0.81 us (1%)
  other arithmetic  0.78 us (1%)
    ppermute x9, waiting for transfers between devices, across(): return lax.ppermute(sums, 'pair', axis_pairs)  14.7 us
    ppermute x3, waiting for transfers between devices, fast(): own.append(lax.ppermute(send, 'aux', [(i, i ^ k) for i in range(count)]))  11.1 us
    ppermute x9, starting transfers between devices, across(): return lax.ppermute(sums, 'pair', axis_pairs)  6.13 us
    ppermute x3, starting transfers between devices, fast(): own.append(lax.ppermute(send, 'aux', [(i, i ^ k) for i in range(count)]))  5.67 us
    ppermute x2, starting transfers between devices, fast(): lax.ppermute(m, ('aux', 'pair'), side)  3.35 us
    ppermute x2, waiting for transfers between devices, fast(): lax.ppermute(m, ('aux', 'pair'), side)  2.24 us
    pallas_call x2, Pallas kernels, near_pairs(): call(kernel, 'near', out_shape=shapes, in_specs=[VMEM] * (count + 5), out...  1.94 us
    ppermute x3, starting transfers between devices, fast(): others = [lax.ppermute(share, 'pair', to) for to in (swap, cross, both)]  1.89 us
  transfers between devices with their start and end apart: 17, of which 9 were waited for; matrix products, arithmetic and copies ran while one was open for 1% of the time, Pallas kernels for 9%

profile of v6, /device:TPU:0, one launch (start us, length us, event | category | flops | bytes accessed | tf_op | source)
XLA Modules:
  0.0 57.2 jit_solution(17821605170746615039)
XLA Ops:
  0.6 1.5 %pack.1 = (bf16[656,128]{1,0:T(8,128)(2,1)S(1)}, bf16[656,128]{1,0:T(8,128)(2,1)S(1)}, bf16[656,128]{1,0:T(8,128)(2,1)S(1)}, bf16[656,128]{1,0:T(8,128)(2,1)S(1)}) custom-call(bf16[80,32,128]{2,1,0:T(8,128)(2,1)} %bitcast.26), custom_call_target="tpu_custom_call" | custom-call | tf_op jit(solution)/shard_map/pack/pallas_call | solution.py:67
  2.1 4.1 %collective-permute-start.1 = (bf16[656,128]{1,0:T(8,128)(2,1)S(1)}, bf16[656,128]{1,0:T(8,128)(2,1)S(1)}, u32[]{:S(2)}, u32[]{:S(2)}) collective-permute-start(bf16[656,128]{1,0:T(8,128)(2,1)S(1)} %get-tuple-element.40), channel_id=1, source_target_pairs={{0,8},{4,12},{8,0},{12,4},{1,9},{5,13},{9,1},{13,5},{2,10},{6,14},... | collective-permute-start | bytes 503816 | tf_op jit(solution)/shard_map/ppermute | solution.py:389
  6.2 1.6 %collective-permute-start = (bf16[656,128]{1,0:T(8,128)(2,1)S(1)}, bf16[656,128]{1,0:T(8,128)(2,1)S(1)}, u32[]{:S(2)}, u32[]{:S(2)}) collective-permute-start(bf16[656,128]{1,0:T(8,128)(2,1)S(1)} %get-tuple-element.53.refs_4_), channel_id=1, source_target_pairs={{0,4},{4,0},{8,12},{12,8},{1,5},{5,1},{9,13},{13,9},{2,6},{6,2},{1... | collective-permute-start | bytes 503816 | tf_op jit(solution)/shard_map/ppermute | solution.py:389
  7.8 8.0 %collective-permute-done.1.refs_2_ = bf16[656,128]{1,0:T(8,128)(2,1)S(1)} collective-permute-done((bf16[656,128]{1,0:T(8,128)(2,1)S(1)}, bf16[656,128]{1,0:T(8,128)(2,1)S(1)}, u32[]{:S(2)}, u32[]{:S(2)}) %collective-permute-start.1) | collective-permute-done | bytes 167968 | tf_op jit(solution)/shard_map/ppermute | solution.py:389
  15.8 3.1 %collective-permute-done.2.refs_3_ = bf16[656,128]{1,0:T(8,128)(2,1)S(1)} collective-permute-done((bf16[656,128]{1,0:T(8,128)(2,1)S(1)}, bf16[656,128]{1,0:T(8,128)(2,1)S(1)}, u32[]{:S(2)}, u32[]{:S(2)}) %collective-permute-start.2) | collective-permute-done | bytes 167968 | tf_op jit(solution)/shard_map/ppermute | solution.py:389
  19.0 0.8 %own.1 = (f32[256,512]{1,0:T(8,128)S(1)}, f32[256,512]{1,0:T(8,128)S(1)}, f32[2,264,512]{2,1,0:T(8,128)S(1)}, f32[8,512]{1,0:T(8,128)S(1)}) custom-call(bf16[656,128]{1,0:T(8,128)(2,1)S(1)} %get-tuple-element.44.refs_0_, bf16[656,128]{1,0:T(8,128)(2,1)S(1)} %collective-permute-done.refs_1_, bf16[656,128]{1,0:T(8,128)(2,1)S(1)} %collective-permute-done.1.refs_2_, ...), custom_call_target="tpu_custom_call" | custom-call | tf_op jit(solution)/shard_map/own/pallas_call | solution.py:144
  19.9 3.2 %collective-permute-start.6 = (bf16[1920,128]{1,0:T(8,128)(2,1)S(1)}, bf16[1920,128]{1,0:T(8,128)(2,1)S(1)}, u32[]{:S(2)}, u32[]{:S(2)}) collective-permute-start(bf16[1920,128]{1,0:T(8,128)(2,1)S(1)} %get-tuple-element.42), channel_id=1, source_target_pairs={{0,4},{1,5},{2,6},{3,7},{4,0},{5,1},{6,2},{7,3},{8,12},{9,13},{10,... | collective-permute-start | bytes 1474568 | tf_op jit(solution)/shard_map/ppermute | solution.py:392
  23.5 1.6 %collective-permute-start.4 = (f16[256,512]{1,0:T(8,128)(2,1)S(1)}, f16[256,512]{1,0:T(8,128)(2,1)S(1)}, u32[]{:S(2)}, u32[]{:S(2)}) collective-permute-start(f16[256,512]{1,0:T(8,128)(2,1)S(1)} %fusion.4), channel_id=1, source_target_pairs={{0,2},{1,3},{2,0},{3,1},{4,6},{5,7},{6,4},{7,5},{8,10},{9,11},{10,... | collective-permute-start | bytes 786440 | tf_op jit(solution)/shard_map/ppermute | solution.py:396
  25.6 0.8 %energies.1 = (f32[2,128,128]{2,1,0:T(8,128)S(1)}, f32[2,3,4,128]{3,2,1,0:T(4,128)S(1)}) custom-call(s32[2,3]{1,0:T(2,128)S(1)} %copy-done.1, f32[4,8]{1,0:T(4,128)S(1)} %bitcast.25, s32[8,128]{1,0:T(8,128)S(1)} %copy-done.2, f32[8,128]{1,0:T(8,128)S(1)} %bitcast.24), custom_call_target="tpu_custom_call" | custom-call | tf_op jit(solution)/shard_map/energies/pallas_call | solution.py:368
  26.4 6.1 %collective-permute-done.5.top_ref = f32[8,512]{1,0:T(8,128)S(1)} collective-permute-done((f32[8,512]{1,0:T(8,128)S(1)}, f32[8,512]{1,0:T(8,128)S(1)}, u32[]{:S(2)}, u32[]{:S(2)}) %collective-permute-start.5) | collective-permute-done | bytes 16416 | tf_op jit(solution)/shard_map/ppermute | solution.py:396
  32.6 2.2 %collective-permute-done.6.refs_6_ = bf16[1920,128]{1,0:T(8,128)(2,1)S(1)} collective-permute-done((bf16[1920,128]{1,0:T(8,128)(2,1)S(1)}, bf16[1920,128]{1,0:T(8,128)(2,1)S(1)}, u32[]{:S(2)}, u32[]{:S(2)}) %collective-permute-start.6) | collective-permute-done | bytes 491552 | tf_op jit(solution)/shard_map/ppermute | solution.py:392
  34.9 0.6 near.2
  35.5 1.4 %near.3 = (f32[384,512]{1,0:T(8,128)S(1)}, f32[384,512]{1,0:T(8,128)S(1)}, f32[384,512]{1,0:T(8,128)S(1)}, f32[384,512]{1,0:T(8,128)S(1)}) custom-call(s32[2,3]{1,0:T(2,128)S(1)} %copy-done.1, bf16[656,128]{1,0:T(8,128)(2,1)S(1)} %get-tuple-element.44.refs_0_, bf16[656,128]{1,0:T(8,128)(2,1)S(1)} %collective-permute-done.refs_1_, ...), custom_call_target="tpu_custom_call" | custom-call | tf_op jit(solution)/shard_map/near/pallas_call | solution.py:203
  37.5 1.5 %collective-permute-start.13 = (f16[128,512]{1,0:T(8,128)(2,1)S(1)}, f16[128,512]{1,0:T(8,128)(2,1)S(1)}, u32[]{:S(2)}, u32[]{:S(2)}) collective-permute-start(f16[128,512]{1,0:T(8,128)(2,1)S(1)} %multiply_convert_fusion.1), channel_id=1, source_target_pairs={{0,2},{1,3},{2,0},{3,1},{4,6},{5,7},{6,4},{7,5},{8,10},{9,11},{10,... | collective-permute-start | bytes 393224 | tf_op jit(solution)/shard_map/ppermute | solution.py:396
  39.7 1.5 %collective-permute-start.11 = (f16[384,512]{1,0:T(8,128)(2,1)S(1)}, f16[384,512]{1,0:T(8,128)(2,1)S(1)}, u32[]{:S(2)}, u32[]{:S(2)}) collective-permute-start(f16[384,512]{1,0:T(8,128)(2,1)S(1)} %multiply_convert_fusion), channel_id=1, source_target_pairs={{0,2},{1,3},{2,0},{3,1},{4,6},{5,7},{6,4},{7,5},{8,10},{9,11},{10,... | collective-permute-start | bytes 1179656 | tf_op jit(solution)/shard_map/ppermute | solution.py:396
  41.3 0.9 %finish.2 = (f32[2,3,128,512]{3,2,1,0:T(8,128)}, f32[2,4,128]{2,1,0:T(4,128)S(1)}) custom-call(f32[256,512]{1,0:T(8,128)S(1)} %fusion.1.total_ref, f32[2,128,128]{2,1,0:T(8,128)S(1)} %get-tuple-element.50.row_ref, f32[2,3,4,128]{3,2,1,0:T(4,128)S(1)} %get-tuple-element.65.col_ref), custom_call_target="tpu_custom_call" | custom-call | tf_op jit(solution)/shard_map/finish/pallas_call | solution.py:268
  42.2 1.2 %collective-permute-done.13 = f16[128,512]{1,0:T(8,128)(2,1)S(1)} collective-permute-done((f16[128,512]{1,0:T(8,128)(2,1)S(1)}, f16[128,512]{1,0:T(8,128)(2,1)S(1)}, u32[]{:S(2)}, u32[]{:S(2)}) %collective-permute-start.13) | collective-permute-done | bytes 131104 | tf_op jit(solution)/shard_map/ppermute | solution.py:396
  43.5 0.8 %finish.3 = (f32[2,3,128,512]{3,2,1,0:T(8,128)}, f32[1,4,128]{2,1,0:T(4,128)S(1)}) custom-call(f32[128,512]{1,0:T(8,128)S(1)} %multiply_add_fusion.1.total_ref, f32[2,128,128]{2,1,0:T(8,128)S(1)} %get-tuple-element.50.row_ref, f32[2,3,4,128]{3,2,1,0:T(4,128)S(1)} %get-tuple-element.65.col_ref, ...), custom_call_target="tpu_custom_call", output_to_operand_aliasing={{0}: (3, {})} | custom-call | tf_op jit(solution)/shard_map/finish/pallas_call | solution.py:268
  44.3 7.2 %collective-permute-done.11 = f16[384,512]{1,0:T(8,128)(2,1)S(1)} collective-permute-done((f16[384,512]{1,0:T(8,128)(2,1)S(1)}, f16[384,512]{1,0:T(8,128)(2,1)S(1)}, u32[]{:S(2)}, u32[]{:S(2)}) %collective-permute-start.11) | collective-permute-done | bytes 393248 | tf_op jit(solution)/shard_map/ppermute | solution.py:396
  52.0 0.9 %collective-permute-start.16 = (f32[2,3,4,4]{3,2,1,0:T(4,128)S(1)}, f32[2,3,4,4]{3,2,1,0:T(4,128)S(1)}, u32[]{:S(2)}, u32[]{:S(2)}) collective-permute-start(f32[2,3,4,4]{3,2,1,0:T(4,128)S(1)} %get-tuple-element.73.refs_0_), channel_id=1, source_target_pairs={{0,3},{1,2},{2,1},{3,0},{4,7},{5,6},{6,5},{7,4},{8,11},{9,10},{10,... | collective-permute-start | bytes 1160 | tf_op jit(solution)/shard_map/ppermute | solution.py:428
  52.9 0.7 %collective-permute-start.15 = (f32[2,3,4,4]{3,2,1,0:T(4,128)S(1)}, f32[2,3,4,4]{3,2,1,0:T(4,128)S(1)}, u32[]{:S(2)}, u32[]{:S(2)}) collective-permute-start(f32[2,3,4,4]{3,2,1,0:T(4,128)S(1)} %get-tuple-element.73.refs_0_), channel_id=1, source_target_pairs={{0,2},{1,3},{2,0},{3,1},{4,6},{5,7},{6,4},{7,5},{8,10},{9,11},{10,... | collective-permute-start | bytes 1160 | tf_op jit(solution)/shard_map/ppermute | solution.py:428
  53.9 0.9 %put.1 = f32[2,3,128,512]{3,2,1,0:T(8,128)} custom-call(f32[3,128,512]{2,1,0:T(8,128)S(1)} %get-tuple-element.71.values_ref, f32[2,3,128,512]{3,2,1,0:T(8,128)} %get-tuple-element.72._), custom_call_target="tpu_custom_call", output_to_operand_aliasing={{}: (1, {})} | custom-call | tf_op jit(solution)/shard_map/put/pallas_call | solution.py:319
  55.2 1.3 %collective-permute-done.15.refs_2_ = f32[2,3,4,4]{3,2,1,0:T(4,128)S(1)} collective-permute-done((f32[2,3,4,4]{3,2,1,0:T(4,128)S(1)}, f32[2,3,4,4]{3,2,1,0:T(4,128)S(1)}, u32[]{:S(2)}, u32[]{:S(2)}) %collective-permute-start.15) | collective-permute-done | bytes 416 | tf_op jit(solution)/shard_map/ppermute | solution.py:428
  56.6 0.6 %last.1 = f32[2,3,4,4]{3,2,1,0:T(4,128)} custom-call(f32[2,3,4,4]{3,2,1,0:T(4,128)S(1)} %get-tuple-element.73.refs_0_, f32[2,3,4,4]{3,2,1,0:T(4,128)S(1)} %collective-permute-done.14.refs_1_, f32[2,3,4,4]{3,2,1,0:T(4,128)S(1)} %collective-permute-done.15.refs_2_, f32[2,3,4,4]{3,2,1,0:T(4,128)S(1)} %collective-permute-done.16.refs_3_), custom_call_target="tpu_custom_call" | custom-call | tf_op jit(solution)/shard_map/last/pallas_call | solution.py:334
  (46 shorter events, 4.1 us)
Async XLA Ops:
  2.1 13.6 %collective-permute-start.1 = (bf16[656,128]{1,0:T(8,128)(2,1)S(1)}, bf16[656,128]{1,0:T(8,128)(2,1)S(1)}, u32[]{:S(2)}, u32[]{:S(2)}) collective-permute-start(bf16[656,128]{1,0:T(8,128)(2,1)S(1)} %get-tuple-element.40), channel_id=1, source_target_pairs={{0,8},{4,12},{8,0},{12,4},{1,9},{5,13},{9,1},{13,5},{2,10},{6,14},... | collective-permute-start | bytes 503816 | tf_op jit(solution)/shard_map/ppermute | solution.py:389
  6.2 9.5 %collective-permute-start = (bf16[656,128]{1,0:T(8,128)(2,1)S(1)}, bf16[656,128]{1,0:T(8,128)(2,1)S(1)}, u32[]{:S(2)}, u32[]{:S(2)}) collective-permute-start(bf16[656,128]{1,0:T(8,128)(2,1)S(1)} %get-tuple-element.53.refs_4_), channel_id=1, source_target_pairs={{0,4},{4,0},{8,12},{12,8},{1,5},{5,1},{9,13},{13,9},{2,6},{6,2},{1... | collective-permute-start | bytes 503816 | tf_op jit(solution)/shard_map/ppermute | solution.py:389
  7.8 11.1 %collective-permute-start.2 = (bf16[656,128]{1,0:T(8,128)(2,1)S(1)}, bf16[656,128]{1,0:T(8,128)(2,1)S(1)}, u32[]{:S(2)}, u32[]{:S(2)}) collective-permute-start(bf16[656,128]{1,0:T(8,128)(2,1)S(1)} %get-tuple-element.41.refs_5_), channel_id=1, source_target_pairs={{0,12},{4,8},{8,4},{12,0},{1,13},{5,9},{9,5},{13,1},{2,14},{6,10},... | collective-permute-start | bytes 503816 | tf_op jit(solution)/shard_map/ppermute | solution.py:389
  19.8 3.4 %collective-permute-start.3 = (f32[2,264,512]{2,1,0:T(8,128)S(1)}, f32[2,264,512]{2,1,0:T(8,128)S(1)}, u32[]{:S(2)}, u32[]{:S(2)}) collective-permute-start(f32[2,264,512]{2,1,0:T(8,128)S(1)} %get-tuple-element.46), channel_id=1, source_target_pairs={{0,1},{1,0},{2,3},{3,2},{4,5},{5,4},{6,7},{7,6},{8,9},{9,8},{10,11... | collective-permute-start | bytes 3244040 | tf_op jit(solution)/shard_map/ppermute | solution.py:396
  19.9 15.0 %collective-permute-start.6 = (bf16[1920,128]{1,0:T(8,128)(2,1)S(1)}, bf16[1920,128]{1,0:T(8,128)(2,1)S(1)}, u32[]{:S(2)}, u32[]{:S(2)}) collective-permute-start(bf16[1920,128]{1,0:T(8,128)(2,1)S(1)} %get-tuple-element.42), channel_id=1, source_target_pairs={{0,4},{1,5},{2,6},{3,7},{4,0},{5,1},{6,2},{7,3},{8,12},{9,13},{10,... | collective-permute-start | bytes 1474568 | tf_op jit(solution)/shard_map/ppermute | solution.py:392
  23.0 11.8 %collective-permute-start.7 = (bf16[1920,128]{1,0:T(8,128)(2,1)S(1)}, bf16[1920,128]{1,0:T(8,128)(2,1)S(1)}, u32[]{:S(2)}, u32[]{:S(2)}) collective-permute-start(bf16[1920,128]{1,0:T(8,128)(2,1)S(1)} %get-tuple-element.43), channel_id=1, source_target_pairs={{0,1},{1,0},{2,3},{3,2},{4,8},{5,9},{6,10},{7,11},{8,4},{9,5},{10,... | collective-permute-start | bytes 1474568 | tf_op jit(solution)/shard_map/ppermute | solution.py:392
  23.2 2.4 %copy-start.1 = (s32[2,3]{1,0:T(2,128)S(1)}, s32[2,3]{1,0:T(2,128)}, u32[]{:S(2)}) copy-start(s32[2,3]{1,0:T(2,128)} %partners_ref.5) | copy-start | bytes 76
  23.2 2.4 %copy-start.2 = (s32[8,128]{1,0:T(8,128)S(1)}, s32[8,128]{1,0:T(8,128)}, u32[]{:S(2)}) copy-start(s32[8,128]{1,0:T(8,128)} %domains_ref.1) | copy-start | bytes 12292
  23.2 2.4 %copy-start.3 = (f32[1024]{0:T(1024)S(1)}, f32[1024]{0:T(1024)}, u32[]{:S(2)}) copy-start(f32[1024]{0:T(1024)} %param.9) | copy-start | bytes 12292
  23.2 2.4 %copy-start.4 = (f32[8,4]{0,1:T(4,128)S(1)}, f32[8,4]{0,1:T(4,128)}, u32[]{:S(2)}) copy-start(f32[8,4]{0,1:T(4,128)} %param.8) | copy-start | bytes 388
  23.5 9.1 %collective-permute-start.4 = (f16[256,512]{1,0:T(8,128)(2,1)S(1)}, f16[256,512]{1,0:T(8,128)(2,1)S(1)}, u32[]{:S(2)}, u32[]{:S(2)}) collective-permute-start(f16[256,512]{1,0:T(8,128)(2,1)S(1)} %fusion.4), channel_id=1, source_target_pairs={{0,2},{1,3},{2,0},{3,1},{4,6},{5,7},{6,4},{7,5},{8,10},{9,11},{10,... | collective-permute-start | bytes 786440 | tf_op jit(solution)/shard_map/ppermute | solution.py:396
  25.1 7.4 %collective-permute-start.5 = (f32[8,512]{1,0:T(8,128)S(1)}, f32[8,512]{1,0:T(8,128)S(1)}, u32[]{:S(2)}, u32[]{:S(2)}) collective-permute-start(f32[8,512]{1,0:T(8,128)S(1)} %get-tuple-element.49), channel_id=1, source_target_pairs={{0,2},{1,3},{2,0},{3,1},{4,6},{5,7},{6,4},{7,5},{8,10},{9,11},{10,... | collective-permute-start | bytes 49160 | tf_op jit(solution)/shard_map/ppermute | solution.py:396
  32.6 4.9 %copy-start = (f32[8,512]{1,0:T(8,128)}, f32[8,512]{1,0:T(8,128)S(1)}, u32[]{:S(2)}) copy-start(f32[8,512]{1,0:T(8,128)S(1)} %scale_up.1) | copy-start | bytes 49156
  35.4 1.6 %collective-permute-start.8 = (f32[128,512]{1,0:T(8,128)S(1)}, f32[128,512]{1,0:T(8,128)S(1)}, u32[]{:S(2)}, u32[]{:S(2)}) collective-permute-start(f32[128,512]{1,0:T(8,128)S(1)} %get-tuple-element.57), channel_id=1, source_target_pairs={{0,1},{1,0},{2,3},{3,2},{4,5},{5,4},{6,7},{7,6},{8,9},{9,8},{10,11... | collective-permute-start | bytes 786440 | tf_op jit(solution)/shard_map/ppermute | solution.py:396
  37.1 2.4 %collective-permute-start.10 = (f32[384,512]{1,0:T(8,128)S(1)}, f32[384,512]{1,0:T(8,128)S(1)}, u32[]{:S(2)}, u32[]{:S(2)}) collective-permute-start(f32[384,512]{1,0:T(8,128)S(1)} %get-tuple-element.61), channel_id=1, source_target_pairs={{0,1},{1,0},{2,3},{3,2},{4,5},{5,4},{6,7},{7,6},{8,9},{9,8},{10,11... | collective-permute-start | bytes 2359304 | tf_op jit(solution)/shard_map/ppermute | solution.py:396
  37.5 3.7 %slice-start = ((f32[8,512]{1,0:T(8,128)}), f32[1,512]{1,0:T(1,128)S(1)}, s32[]{:S(2)}) async-start(f32[8,512]{1,0:T(8,128)} %copy-done), calls=%async_computation | async-start | bytes 4096 | tf_op jit(solution)/shard_map/slice | solution.py:423
  37.5 5.9 %collective-permute-start.13 = (f16[128,512]{1,0:T(8,128)(2,1)S(1)}, f16[128,512]{1,0:T(8,128)(2,1)S(1)}, u32[]{:S(2)}, u32[]{:S(2)}) collective-permute-start(f16[128,512]{1,0:T(8,128)(2,1)S(1)} %multiply_convert_fusion.1), channel_id=1, source_target_pairs={{0,2},{1,3},{2,0},{3,1},{4,6},{5,7},{6,4},{7,5},{8,10},{9,11},{10,... | collective-permute-start | bytes 393224 | tf_op jit(solution)/shard_map/ppermute | solution.py:396
  39.0 4.4 %collective-permute-start.12 = (f32[128,512]{1,0:T(8,128)S(1)}, f32[128,512]{1,0:T(8,128)S(1)}, u32[]{:S(2)}, u32[]{:S(2)}) collective-permute-start(f32[128,512]{1,0:T(8,128)S(1)} %get-tuple-element.63), channel_id=1, source_target_pairs={{0,1},{1,0},{2,3},{3,2},{4,5},{5,4},{6,7},{7,6},{8,9},{9,8},{10,11... | collective-permute-start | bytes 786440 | tf_op jit(solution)/shard_map/ppermute | solution.py:396
  39.0 5.3 %collective-permute-start.9 = (f32[384,512]{1,0:T(8,128)S(1)}, f32[384,512]{1,0:T(8,128)S(1)}, u32[]{:S(2)}, u32[]{:S(2)}) collective-permute-start(f32[384,512]{1,0:T(8,128)S(1)} %get-tuple-element.58), channel_id=1, source_target_pairs={{0,1},{1,0},{2,3},{3,2},{4,5},{5,4},{6,7},{7,6},{8,9},{9,8},{10,11... | collective-permute-start | bytes 2359304 | tf_op jit(solution)/shard_map/ppermute | solution.py:396
  39.7 11.8 %collective-permute-start.11 = (f16[384,512]{1,0:T(8,128)(2,1)S(1)}, f16[384,512]{1,0:T(8,128)(2,1)S(1)}, u32[]{:S(2)}, u32[]{:S(2)}) collective-permute-start(f16[384,512]{1,0:T(8,128)(2,1)S(1)} %multiply_convert_fusion), channel_id=1, source_target_pairs={{0,2},{1,3},{2,0},{3,1},{4,6},{5,7},{6,4},{7,5},{8,10},{9,11},{10,... | collective-permute-start | bytes 1179656 | tf_op jit(solution)/shard_map/ppermute | solution.py:396
  43.5 8.0 %slice-start.2 = ((f32[8,512]{1,0:T(8,128)}), f32[1,512]{1,0:T(1,128)S(1)}, s32[]{:S(2)}) async-start(f32[8,512]{1,0:T(8,128)} %copy-done), calls=%async_computation.2 | async-start | bytes 4096 | tf_op jit(solution)/shard_map/slice | solution.py:423
  52.0 3.2 %collective-permute-start.16 = (f32[2,3,4,4]{3,2,1,0:T(4,128)S(1)}, f32[2,3,4,4]{3,2,1,0:T(4,128)S(1)}, u32[]{:S(2)}, u32[]{:S(2)}) collective-permute-start(f32[2,3,4,4]{3,2,1,0:T(4,128)S(1)} %get-tuple-element.73.refs_0_), channel_id=1, source_target_pairs={{0,3},{1,2},{2,1},{3,0},{4,7},{5,6},{6,5},{7,4},{8,11},{9,10},{10,... | collective-permute-start | bytes 1160 | tf_op jit(solution)/shard_map/ppermute | solution.py:428
  52.9 3.7 %collective-permute-start.15 = (f32[2,3,4,4]{3,2,1,0:T(4,128)S(1)}, f32[2,3,4,4]{3,2,1,0:T(4,128)S(1)}, u32[]{:S(2)}, u32[]{:S(2)}) collective-permute-start(f32[2,3,4,4]{3,2,1,0:T(4,128)S(1)} %get-tuple-element.73.refs_0_), channel_id=1, source_target_pairs={{0,2},{1,3},{2,0},{3,1},{4,6},{5,7},{6,4},{7,5},{8,10},{9,11},{10,... | collective-permute-start | bytes 1160 | tf_op jit(solution)/shard_map/ppermute | solution.py:428
  53.6 3.0 %collective-permute-start.14 = (f32[2,3,4,4]{3,2,1,0:T(4,128)S(1)}, f32[2,3,4,4]{3,2,1,0:T(4,128)S(1)}, u32[]{:S(2)}, u32[]{:S(2)}) collective-permute-start(f32[2,3,4,4]{3,2,1,0:T(4,128)S(1)} %get-tuple-element.73.refs_0_), channel_id=1, source_target_pairs={{0,1},{1,0},{2,3},{3,2},{4,5},{5,4},{6,7},{7,6},{8,9},{9,8},{10,11... | collective-permute-start | bytes 1160 | tf_op jit(solution)/shard_map/ppermute | solution.py:428
  (1 other events, 2.3 us)

commit v7 on v6

--- a/solution.py
+++ b/solution.py
@@ -100,12 +100,12 @@
     return lax.dot_general(left, right, (((0,), (0,)), ((), ())), preferred_element_type=F32)
 
 
-def left_rows(own_refs, depth, r):
+def left_rows(own_refs, depth, r, part=slice(0, 4)):
     p = lax.axis_index("pair")
     x, c = p // 2, lax.rem(p, 2)
     order = (2 * x + c, 2 * (1 - x) + c, 2 * x + 1 - c, 2 * (1 - x) + 1 - c)
     columns = [
-        jnp.concatenate([ref[panel_at(depth, i, r), :] for ref in own_refs], axis=0) for i in order
+        jnp.concatenate([ref[panel_at(depth, i, r), :] for ref in own_refs], axis=0) for i in order[part]
     ]
     return jnp.concatenate(columns, axis=1)
 
@@ -116,42 +116,45 @@
         out[at] = sums[n * domain : (n + 1) * domain]
 
 
-def own_pairs(own, orbitals):
+def own_right(own_refs, depth, r, orbitals):
+    columns = [
+        jnp.concatenate([ref[panel_at(depth, j, r), :] for ref in own_refs], axis=0)
+        for j in range(orbitals)
+    ]
+    return jnp.concatenate(columns, axis=1)
+
+
+def own_pairs(own, orbitals, given):
     count, domain = len(own), own[0].shape[1]
     depth = depth_of(own[0], orbitals)
     wide = orbitals * domain
+    part = slice(2, 4) if given else slice(0, 2)
 
     def kernel(*refs):
-        own_refs, (mine, other, give, peak) = refs[:count], refs[count:]
-        top = own_refs[0][-PEAK_ROWS:, :].astype(F32)
-        for ref in own_refs[1:]:
-            top = jnp.maximum(top, ref[-PEAK_ROWS:, :].astype(F32))
-        top = jnp.maximum(top[:8], top[8:])
-        peak[...] = jnp.concatenate([top] * orbitals, axis=1)
-        for n in range(2):
-            give[n, 2 * domain :] = peak[...]
+        own_refs, outs = refs[:count], refs[count:]
+        if given:
+            give, peak = outs
+            top = own_refs[0][-PEAK_ROWS:, :].astype(F32)
+            for ref in own_refs[1:]:
+                top = jnp.maximum(top, ref[-PEAK_ROWS:, :].astype(F32))
+            top = jnp.maximum(top[:8], top[8:])
+            peak[...] = jnp.concatenate([top] * orbitals, axis=1)
+            for n in range(2):
+                give[n, 2 * domain :] = peak[...]
+            outs = (give.at[0], give.at[1])
         for r in range(2):
-            right = jnp.concatenate(
-                [
-                    jnp.concatenate([ref[panel_at(depth, j, r), :] for ref in own_refs], axis=0)
-                    for j in range(orbitals)
-                ],
-                axis=1,
-            )
+            left = left_rows(own_refs, depth, r, part)
+            sums = product(left, own_right(own_refs, depth, r, orbitals))
             at = slice(r * domain, (r + 1) * domain)
-            store_sums(product(left_rows(own_refs, depth, r), right), at, mine, other, give.at[0], give.at[1])
-
-    return call(
-        kernel,
-        "own",
-        out_shape=[
-            shape(2 * domain, wide),
-            shape(2 * domain, wide),
-            shape(2, 2 * domain + 8, wide),
-            shape(8, wide),
-        ],
+            outs[0][at], outs[1][at] = sums[:domain], sums[domain:]
+
+    kept = [shape(2 * domain, wide)] * 2
+    return call(
+        kernel,
+        "own_give" if given else "own_keep",
+        out_shape=[shape(2, 2 * domain + 8, wide), shape(8, wide)] if given else kept,
         in_specs=[VMEM] * count,
-        out_specs=[VMEM] * 4,
+        out_specs=[VMEM] * 2,
     )(*own)
 
 
@@ -395,7 +398,8 @@
     def across(sums, axis_pairs):
         return lax.ppermute(sums, "pair", axis_pairs)
 
-    mine, other, give, peak = own_pairs(own, orbitals)
+    give, peak = own_pairs(own, orbitals, True)
+    mine, other = own_pairs(own, orbitals, False)
     got = across(give, swap)
     top, to_half = scale_down(peak, got, 2 * count * depth)
     half = ((other + got[1, : 2 * domain]) * to_half[:1]).astype(F16)

time: 57.3 us -> 57.1 us (level)
  no operation moved by 1% of the time
where the time goes in v7:
time: 57.1 us; the launch traced here: 56.9 us
  waiting for transfers between devices  29.3 us (51%)
  starting transfers between devices  17 us (30%)
  Pallas kernels  8.87 us (16%)
  between operations  0.85 us (1%)
  other arithmetic  0.78 us (1%)
    ppermute x9, waiting for transfers between devices, across(): return lax.ppermute(sums, 'pair', axis_pairs)  14.7 us
    ppermute x3, waiting for transfers between devices, fast(): own.append(lax.ppermute(send, 'aux', [(i, i ^ k) for i in range(count)]))  11.1 us
    ppermute x9, starting transfers between devices, across(): return lax.ppermute(sums, 'pair', axis_pairs)  6.13 us
    ppermute x3, starting transfers between devices, fast(): own.append(lax.ppermute(send, 'aux', [(i, i ^ k) for i in range(count)]))  5.67 us
    ppermute x2, starting transfers between devices, fast(): lax.ppermute(m, ('aux', 'pair'), side)  3.34 us
    pallas_call x2, Pallas kernels, near_pairs(): call(kernel, 'near', out_shape=shapes, in_specs=[VMEM] * (count + 5), out...  1.93 us
    ppermute x3, starting transfers between devices, fast(): others = [lax.ppermute(share, 'pair', to) for to in (swap, cross, both)]  1.89 us
    ppermute x3, waiting for transfers between devices, fast(): others = [lax.ppermute(share, 'pair', to) for to in (swap, cross, both)]  1.77 us
  transfers between devices with their start and end apart: 17, of which 9 were waited for; matrix products, arithmetic and copies ran while one was open for 1% of the time, Pallas kernels for 9%

profile of v7, /device:TPU:0, one launch (start us, length us, event | category | flops | bytes accessed | tf_op | source)
XLA Modules:
  0.0 56.9 jit_solution(8501445861101869698)
XLA Ops:
  0.6 1.5 %pack.1 = (bf16[656,128]{1,0:T(8,128)(2,1)S(1)}, bf16[656,128]{1,0:T(8,128)(2,1)S(1)}, bf16[656,128]{1,0:T(8,128)(2,1)S(1)}, bf16[656,128]{1,0:T(8,128)(2,1)S(1)}) custom-call(bf16[80,32,128]{2,1,0:T(8,128)(2,1)} %bitcast.26), custom_call_target="tpu_custom_call" | custom-call | tf_op jit(solution)/shard_map/pack/pallas_call | solution.py:67
  2.1 4.1 %collective-permute-start.1 = (bf16[656,128]{1,0:T(8,128)(2,1)S(1)}, bf16[656,128]{1,0:T(8,128)(2,1)S(1)}, u32[]{:S(2)}, u32[]{:S(2)}) collective-permute-start(bf16[656,128]{1,0:T(8,128)(2,1)S(1)} %get-tuple-element.40), channel_id=1, source_target_pairs={{0,8},{4,12},{8,0},{12,4},{1,9},{5,13},{9,1},{13,5},{2,10},{6,14},... | collective-permute-start | bytes 503816 | tf_op jit(solution)/shard_map/ppermute | solution.py:392
  6.2 1.6 %collective-permute-start = (bf16[656,128]{1,0:T(8,128)(2,1)S(1)}, bf16[656,128]{1,0:T(8,128)(2,1)S(1)}, u32[]{:S(2)}, u32[]{:S(2)}) collective-permute-start(bf16[656,128]{1,0:T(8,128)(2,1)S(1)} %get-tuple-element.53.refs_4_), channel_id=1, source_target_pairs={{0,4},{4,0},{8,12},{12,8},{1,5},{5,1},{9,13},{13,9},{2,6},{6,2},{1... | collective-permute-start | bytes 503816 | tf_op jit(solution)/shard_map/ppermute | solution.py:392
  7.8 8.0 %collective-permute-done.1.refs_2_ = bf16[656,128]{1,0:T(8,128)(2,1)S(1)} collective-permute-done((bf16[656,128]{1,0:T(8,128)(2,1)S(1)}, bf16[656,128]{1,0:T(8,128)(2,1)S(1)}, u32[]{:S(2)}, u32[]{:S(2)}) %collective-permute-start.1) | collective-permute-done | bytes 167968 | tf_op jit(solution)/shard_map/ppermute | solution.py:392
  15.8 3.1 %collective-permute-done.2.refs_3_ = bf16[656,128]{1,0:T(8,128)(2,1)S(1)} collective-permute-done((bf16[656,128]{1,0:T(8,128)(2,1)S(1)}, bf16[656,128]{1,0:T(8,128)(2,1)S(1)}, u32[]{:S(2)}, u32[]{:S(2)}) %collective-permute-start.2) | collective-permute-done | bytes 167968 | tf_op jit(solution)/shard_map/ppermute | solution.py:392
  19.6 3.2 %collective-permute-start.6 = (bf16[1920,128]{1,0:T(8,128)(2,1)S(1)}, bf16[1920,128]{1,0:T(8,128)(2,1)S(1)}, u32[]{:S(2)}, u32[]{:S(2)}) collective-permute-start(bf16[1920,128]{1,0:T(8,128)(2,1)S(1)} %get-tuple-element.42), channel_id=1, source_target_pairs={{0,4},{1,5},{2,6},{3,7},{4,0},{5,1},{6,2},{7,3},{8,12},{9,13},{10,... | collective-permute-start | bytes 1474568 | tf_op jit(solution)/shard_map/ppermute | solution.py:395
  23.7 1.6 %collective-permute-start.4 = (f16[256,512]{1,0:T(8,128)(2,1)S(1)}, f16[256,512]{1,0:T(8,128)(2,1)S(1)}, u32[]{:S(2)}, u32[]{:S(2)}) collective-permute-start(f16[256,512]{1,0:T(8,128)(2,1)S(1)} %fusion.4), channel_id=1, source_target_pairs={{0,2},{1,3},{2,0},{3,1},{4,6},{5,7},{6,4},{7,5},{8,10},{9,11},{10,... | collective-permute-start | bytes 786440 | tf_op jit(solution)/shard_map/ppermute | solution.py:399
  25.3 0.5 collective-permute-start.5
  25.8 0.8 %energies.1 = (f32[2,128,128]{2,1,0:T(8,128)S(1)}, f32[2,3,4,128]{3,2,1,0:T(4,128)S(1)}) custom-call(s32[2,3]{1,0:T(2,128)S(1)} %copy-done.1, f32[4,8]{1,0:T(4,128)S(1)} %bitcast.25, s32[8,128]{1,0:T(8,128)S(1)} %copy-done.2, f32[8,128]{1,0:T(8,128)S(1)} %bitcast.24), custom_call_target="tpu_custom_call" | custom-call | tf_op jit(solution)/shard_map/energies/pallas_call | solution.py:371
  26.6 6.1 %collective-permute-done.5.top_ref = f32[8,512]{1,0:T(8,128)S(1)} collective-permute-done((f32[8,512]{1,0:T(8,128)S(1)}, f32[8,512]{1,0:T(8,128)S(1)}, u32[]{:S(2)}, u32[]{:S(2)}) %collective-permute-start.5) | collective-permute-done | bytes 16416 | tf_op jit(solution)/shard_map/ppermute | solution.py:399
  32.9 1.7 %collective-permute-done.6.refs_6_ = bf16[1920,128]{1,0:T(8,128)(2,1)S(1)} collective-permute-done((bf16[1920,128]{1,0:T(8,128)(2,1)S(1)}, bf16[1920,128]{1,0:T(8,128)(2,1)S(1)}, u32[]{:S(2)}, u32[]{:S(2)}) %collective-permute-start.6) | collective-permute-done | bytes 491552 | tf_op jit(solution)/shard_map/ppermute | solution.py:395
  34.6 0.6 near.2
  35.2 1.4 %near.3 = (f32[384,512]{1,0:T(8,128)S(1)}, f32[384,512]{1,0:T(8,128)S(1)}, f32[384,512]{1,0:T(8,128)S(1)}, f32[384,512]{1,0:T(8,128)S(1)}) custom-call(s32[2,3]{1,0:T(2,128)S(1)} %copy-done.1, bf16[656,128]{1,0:T(8,128)(2,1)S(1)} %get-tuple-element.44.refs_0_, bf16[656,128]{1,0:T(8,128)(2,1)S(1)} %collective-permute-done.refs_1_, ...), custom_call_target="tpu_custom_call" | custom-call | tf_op jit(solution)/shard_map/near/pallas_call | solution.py:206
  37.2 1.5 %collective-permute-start.13 = (f16[128,512]{1,0:T(8,128)(2,1)S(1)}, f16[128,512]{1,0:T(8,128)(2,1)S(1)}, u32[]{:S(2)}, u32[]{:S(2)}) collective-permute-start(f16[128,512]{1,0:T(8,128)(2,1)S(1)} %multiply_convert_fusion.1), channel_id=1, source_target_pairs={{0,2},{1,3},{2,0},{3,1},{4,6},{5,7},{6,4},{7,5},{8,10},{9,11},{10,... | collective-permute-start | bytes 393224 | tf_op jit(solution)/shard_map/ppermute | solution.py:399
  39.4 1.5 %collective-permute-start.11 = (f16[384,512]{1,0:T(8,128)(2,1)S(1)}, f16[384,512]{1,0:T(8,128)(2,1)S(1)}, u32[]{:S(2)}, u32[]{:S(2)}) collective-permute-start(f16[384,512]{1,0:T(8,128)(2,1)S(1)} %multiply_convert_fusion), channel_id=1, source_target_pairs={{0,2},{1,3},{2,0},{3,1},{4,6},{5,7},{6,4},{7,5},{8,10},{9,11},{10,... | collective-permute-start | bytes 1179656 | tf_op jit(solution)/shard_map/ppermute | solution.py:399
  41.0 0.9 %finish.2 = (f32[2,3,128,512]{3,2,1,0:T(8,128)}, f32[2,4,128]{2,1,0:T(4,128)S(1)}) custom-call(f32[256,512]{1,0:T(8,128)S(1)} %fusion.1.total_ref, f32[2,128,128]{2,1,0:T(8,128)S(1)} %get-tuple-element.50.row_ref, f32[2,3,4,128]{3,2,1,0:T(4,128)S(1)} %get-tuple-element.65.col_ref), custom_call_target="tpu_custom_call" | custom-call | tf_op jit(solution)/shard_map/finish/pallas_call | solution.py:271
  41.9 1.2 %collective-permute-done.13 = f16[128,512]{1,0:T(8,128)(2,1)S(1)} collective-permute-done((f16[128,512]{1,0:T(8,128)(2,1)S(1)}, f16[128,512]{1,0:T(8,128)(2,1)S(1)}, u32[]{:S(2)}, u32[]{:S(2)}) %collective-permute-start.13) | collective-permute-done | bytes 131104 | tf_op jit(solution)/shard_map/ppermute | solution.py:399
  43.2 0.8 %finish.3 = (f32[2,3,128,512]{3,2,1,0:T(8,128)}, f32[1,4,128]{2,1,0:T(4,128)S(1)}) custom-call(f32[128,512]{1,0:T(8,128)S(1)} %multiply_add_fusion.1.total_ref, f32[2,128,128]{2,1,0:T(8,128)S(1)} %get-tuple-element.50.row_ref, f32[2,3,4,128]{3,2,1,0:T(4,128)S(1)} %get-tuple-element.65.col_ref, ...), custom_call_target="tpu_custom_call", output_to_operand_aliasing={{0}: (3, {})} | custom-call | tf_op jit(solution)/shard_map/finish/pallas_call | solution.py:271
  44.0 7.2 %collective-permute-done.11 = f16[384,512]{1,0:T(8,128)(2,1)S(1)} collective-permute-done((f16[384,512]{1,0:T(8,128)(2,1)S(1)}, f16[384,512]{1,0:T(8,128)(2,1)S(1)}, u32[]{:S(2)}, u32[]{:S(2)}) %collective-permute-start.11) | collective-permute-done | bytes 393248 | tf_op jit(solution)/shard_map/ppermute | solution.py:399
  51.7 0.9 %collective-permute-start.16 = (f32[2,3,4,4]{3,2,1,0:T(4,128)S(1)}, f32[2,3,4,4]{3,2,1,0:T(4,128)S(1)}, u32[]{:S(2)}, u32[]{:S(2)}) collective-permute-start(f32[2,3,4,4]{3,2,1,0:T(4,128)S(1)} %get-tuple-element.73.refs_0_), channel_id=1, source_target_pairs={{0,3},{1,2},{2,1},{3,0},{4,7},{5,6},{6,5},{7,4},{8,11},{9,10},{10,... | collective-permute-start | bytes 1160 | tf_op jit(solution)/shard_map/ppermute | solution.py:432
  52.6 0.7 %collective-permute-start.15 = (f32[2,3,4,4]{3,2,1,0:T(4,128)S(1)}, f32[2,3,4,4]{3,2,1,0:T(4,128)S(1)}, u32[]{:S(2)}, u32[]{:S(2)}) collective-permute-start(f32[2,3,4,4]{3,2,1,0:T(4,128)S(1)} %get-tuple-element.73.refs_0_), channel_id=1, source_target_pairs={{0,2},{1,3},{2,0},{3,1},{4,6},{5,7},{6,4},{7,5},{8,10},{9,11},{10,... | collective-permute-start | bytes 1160 | tf_op jit(solution)/shard_map/ppermute | solution.py:432
  53.6 0.9 %put.1 = f32[2,3,128,512]{3,2,1,0:T(8,128)} custom-call(f32[3,128,512]{2,1,0:T(8,128)S(1)} %get-tuple-element.71.values_ref, f32[2,3,128,512]{3,2,1,0:T(8,128)} %get-tuple-element.72._), custom_call_target="tpu_custom_call", output_to_operand_aliasing={{}: (1, {})} | custom-call | tf_op jit(solution)/shard_map/put/pallas_call | solution.py:322
  55.0 1.3 %collective-permute-done.15.refs_2_ = f32[2,3,4,4]{3,2,1,0:T(4,128)S(1)} collective-permute-done((f32[2,3,4,4]{3,2,1,0:T(4,128)S(1)}, f32[2,3,4,4]{3,2,1,0:T(4,128)S(1)}, u32[]{:S(2)}, u32[]{:S(2)}) %collective-permute-start.15) | collective-permute-done | bytes 416 | tf_op jit(solution)/shard_map/ppermute | solution.py:432
  56.3 0.6 %last.1 = f32[2,3,4,4]{3,2,1,0:T(4,128)} custom-call(f32[2,3,4,4]{3,2,1,0:T(4,128)S(1)} %get-tuple-element.73.refs_0_, f32[2,3,4,4]{3,2,1,0:T(4,128)S(1)} %collective-permute-done.14.refs_1_, f32[2,3,4,4]{3,2,1,0:T(4,128)S(1)} %collective-permute-done.15.refs_2_, f32[2,3,4,4]{3,2,1,0:T(4,128)S(1)} %collective-permute-done.16.refs_3_), custom_call_target="tpu_custom_call" | custom-call | tf_op jit(solution)/shard_map/last/pallas_call | solution.py:337
  (47 shorter events, 4.5 us)
Async XLA Ops:
  2.1 13.6 %collective-permute-start.1 = (bf16[656,128]{1,0:T(8,128)(2,1)S(1)}, bf16[656,128]{1,0:T(8,128)(2,1)S(1)}, u32[]{:S(2)}, u32[]{:S(2)}) collective-permute-start(bf16[656,128]{1,0:T(8,128)(2,1)S(1)} %get-tuple-element.40), channel_id=1, source_target_pairs={{0,8},{4,12},{8,0},{12,4},{1,9},{5,13},{9,1},{13,5},{2,10},{6,14},... | collective-permute-start | bytes 503816 | tf_op jit(solution)/shard_map/ppermute | solution.py:392
  6.2 9.5 %collective-permute-start = (bf16[656,128]{1,0:T(8,128)(2,1)S(1)}, bf16[656,128]{1,0:T(8,128)(2,1)S(1)}, u32[]{:S(2)}, u32[]{:S(2)}) collective-permute-start(bf16[656,128]{1,0:T(8,128)(2,1)S(1)} %get-tuple-element.53.refs_4_), channel_id=1, source_target_pairs={{0,4},{4,0},{8,12},{12,8},{1,5},{5,1},{9,13},{13,9},{2,6},{6,2},{1... | collective-permute-start | bytes 503816 | tf_op jit(solution)/shard_map/ppermute | solution.py:392
  7.8 11.1 %collective-permute-start.2 = (bf16[656,128]{1,0:T(8,128)(2,1)S(1)}, bf16[656,128]{1,0:T(8,128)(2,1)S(1)}, u32[]{:S(2)}, u32[]{:S(2)}) collective-permute-start(bf16[656,128]{1,0:T(8,128)(2,1)S(1)} %get-tuple-element.41.refs_5_), channel_id=1, source_target_pairs={{0,12},{4,8},{8,4},{12,0},{1,13},{5,9},{9,5},{13,1},{2,14},{6,10},... | collective-permute-start | bytes 503816 | tf_op jit(solution)/shard_map/ppermute | solution.py:392
  19.5 3.9 %collective-permute-start.3 = (f32[2,264,512]{2,1,0:T(8,128)S(1)}, f32[2,264,512]{2,1,0:T(8,128)S(1)}, u32[]{:S(2)}, u32[]{:S(2)}) collective-permute-start(f32[2,264,512]{2,1,0:T(8,128)S(1)} %get-tuple-element.46), channel_id=1, source_target_pairs={{0,1},{1,0},{2,3},{3,2},{4,5},{5,4},{6,7},{7,6},{8,9},{9,8},{10,11... | collective-permute-start | bytes 3244040 | tf_op jit(solution)/shard_map/ppermute | solution.py:399
  19.6 15.0 %collective-permute-start.6 = (bf16[1920,128]{1,0:T(8,128)(2,1)S(1)}, bf16[1920,128]{1,0:T(8,128)(2,1)S(1)}, u32[]{:S(2)}, u32[]{:S(2)}) collective-permute-start(bf16[1920,128]{1,0:T(8,128)(2,1)S(1)} %get-tuple-element.42), channel_id=1, source_target_pairs={{0,4},{1,5},{2,6},{3,7},{4,0},{5,1},{6,2},{7,3},{8,12},{9,13},{10,... | collective-permute-start | bytes 1474568 | tf_op jit(solution)/shard_map/ppermute | solution.py:395
  22.8 11.8 %collective-permute-start.7 = (bf16[1920,128]{1,0:T(8,128)(2,1)S(1)}, bf16[1920,128]{1,0:T(8,128)(2,1)S(1)}, u32[]{:S(2)}, u32[]{:S(2)}) collective-permute-start(bf16[1920,128]{1,0:T(8,128)(2,1)S(1)} %get-tuple-element.43), channel_id=1, source_target_pairs={{0,1},{1,0},{2,3},{3,2},{4,8},{5,9},{6,10},{7,11},{8,4},{9,5},{10,... | collective-permute-start | bytes 1474568 | tf_op jit(solution)/shard_map/ppermute | solution.py:395
  23.4 2.4 %copy-start.1 = (s32[2,3]{1,0:T(2,128)S(1)}, s32[2,3]{1,0:T(2,128)}, u32[]{:S(2)}) copy-start(s32[2,3]{1,0:T(2,128)} %partners_ref.5) | copy-start | bytes 76
  23.4 2.4 %copy-start.2 = (s32[8,128]{1,0:T(8,128)S(1)}, s32[8,128]{1,0:T(8,128)}, u32[]{:S(2)}) copy-start(s32[8,128]{1,0:T(8,128)} %domains_ref.1) | copy-start | bytes 12292
  23.4 2.4 %copy-start.3 = (f32[1024]{0:T(1024)S(1)}, f32[1024]{0:T(1024)}, u32[]{:S(2)}) copy-start(f32[1024]{0:T(1024)} %param.9) | copy-start | bytes 12292
  23.5 2.4 %copy-start.4 = (f32[8,4]{0,1:T(4,128)S(1)}, f32[8,4]{0,1:T(4,128)}, u32[]{:S(2)}) copy-start(f32[8,4]{0,1:T(4,128)} %param.8) | copy-start | bytes 388
  23.7 9.1 %collective-permute-start.4 = (f16[256,512]{1,0:T(8,128)(2,1)S(1)}, f16[256,512]{1,0:T(8,128)(2,1)S(1)}, u32[]{:S(2)}, u32[]{:S(2)}) collective-permute-start(f16[256,512]{1,0:T(8,128)(2,1)S(1)} %fusion.4), channel_id=1, source_target_pairs={{0,2},{1,3},{2,0},{3,1},{4,6},{5,7},{6,4},{7,5},{8,10},{9,11},{10,... | collective-permute-start | bytes 786440 | tf_op jit(solution)/shard_map/ppermute | solution.py:399
  25.3 7.4 %collective-permute-start.5 = (f32[8,512]{1,0:T(8,128)S(1)}, f32[8,512]{1,0:T(8,128)S(1)}, u32[]{:S(2)}, u32[]{:S(2)}) collective-permute-start(f32[8,512]{1,0:T(8,128)S(1)} %get-tuple-element.49), channel_id=1, source_target_pairs={{0,2},{1,3},{2,0},{3,1},{4,6},{5,7},{6,4},{7,5},{8,10},{9,11},{10,... | collective-permute-start | bytes 49160 | tf_op jit(solution)/shard_map/ppermute | solution.py:399
  32.8 4.4 %copy-start = (f32[8,512]{1,0:T(8,128)}, f32[8,512]{1,0:T(8,128)S(1)}, u32[]{:S(2)}) copy-start(f32[8,512]{1,0:T(8,128)S(1)} %scale_up.1) | copy-start | bytes 49156
  35.1 1.6 %collective-permute-start.8 = (f32[128,512]{1,0:T(8,128)S(1)}, f32[128,512]{1,0:T(8,128)S(1)}, u32[]{:S(2)}, u32[]{:S(2)}) collective-permute-start(f32[128,512]{1,0:T(8,128)S(1)} %get-tuple-element.57), channel_id=1, source_target_pairs={{0,1},{1,0},{2,3},{3,2},{4,5},{5,4},{6,7},{7,6},{8,9},{9,8},{10,11... | collective-permute-start | bytes 786440 | tf_op jit(solution)/shard_map/ppermute | solution.py:399
  36.8 2.4 %collective-permute-start.10 = (f32[384,512]{1,0:T(8,128)S(1)}, f32[384,512]{1,0:T(8,128)S(1)}, u32[]{:S(2)}, u32[]{:S(2)}) collective-permute-start(f32[384,512]{1,0:T(8,128)S(1)} %get-tuple-element.61), channel_id=1, source_target_pairs={{0,1},{1,0},{2,3},{3,2},{4,5},{5,4},{6,7},{7,6},{8,9},{9,8},{10,11... | collective-permute-start | bytes 2359304 | tf_op jit(solution)/shard_map/ppermute | solution.py:399
  37.2 3.7 %slice-start = ((f32[8,512]{1,0:T(8,128)}), f32[1,512]{1,0:T(1,128)S(1)}, s32[]{:S(2)}) async-start(f32[8,512]{1,0:T(8,128)} %copy-done), calls=%async_computation | async-start | bytes 4096 | tf_op jit(solution)/shard_map/slice | solution.py:427
  37.2 5.9 %collective-permute-start.13 = (f16[128,512]{1,0:T(8,128)(2,1)S(1)}, f16[128,512]{1,0:T(8,128)(2,1)S(1)}, u32[]{:S(2)}, u32[]{:S(2)}) collective-permute-start(f16[128,512]{1,0:T(8,128)(2,1)S(1)} %multiply_convert_fusion.1), channel_id=1, source_target_pairs={{0,2},{1,3},{2,0},{3,1},{4,6},{5,7},{6,4},{7,5},{8,10},{9,11},{10,... | collective-permute-start | bytes 393224 | tf_op jit(solution)/shard_map/ppermute | solution.py:399
  38.7 4.4 %collective-permute-start.12 = (f32[128,512]{1,0:T(8,128)S(1)}, f32[128,512]{1,0:T(8,128)S(1)}, u32[]{:S(2)}, u32[]{:S(2)}) collective-permute-start(f32[128,512]{1,0:T(8,128)S(1)} %get-tuple-element.63), channel_id=1, source_target_pairs={{0,1},{1,0},{2,3},{3,2},{4,5},{5,4},{6,7},{7,6},{8,9},{9,8},{10,11... | collective-permute-start | bytes 786440 | tf_op jit(solution)/shard_map/ppermute | solution.py:399
  38.7 5.3 %collective-permute-start.9 = (f32[384,512]{1,0:T(8,128)S(1)}, f32[384,512]{1,0:T(8,128)S(1)}, u32[]{:S(2)}, u32[]{:S(2)}) collective-permute-start(f32[384,512]{1,0:T(8,128)S(1)} %get-tuple-element.58), channel_id=1, source_target_pairs={{0,1},{1,0},{2,3},{3,2},{4,5},{5,4},{6,7},{7,6},{8,9},{9,8},{10,11... | collective-permute-start | bytes 2359304 | tf_op jit(solution)/shard_map/ppermute | solution.py:399
  39.4 11.8 %collective-permute-start.11 = (f16[384,512]{1,0:T(8,128)(2,1)S(1)}, f16[384,512]{1,0:T(8,128)(2,1)S(1)}, u32[]{:S(2)}, u32[]{:S(2)}) collective-permute-start(f16[384,512]{1,0:T(8,128)(2,1)S(1)} %multiply_convert_fusion), channel_id=1, source_target_pairs={{0,2},{1,3},{2,0},{3,1},{4,6},{5,7},{6,4},{7,5},{8,10},{9,11},{10,... | collective-permute-start | bytes 1179656 | tf_op jit(solution)/shard_map/ppermute | solution.py:399
  43.2 8.0 %slice-start.2 = ((f32[8,512]{1,0:T(8,128)}), f32[1,512]{1,0:T(1,128)S(1)}, s32[]{:S(2)}) async-start(f32[8,512]{1,0:T(8,128)} %copy-done), calls=%async_computation.2 | async-start | bytes 4096 | tf_op jit(solution)/shard_map/slice | solution.py:427
  51.7 3.2 %collective-permute-start.16 = (f32[2,3,4,4]{3,2,1,0:T(4,128)S(1)}, f32[2,3,4,4]{3,2,1,0:T(4,128)S(1)}, u32[]{:S(2)}, u32[]{:S(2)}) collective-permute-start(f32[2,3,4,4]{3,2,1,0:T(4,128)S(1)} %get-tuple-element.73.refs_0_), channel_id=1, source_target_pairs={{0,3},{1,2},{2,1},{3,0},{4,7},{5,6},{6,5},{7,4},{8,11},{9,10},{10,... | collective-permute-start | bytes 1160 | tf_op jit(solution)/shard_map/ppermute | solution.py:432
  52.6 3.7 %collective-permute-start.15 = (f32[2,3,4,4]{3,2,1,0:T(4,128)S(1)}, f32[2,3,4,4]{3,2,1,0:T(4,128)S(1)}, u32[]{:S(2)}, u32[]{:S(2)}) collective-permute-start(f32[2,3,4,4]{3,2,1,0:T(4,128)S(1)} %get-tuple-element.73.refs_0_), channel_id=1, source_target_pairs={{0,2},{1,3},{2,0},{3,1},{4,6},{5,7},{6,4},{7,5},{8,10},{9,11},{10,... | collective-permute-start | bytes 1160 | tf_op jit(solution)/shard_map/ppermute | solution.py:432
  53.3 3.0 %collective-permute-start.14 = (f32[2,3,4,4]{3,2,1,0:T(4,128)S(1)}, f32[2,3,4,4]{3,2,1,0:T(4,128)S(1)}, u32[]{:S(2)}, u32[]{:S(2)}) collective-permute-start(f32[2,3,4,4]{3,2,1,0:T(4,128)S(1)} %get-tuple-element.73.refs_0_), channel_id=1, source_target_pairs={{0,1},{1,0},{2,3},{3,2},{4,5},{5,4},{6,7},{7,6},{8,9},{9,8},{10,11... | collective-permute-start | bytes 1160 | tf_op jit(solution)/shard_map/ppermute | solution.py:432
  (1 other events, 2.2 us)

commit v8 on v7

--- a/solution.py
+++ b/solution.py
@@ -158,12 +158,29 @@
     )(*own)
 
 
-def near_pairs(partners, own, here, sides, orbitals, groups):
+def turn(own, orbitals):
+    count, domain = len(own), own[0].shape[1]
+    depth = depth_of(own[0], orbitals)
+
+    def kernel(*refs):
+        for r in range(2):
+            refs[-1][r] = left_rows(refs[:count], depth, r).T
+
+    return call(
+        kernel,
+        "turn",
+        out_shape=shape(2, orbitals * domain, count * depth, dtype=BF16),
+        in_specs=[VMEM] * count,
+        out_specs=VMEM,
+    )(*own)
+
+
+def near_pairs(partners, turned, own, here, sides, orbitals, groups):
     count, domain = len(own), own[0].shape[1]
     depth = depth_of(own[0], orbitals)
     rows, wide = 2 * orbitals * depth, orbitals * domain
 
-    def kernel(partners_ref, *refs):
+    def kernel(partners_ref, turned_ref, *refs):
         own_refs, here_refs, side_refs = refs[:count], refs[count : count + 2], refs[count + 2 :][:2]
         outs = refs[count + 4 :]
         z = lax.axis_index("aux")
@@ -196,7 +213,7 @@
             for t, (r, slot) in enumerate(tiles):
                 w = partners_ref[r : r + 1, slot : slot + 1] - 2 * z + 2
                 right = jnp.concatenate([panels(r, j, slot, w) for j in range(orbitals)], axis=1)
-                sums = product(left_rows(own_refs, depth, r), right)
+                sums = jnp.dot(turned_ref[r], right, preferred_element_type=F32)
                 at = slice(t * domain, (t + 1) * domain)
                 store_sums(sums, at, *outs[4 * n : 4 * n + 4])
 
@@ -207,9 +224,9 @@
         kernel,
         "near",
         out_shape=shapes,
-        in_specs=[VMEM] * (count + 5),
+        in_specs=[VMEM] * (count + 6),
         out_specs=[VMEM] * len(shapes),
-    )(partners, *own, *here, *sides)
+    )(partners, turned, *own, *here, *sides)
 
 
 def scale_down(peak, got, depth):
@@ -408,9 +425,10 @@
     here[0] = after(here[0], parts[0][2], from_half, row_vals)
 
     groups = [[(0, 0), (1, 0)], *GROUPS[0], *GROUPS[1]]
-    sums = near_pairs(partners, own, here, near, orbitals, GROUPS[0])
+    turned = turn(own, orbitals)
+    sums = near_pairs(partners, turned, own, here, near, orbitals, GROUPS[0])
     here[0] = after(here[0], sums[0])
-    sums += near_pairs(partners, own, here, near, orbitals, GROUPS[1])
+    sums += near_pairs(partners, turned, own, here, near, orbitals, GROUPS[1])
     mine_a, other_a, give_a, on_a, mine_b, other_b, give_b, on_b = sums
     half_a = ((other_a + across(on_a, swap)) * to_half[:1]).astype(F16)
     x_a = across(half_a, cross)

time: 57.1 us -> 57 us (level)
    pallas_call x2 -> x3, Pallas kernels: 1.93 us -> 2.15 us  [the longest x2 1.87 us: near_pairs(): call(kernel, 'near', out_shape=shapes, in_specs=[VMEM] * (count + 6), out...]
  transfers between devices with their start and end apart: 17 -> 17, of which waited for: 9 -> 9; matrix products, arithmetic and copies ran while one was open for 1% -> 1% of each run, Pallas kernels for 9% -> 10%
where the time goes in v8:
time: 57 us; the launch traced here: 56.8 us
  waiting for transfers between devices  29 us (51%)
  starting transfers between devices  17 us (30%)
  Pallas kernels  9.09 us (16%)
  between operations  0.86 us (2%)
  other arithmetic  0.78 us (1%)
    ppermute x9, waiting for transfers between devices, across(): return lax.ppermute(sums, 'pair', axis_pairs)  14.5 us
    ppermute x3, waiting for transfers between devices, fast(): own.append(lax.ppermute(send, 'aux', [(i, i ^ k) for i in range(count)]))  11.1 us
    ppermute x9, starting transfers between devices, across(): return lax.ppermute(sums, 'pair', axis_pairs)  6.13 us
    ppermute x3, starting transfers between devices, fast(): own.append(lax.ppermute(send, 'aux', [(i, i ^ k) for i in range(count)]))  5.67 us
    ppermute x2, starting transfers between devices, fast(): lax.ppermute(m, ('aux', 'pair'), side)  3.34 us
    ppermute x3, starting transfers between devices, fast(): others = [lax.ppermute(share, 'pair', to) for to in (swap, cross, both)]  1.9 us
    pallas_call x2, Pallas kernels, near_pairs(): call(kernel, 'near', out_shape=shapes, in_specs=[VMEM] * (count + 6), out...  1.87 us
    ppermute x2, waiting for transfers between devices, fast(): lax.ppermute(m, ('aux', 'pair'), side)  1.72 us
  transfers between devices with their start and end apart: 17, of which 9 were waited for; matrix products, arithmetic and copies ran while one was open for 1% of the time, Pallas kernels for 10%

profile of v8, /device:TPU:0, one launch (start us, length us, event | category | flops | bytes accessed | tf_op | source)
XLA Modules:
  0.0 56.8 jit_solution(7298983998638959618)
XLA Ops:
  0.6 1.5 %pack.1 = (bf16[656,128]{1,0:T(8,128)(2,1)S(1)}, bf16[656,128]{1,0:T(8,128)(2,1)S(1)}, bf16[656,128]{1,0:T(8,128)(2,1)S(1)}, bf16[656,128]{1,0:T(8,128)(2,1)S(1)}) custom-call(bf16[80,32,128]{2,1,0:T(8,128)(2,1)} %bitcast.26), custom_call_target="tpu_custom_call" | custom-call | tf_op jit(solution)/shard_map/pack/pallas_call | solution.py:67
  2.1 4.1 %collective-permute-start.1 = (bf16[656,128]{1,0:T(8,128)(2,1)S(1)}, bf16[656,128]{1,0:T(8,128)(2,1)S(1)}, u32[]{:S(2)}, u32[]{:S(2)}) collective-permute-start(bf16[656,128]{1,0:T(8,128)(2,1)S(1)} %get-tuple-element.40), channel_id=1, source_target_pairs={{0,8},{4,12},{8,0},{12,4},{1,9},{5,13},{9,1},{13,5},{2,10},{6,14},... | collective-permute-start | bytes 503816 | tf_op jit(solution)/shard_map/ppermute | solution.py:409
  6.2 1.6 %collective-permute-start = (bf16[656,128]{1,0:T(8,128)(2,1)S(1)}, bf16[656,128]{1,0:T(8,128)(2,1)S(1)}, u32[]{:S(2)}, u32[]{:S(2)}) collective-permute-start(bf16[656,128]{1,0:T(8,128)(2,1)S(1)} %get-tuple-element.53.refs_4_), channel_id=1, source_target_pairs={{0,4},{4,0},{8,12},{12,8},{1,5},{5,1},{9,13},{13,9},{2,6},{6,2},{1... | collective-permute-start | bytes 503816 | tf_op jit(solution)/shard_map/ppermute | solution.py:409
  7.8 8.0 %collective-permute-done.1.refs_2_ = bf16[656,128]{1,0:T(8,128)(2,1)S(1)} collective-permute-done((bf16[656,128]{1,0:T(8,128)(2,1)S(1)}, bf16[656,128]{1,0:T(8,128)(2,1)S(1)}, u32[]{:S(2)}, u32[]{:S(2)}) %collective-permute-start.1) | collective-permute-done | bytes 167968 | tf_op jit(solution)/shard_map/ppermute | solution.py:409
  15.8 3.1 %collective-permute-done.2.refs_3_ = bf16[656,128]{1,0:T(8,128)(2,1)S(1)} collective-permute-done((bf16[656,128]{1,0:T(8,128)(2,1)S(1)}, bf16[656,128]{1,0:T(8,128)(2,1)S(1)}, u32[]{:S(2)}, u32[]{:S(2)}) %collective-permute-start.2) | collective-permute-done | bytes 167968 | tf_op jit(solution)/shard_map/ppermute | solution.py:409
  19.6 3.2 %collective-permute-start.6 = (bf16[1920,128]{1,0:T(8,128)(2,1)S(1)}, bf16[1920,128]{1,0:T(8,128)(2,1)S(1)}, u32[]{:S(2)}, u32[]{:S(2)}) collective-permute-start(bf16[1920,128]{1,0:T(8,128)(2,1)S(1)} %get-tuple-element.42), channel_id=1, source_target_pairs={{0,4},{1,5},{2,6},{3,7},{4,0},{5,1},{6,2},{7,3},{8,12},{9,13},{10,... | collective-permute-start | bytes 1474568 | tf_op jit(solution)/shard_map/ppermute | solution.py:412
  23.7 1.6 %collective-permute-start.4 = (f16[256,512]{1,0:T(8,128)(2,1)S(1)}, f16[256,512]{1,0:T(8,128)(2,1)S(1)}, u32[]{:S(2)}, u32[]{:S(2)}) collective-permute-start(f16[256,512]{1,0:T(8,128)(2,1)S(1)} %fusion.4), channel_id=1, source_target_pairs={{0,2},{1,3},{2,0},{3,1},{4,6},{5,7},{6,4},{7,5},{8,10},{9,11},{10,... | collective-permute-start | bytes 786440 | tf_op jit(solution)/shard_map/ppermute | solution.py:416
  25.3 0.5 collective-permute-start.5
  25.8 0.8 %energies.1 = (f32[2,128,128]{2,1,0:T(8,128)S(1)}, f32[2,3,4,128]{3,2,1,0:T(4,128)S(1)}) custom-call(s32[2,3]{1,0:T(2,128)S(1)} %copy-done.1, f32[4,8]{1,0:T(4,128)S(1)} %bitcast.25, s32[8,128]{1,0:T(8,128)S(1)} %copy-done.2, f32[8,128]{1,0:T(8,128)S(1)} %bitcast.24), custom_call_target="tpu_custom_call" | custom-call | tf_op jit(solution)/shard_map/energies/pallas_call | solution.py:388
  26.9 5.8 %collective-permute-done.5.top_ref = f32[8,512]{1,0:T(8,128)S(1)} collective-permute-done((f32[8,512]{1,0:T(8,128)S(1)}, f32[8,512]{1,0:T(8,128)S(1)}, u32[]{:S(2)}, u32[]{:S(2)}) %collective-permute-start.5) | collective-permute-done | bytes 16416 | tf_op jit(solution)/shard_map/ppermute | solution.py:416
  32.9 1.7 %collective-permute-done.6.refs_6_ = bf16[1920,128]{1,0:T(8,128)(2,1)S(1)} collective-permute-done((bf16[1920,128]{1,0:T(8,128)(2,1)S(1)}, bf16[1920,128]{1,0:T(8,128)(2,1)S(1)}, u32[]{:S(2)}, u32[]{:S(2)}) %collective-permute-start.6) | collective-permute-done | bytes 491552 | tf_op jit(solution)/shard_map/ppermute | solution.py:412
  34.6 0.6 near.2
  35.2 1.3 %near.3 = (f32[384,512]{1,0:T(8,128)S(1)}, f32[384,512]{1,0:T(8,128)S(1)}, f32[384,512]{1,0:T(8,128)S(1)}, f32[384,512]{1,0:T(8,128)S(1)}) custom-call(s32[2,3]{1,0:T(2,128)S(1)} %copy-done.1, bf16[2,512,320]{2,1,0:T(8,128)(2,1)S(1)} %turn.1.turned_ref, bf16[656,128]{1,0:T(8,128)(2,1)S(1)} %get-tuple-element.44.refs_0_, ...), custom_call_target="tpu_custom_call" | custom-call | tf_op jit(solution)/shard_map/near/pallas_call | solution.py:223
  37.2 1.5 %collective-permute-start.13 = (f16[128,512]{1,0:T(8,128)(2,1)S(1)}, f16[128,512]{1,0:T(8,128)(2,1)S(1)}, u32[]{:S(2)}, u32[]{:S(2)}) collective-permute-start(f16[128,512]{1,0:T(8,128)(2,1)S(1)} %multiply_convert_fusion.1), channel_id=1, source_target_pairs={{0,2},{1,3},{2,0},{3,1},{4,6},{5,7},{6,4},{7,5},{8,10},{9,11},{10,... | collective-permute-start | bytes 393224 | tf_op jit(solution)/shard_map/ppermute | solution.py:416
  39.4 1.5 %collective-permute-start.11 = (f16[384,512]{1,0:T(8,128)(2,1)S(1)}, f16[384,512]{1,0:T(8,128)(2,1)S(1)}, u32[]{:S(2)}, u32[]{:S(2)}) collective-permute-start(f16[384,512]{1,0:T(8,128)(2,1)S(1)} %multiply_convert_fusion), channel_id=1, source_target_pairs={{0,2},{1,3},{2,0},{3,1},{4,6},{5,7},{6,4},{7,5},{8,10},{9,11},{10,... | collective-permute-start | bytes 1179656 | tf_op jit(solution)/shard_map/ppermute | solution.py:416
  41.0 0.9 %finish.2 = (f32[2,3,128,512]{3,2,1,0:T(8,128)}, f32[2,4,128]{2,1,0:T(4,128)S(1)}) custom-call(f32[256,512]{1,0:T(8,128)S(1)} %fusion.1.total_ref, f32[2,128,128]{2,1,0:T(8,128)S(1)} %get-tuple-element.50.row_ref, f32[2,3,4,128]{3,2,1,0:T(4,128)S(1)} %get-tuple-element.65.col_ref), custom_call_target="tpu_custom_call" | custom-call | tf_op jit(solution)/shard_map/finish/pallas_call | solution.py:288
  41.9 1.3 %collective-permute-done.13 = f16[128,512]{1,0:T(8,128)(2,1)S(1)} collective-permute-done((f16[128,512]{1,0:T(8,128)(2,1)S(1)}, f16[128,512]{1,0:T(8,128)(2,1)S(1)}, u32[]{:S(2)}, u32[]{:S(2)}) %collective-permute-start.13) | collective-permute-done | bytes 131104 | tf_op jit(solution)/shard_map/ppermute | solution.py:416
  43.3 0.8 %finish.3 = (f32[2,3,128,512]{3,2,1,0:T(8,128)}, f32[1,4,128]{2,1,0:T(4,128)S(1)}) custom-call(f32[128,512]{1,0:T(8,128)S(1)} %multiply_add_fusion.1.total_ref, f32[2,128,128]{2,1,0:T(8,128)S(1)} %get-tuple-element.50.row_ref, f32[2,3,4,128]{3,2,1,0:T(4,128)S(1)} %get-tuple-element.65.col_ref, ...), custom_call_target="tpu_custom_call", output_to_operand_aliasing={{0}: (3, {})} | custom-call | tf_op jit(solution)/shard_map/finish/pallas_call | solution.py:288
  44.1 7.1 %collective-permute-done.11 = f16[384,512]{1,0:T(8,128)(2,1)S(1)} collective-permute-done((f16[384,512]{1,0:T(8,128)(2,1)S(1)}, f16[384,512]{1,0:T(8,128)(2,1)S(1)}, u32[]{:S(2)}, u32[]{:S(2)}) %collective-permute-start.11) | collective-permute-done | bytes 393248 | tf_op jit(solution)/shard_map/ppermute | solution.py:416
  51.7 0.8 %collective-permute-start.16 = (f32[2,3,4,4]{3,2,1,0:T(4,128)S(1)}, f32[2,3,4,4]{3,2,1,0:T(4,128)S(1)}, u32[]{:S(2)}, u32[]{:S(2)}) collective-permute-start(f32[2,3,4,4]{3,2,1,0:T(4,128)S(1)} %get-tuple-element.73.refs_0_), channel_id=1, source_target_pairs={{0,3},{1,2},{2,1},{3,0},{4,7},{5,6},{6,5},{7,4},{8,11},{9,10},{10,... | collective-permute-start | bytes 1160 | tf_op jit(solution)/shard_map/ppermute | solution.py:450
  52.5 0.8 %collective-permute-start.15 = (f32[2,3,4,4]{3,2,1,0:T(4,128)S(1)}, f32[2,3,4,4]{3,2,1,0:T(4,128)S(1)}, u32[]{:S(2)}, u32[]{:S(2)}) collective-permute-start(f32[2,3,4,4]{3,2,1,0:T(4,128)S(1)} %get-tuple-element.73.refs_0_), channel_id=1, source_target_pairs={{0,2},{1,3},{2,0},{3,1},{4,6},{5,7},{6,4},{7,5},{8,10},{9,11},{10,... | collective-permute-start | bytes 1160 | tf_op jit(solution)/shard_map/ppermute | solution.py:450
  53.6 0.9 %put.1 = f32[2,3,128,512]{3,2,1,0:T(8,128)} custom-call(f32[3,128,512]{2,1,0:T(8,128)S(1)} %get-tuple-element.71.values_ref, f32[2,3,128,512]{3,2,1,0:T(8,128)} %get-tuple-element.72._), custom_call_target="tpu_custom_call", output_to_operand_aliasing={{}: (1, {})} | custom-call | tf_op jit(solution)/shard_map/put/pallas_call | solution.py:339
  54.9 1.3 %collective-permute-done.15.refs_2_ = f32[2,3,4,4]{3,2,1,0:T(4,128)S(1)} collective-permute-done((f32[2,3,4,4]{3,2,1,0:T(4,128)S(1)}, f32[2,3,4,4]{3,2,1,0:T(4,128)S(1)}, u32[]{:S(2)}, u32[]{:S(2)}) %collective-permute-start.15) | collective-permute-done | bytes 416 | tf_op jit(solution)/shard_map/ppermute | solution.py:450
  56.2 0.6 %last.1 = f32[2,3,4,4]{3,2,1,0:T(4,128)} custom-call(f32[2,3,4,4]{3,2,1,0:T(4,128)S(1)} %get-tuple-element.73.refs_0_, f32[2,3,4,4]{3,2,1,0:T(4,128)S(1)} %collective-permute-done.14.refs_1_, f32[2,3,4,4]{3,2,1,0:T(4,128)S(1)} %collective-permute-done.15.refs_2_, f32[2,3,4,4]{3,2,1,0:T(4,128)S(1)} %collective-permute-done.16.refs_3_), custom_call_target="tpu_custom_call" | custom-call | tf_op jit(solution)/shard_map/last/pallas_call | solution.py:354
  (48 shorter events, 4.8 us)
Async XLA Ops:
  2.1 13.6 %collective-permute-start.1 = (bf16[656,128]{1,0:T(8,128)(2,1)S(1)}, bf16[656,128]{1,0:T(8,128)(2,1)S(1)}, u32[]{:S(2)}, u32[]{:S(2)}) collective-permute-start(bf16[656,128]{1,0:T(8,128)(2,1)S(1)} %get-tuple-element.40), channel_id=1, source_target_pairs={{0,8},{4,12},{8,0},{12,4},{1,9},{5,13},{9,1},{13,5},{2,10},{6,14},... | collective-permute-start | bytes 503816 | tf_op jit(solution)/shard_map/ppermute | solution.py:409
  6.2 9.5 %collective-permute-start = (bf16[656,128]{1,0:T(8,128)(2,1)S(1)}, bf16[656,128]{1,0:T(8,128)(2,1)S(1)}, u32[]{:S(2)}, u32[]{:S(2)}) collective-permute-start(bf16[656,128]{1,0:T(8,128)(2,1)S(1)} %get-tuple-element.53.refs_4_), channel_id=1, source_target_pairs={{0,4},{4,0},{8,12},{12,8},{1,5},{5,1},{9,13},{13,9},{2,6},{6,2},{1... | collective-permute-start | bytes 503816 | tf_op jit(solution)/shard_map/ppermute | solution.py:409
  7.8 11.1 %collective-permute-start.2 = (bf16[656,128]{1,0:T(8,128)(2,1)S(1)}, bf16[656,128]{1,0:T(8,128)(2,1)S(1)}, u32[]{:S(2)}, u32[]{:S(2)}) collective-permute-start(bf16[656,128]{1,0:T(8,128)(2,1)S(1)} %get-tuple-element.41.refs_5_), channel_id=1, source_target_pairs={{0,12},{4,8},{8,4},{12,0},{1,13},{5,9},{9,5},{13,1},{2,14},{6,10},... | collective-permute-start | bytes 503816 | tf_op jit(solution)/shard_map/ppermute | solution.py:409
  19.5 3.9 %collective-permute-start.3 = (f32[2,264,512]{2,1,0:T(8,128)S(1)}, f32[2,264,512]{2,1,0:T(8,128)S(1)}, u32[]{:S(2)}, u32[]{:S(2)}) collective-permute-start(f32[2,264,512]{2,1,0:T(8,128)S(1)} %get-tuple-element.46), channel_id=1, source_target_pairs={{0,1},{1,0},{2,3},{3,2},{4,5},{5,4},{6,7},{7,6},{8,9},{9,8},{10,11... | collective-permute-start | bytes 3244040 | tf_op jit(solution)/shard_map/ppermute | solution.py:416
  19.6 15.0 %collective-permute-start.6 = (bf16[1920,128]{1,0:T(8,128)(2,1)S(1)}, bf16[1920,128]{1,0:T(8,128)(2,1)S(1)}, u32[]{:S(2)}, u32[]{:S(2)}) collective-permute-start(bf16[1920,128]{1,0:T(8,128)(2,1)S(1)} %get-tuple-element.42), channel_id=1, source_target_pairs={{0,4},{1,5},{2,6},{3,7},{4,0},{5,1},{6,2},{7,3},{8,12},{9,13},{10,... | collective-permute-start | bytes 1474568 | tf_op jit(solution)/shard_map/ppermute | solution.py:412
  22.8 11.8 %collective-permute-start.7 = (bf16[1920,128]{1,0:T(8,128)(2,1)S(1)}, bf16[1920,128]{1,0:T(8,128)(2,1)S(1)}, u32[]{:S(2)}, u32[]{:S(2)}) collective-permute-start(bf16[1920,128]{1,0:T(8,128)(2,1)S(1)} %get-tuple-element.43), channel_id=1, source_target_pairs={{0,1},{1,0},{2,3},{3,2},{4,8},{5,9},{6,10},{7,11},{8,4},{9,5},{10,... | collective-permute-start | bytes 1474568 | tf_op jit(solution)/shard_map/ppermute | solution.py:412
  23.4 2.4 %copy-start.1 = (s32[2,3]{1,0:T(2,128)S(1)}, s32[2,3]{1,0:T(2,128)}, u32[]{:S(2)}) copy-start(s32[2,3]{1,0:T(2,128)} %partners_ref.5) | copy-start | bytes 76
  23.4 2.4 %copy-start.2 = (s32[8,128]{1,0:T(8,128)S(1)}, s32[8,128]{1,0:T(8,128)}, u32[]{:S(2)}) copy-start(s32[8,128]{1,0:T(8,128)} %domains_ref.1) | copy-start | bytes 12292
  23.4 2.4 %copy-start.3 = (f32[1024]{0:T(1024)S(1)}, f32[1024]{0:T(1024)}, u32[]{:S(2)}) copy-start(f32[1024]{0:T(1024)} %param.9) | copy-start | bytes 12292
  23.5 2.4 %copy-start.4 = (f32[8,4]{0,1:T(4,128)S(1)}, f32[8,4]{0,1:T(4,128)}, u32[]{:S(2)}) copy-start(f32[8,4]{0,1:T(4,128)} %param.8) | copy-start | bytes 388
  23.7 9.1 %collective-permute-start.4 = (f16[256,512]{1,0:T(8,128)(2,1)S(1)}, f16[256,512]{1,0:T(8,128)(2,1)S(1)}, u32[]{:S(2)}, u32[]{:S(2)}) collective-permute-start(f16[256,512]{1,0:T(8,128)(2,1)S(1)} %fusion.4), channel_id=1, source_target_pairs={{0,2},{1,3},{2,0},{3,1},{4,6},{5,7},{6,4},{7,5},{8,10},{9,11},{10,... | collective-permute-start | bytes 786440 | tf_op jit(solution)/shard_map/ppermute | solution.py:416
  25.3 7.4 %collective-permute-start.5 = (f32[8,512]{1,0:T(8,128)S(1)}, f32[8,512]{1,0:T(8,128)S(1)}, u32[]{:S(2)}, u32[]{:S(2)}) collective-permute-start(f32[8,512]{1,0:T(8,128)S(1)} %get-tuple-element.49), channel_id=1, source_target_pairs={{0,2},{1,3},{2,0},{3,1},{4,6},{5,7},{6,4},{7,5},{8,10},{9,11},{10,... | collective-permute-start | bytes 49160 | tf_op jit(solution)/shard_map/ppermute | solution.py:416
  32.8 4.3 %copy-start = (f32[8,512]{1,0:T(8,128)}, f32[8,512]{1,0:T(8,128)S(1)}, u32[]{:S(2)}) copy-start(f32[8,512]{1,0:T(8,128)S(1)} %scale_up.1) | copy-start | bytes 49156
  35.1 1.6 %collective-permute-start.8 = (f32[128,512]{1,0:T(8,128)S(1)}, f32[128,512]{1,0:T(8,128)S(1)}, u32[]{:S(2)}, u32[]{:S(2)}) collective-permute-start(f32[128,512]{1,0:T(8,128)S(1)} %get-tuple-element.57), channel_id=1, source_target_pairs={{0,1},{1,0},{2,3},{3,2},{4,5},{5,4},{6,7},{7,6},{8,9},{9,8},{10,11... | collective-permute-start | bytes 786440 | tf_op jit(solution)/shard_map/ppermute | solution.py:416
  36.8 2.4 %collective-permute-start.10 = (f32[384,512]{1,0:T(8,128)S(1)}, f32[384,512]{1,0:T(8,128)S(1)}, u32[]{:S(2)}, u32[]{:S(2)}) collective-permute-start(f32[384,512]{1,0:T(8,128)S(1)} %get-tuple-element.61), channel_id=1, source_target_pairs={{0,1},{1,0},{2,3},{3,2},{4,5},{5,4},{6,7},{7,6},{8,9},{9,8},{10,11... | collective-permute-start | bytes 2359304 | tf_op jit(solution)/shard_map/ppermute | solution.py:416
  37.2 3.7 %slice-start = ((f32[8,512]{1,0:T(8,128)}), f32[1,512]{1,0:T(1,128)S(1)}, s32[]{:S(2)}) async-start(f32[8,512]{1,0:T(8,128)} %copy-done), calls=%async_computation | async-start | bytes 4096 | tf_op jit(solution)/shard_map/slice | solution.py:445
  37.2 6.0 %collective-permute-start.13 = (f16[128,512]{1,0:T(8,128)(2,1)S(1)}, f16[128,512]{1,0:T(8,128)(2,1)S(1)}, u32[]{:S(2)}, u32[]{:S(2)}) collective-permute-start(f16[128,512]{1,0:T(8,128)(2,1)S(1)} %multiply_convert_fusion.1), channel_id=1, source_target_pairs={{0,2},{1,3},{2,0},{3,1},{4,6},{5,7},{6,4},{7,5},{8,10},{9,11},{10,... | collective-permute-start | bytes 393224 | tf_op jit(solution)/shard_map/ppermute | solution.py:416
  38.7 4.5 %collective-permute-start.12 = (f32[128,512]{1,0:T(8,128)S(1)}, f32[128,512]{1,0:T(8,128)S(1)}, u32[]{:S(2)}, u32[]{:S(2)}) collective-permute-start(f32[128,512]{1,0:T(8,128)S(1)} %get-tuple-element.63), channel_id=1, source_target_pairs={{0,1},{1,0},{2,3},{3,2},{4,5},{5,4},{6,7},{7,6},{8,9},{9,8},{10,11... | collective-permute-start | bytes 786440 | tf_op jit(solution)/shard_map/ppermute | solution.py:416
  38.7 5.4 %collective-permute-start.9 = (f32[384,512]{1,0:T(8,128)S(1)}, f32[384,512]{1,0:T(8,128)S(1)}, u32[]{:S(2)}, u32[]{:S(2)}) collective-permute-start(f32[384,512]{1,0:T(8,128)S(1)} %get-tuple-element.58), channel_id=1, source_target_pairs={{0,1},{1,0},{2,3},{3,2},{4,5},{5,4},{6,7},{7,6},{8,9},{9,8},{10,11... | collective-permute-start | bytes 2359304 | tf_op jit(solution)/shard_map/ppermute | solution.py:416
  39.4 11.8 %collective-permute-start.11 = (f16[384,512]{1,0:T(8,128)(2,1)S(1)}, f16[384,512]{1,0:T(8,128)(2,1)S(1)}, u32[]{:S(2)}, u32[]{:S(2)}) collective-permute-start(f16[384,512]{1,0:T(8,128)(2,1)S(1)} %multiply_convert_fusion), channel_id=1, source_target_pairs={{0,2},{1,3},{2,0},{3,1},{4,6},{5,7},{6,4},{7,5},{8,10},{9,11},{10,... | collective-permute-start | bytes 1179656 | tf_op jit(solution)/shard_map/ppermute | solution.py:416
  43.3 7.9 %slice-start.2 = ((f32[8,512]{1,0:T(8,128)}), f32[1,512]{1,0:T(1,128)S(1)}, s32[]{:S(2)}) async-start(f32[8,512]{1,0:T(8,128)} %copy-done), calls=%async_computation.2 | async-start | bytes 4096 | tf_op jit(solution)/shard_map/slice | solution.py:445
  51.7 3.2 %collective-permute-start.16 = (f32[2,3,4,4]{3,2,1,0:T(4,128)S(1)}, f32[2,3,4,4]{3,2,1,0:T(4,128)S(1)}, u32[]{:S(2)}, u32[]{:S(2)}) collective-permute-start(f32[2,3,4,4]{3,2,1,0:T(4,128)S(1)} %get-tuple-element.73.refs_0_), channel_id=1, source_target_pairs={{0,3},{1,2},{2,1},{3,0},{4,7},{5,6},{6,5},{7,4},{8,11},{9,10},{10,... | collective-permute-start | bytes 1160 | tf_op jit(solution)/shard_map/ppermute | solution.py:450
  52.5 3.7 %collective-permute-start.15 = (f32[2,3,4,4]{3,2,1,0:T(4,128)S(1)}, f32[2,3,4,4]{3,2,1,0:T(4,128)S(1)}, u32[]{:S(2)}, u32[]{:S(2)}) collective-permute-start(f32[2,3,4,4]{3,2,1,0:T(4,128)S(1)} %get-tuple-element.73.refs_0_), channel_id=1, source_target_pairs={{0,2},{1,3},{2,0},{3,1},{4,6},{5,7},{6,4},{7,5},{8,10},{9,11},{10,... | collective-permute-start | bytes 1160 | tf_op jit(solution)/shard_map/ppermute | solution.py:450
  53.3 2.9 %collective-permute-start.14 = (f32[2,3,4,4]{3,2,1,0:T(4,128)S(1)}, f32[2,3,4,4]{3,2,1,0:T(4,128)S(1)}, u32[]{:S(2)}, u32[]{:S(2)}) collective-permute-start(f32[2,3,4,4]{3,2,1,0:T(4,128)S(1)} %get-tuple-element.73.refs_0_), channel_id=1, source_target_pairs={{0,1},{1,0},{2,3},{3,2},{4,5},{5,4},{6,7},{7,6},{8,9},{9,8},{10,11... | collective-permute-start | bytes 1160 | tf_op jit(solution)/shard_map/ppermute | solution.py:450
  (1 other events, 2.3 us)
